TPU v7x, 32 devices: a whole 2x2x4 slice. The times are simulated.
32 devices in a mesh: batch: 8 (over y, x, core), head: 4 (over z).
Axes of the slice: x: 2, y: 2, z: 4, core: 2. Of those that a mesh axis runs over, the one named last changes fastest.
Arguments:
- tokens: bfloat16 [2, 3072, 2048], P(None, 'batch'), may hold values from -6 to 6
- cotangent: bfloat16 [2, 3072, 2048], P(None, 'batch'), may hold values from -6 to 6
- lengths: int32 [2, 8], P(None, 'batch'), may hold values from 48 to 384, as said below
- norm_in: float32 [2048], replicated, may hold values from 0.5 to 1.5
- w_query: bfloat16 [2048, 2048], P(None, 'head'), may hold values from -0.125 to 0.125
- w_key: bfloat16 [2048, 2048], P(None, 'head'), may hold values from -0.125 to 0.125
- w_value: bfloat16 [2048, 2048], P(None, 'head'), may hold values from -0.125 to 0.125
- w_gate: bfloat16 [2048, 2048], P(None, 'head'), may hold values from -0.125 to 0.125
- w_beta: bfloat16 [2048, 16], P(None, 'head'), may hold values from -0.125 to 0.125
- w_alpha: bfloat16 [2048, 16], P(None, 'head'), may hold values from -0.125 to 0.125
- conv_taps: float32 [3, 4, 2048], P(None, None, 'head'), may hold values from -2.5 to 2.5
- decay_log: float32 [16], P('head'), may hold values from -5 to -2.5
- decay_bias: float32 [16], P('head'), may hold values from -1 to 1
- norm_head: float32 [128], replicated, may hold values from 0.5 to 1.5
- w_out: bfloat16 [2048, 2048], P('head'), may hold values from -0.25 to 0.25
- norm_mid: float32 [2048], replicated, may hold values from 0.5 to 1.5
- w_up_gate: bfloat16 [2048, 5632], P(None, 'head'), may hold values from -0.125 to 0.125
- w_up: bfloat16 [2048, 5632], P(None, 'head'), may hold values from -0.125 to 0.125
- w_down: bfloat16 [5632, 2048], P('head'), may hold values from -0.109375 to 0.109375
Outputs:
- out_tokens: bfloat16 [2, 3072, 2048], P(None, 'batch')
- grad_tokens: bfloat16 [2, 3072, 2048], P(None, 'batch')
- grad_norm_in: float32 [2048], replicated
- grad_query: float32 [2048, 2048], P('batch', 'head')
- grad_key: float32 [2048, 2048], P('batch', 'head')
- grad_value: float32 [2048, 2048], P('batch', 'head')
- grad_gate: float32 [2048, 2048], P('batch', 'head')
- grad_beta: float32 [2048, 16], P('batch', 'head')
- grad_alpha: float32 [2048, 16], P('batch', 'head')
- grad_conv: float32 [3, 4, 2048], P(None, None, 'head')
- grad_decay_log: float32 [16], P('head')
- grad_decay_bias: float32 [16], P('head')
- grad_norm_head: float32 [128], replicated
- grad_out: float32 [2048, 2048], P('head', 'batch')
- grad_norm_mid: float32 [2048], replicated
- grad_up_gate: float32 [2048, 5632], P('batch', 'head')
- grad_up: float32 [2048, 5632], P('batch', 'head')
- grad_down: float32 [5632, 2048], P('head', 'batch')
Inputs may be any that keep to these rules, and one draw needn't show every extreme that they name: `lengths`: in every micro-batch some slot's length is exactly 384.
All inputs are finite; a program needn't handle non-finite values.
Results may differ from a plain program's by a relative error of at most 0.017.
Values may be sent and summed in bfloat16 or wider, within the bound.
No kernel may reach another device: no remote copies, remote signals or barrier semaphores. Data moves between devices by JAX's collectives and lax.ppermute only.
A program may use at most 448 MiB of HBM per device.

v0:
```python
import math

import jax
import jax.numpy as jnp
from jax import lax
from jax.sharding import PartitionSpec as P

BLOCK = 64


EPSILON = 1e-06
FULL_PRECISION = lax.Precision.HIGHEST


def bf_dot(left, right):
    return jnp.dot(left, right, preferred_element_type=jnp.float32)


def dot_tn(left, right):
    return lax.dot_general(
        left, right, (((0,), (0,)), ((), ())), preferred_element_type=jnp.float32
    )


def dot_nt(left, right):
    return lax.dot_general(
        left, right, (((1,), (1,)), ((), ())), preferred_element_type=jnp.float32
    )


def exact_dot(left, right):
    return jnp.dot(left, right, precision=FULL_PRECISION)


def rms_scale(vector, gain):
    return vector * lax.rsqrt(jnp.mean(vector * vector, axis=-1, keepdims=True) + EPSILON) * gain


def rms_back(grad_norm, vector, gain):
    inverse = lax.rsqrt(jnp.mean(vector * vector, axis=-1, keepdims=True) + EPSILON)
    normal = vector * inverse
    scaled = grad_norm * gain
    return inverse * (scaled - normal * jnp.mean(scaled * normal, axis=-1, keepdims=True))


def unit_rows(vector):
    return vector * lax.rsqrt(jnp.sum(vector * vector, axis=-1, keepdims=True) + EPSILON)


def short_conv(projected, taps):
    tap_count = taps.shape[0]
    padded = jnp.concatenate(
        [jnp.zeros((tap_count - 1, projected.shape[1]), jnp.float32), projected], axis=0
    )
    summed = jnp.zeros_like(projected)
    for offset in range(tap_count):
        summed = summed + padded[offset : offset + projected.shape[0]] * taps[offset]
    return summed


def head_rule(query_seq, key_seq, value_seq, beta_seq, decay_seq):
    seq_len, head_dim = query_seq.shape
    blocks = seq_len // BLOCK
    row_index = lax.broadcasted_iota(jnp.int32, (BLOCK, BLOCK), 0)
    col_index = lax.broadcasted_iota(jnp.int32, (BLOCK, BLOCK), 1)
    strict = row_index > col_index
    inclusive = row_index >= col_index
    identity = (row_index == col_index).astype(jnp.float32)

    def one_block(recurrent_state, pieces):
        query_blk, key_blk, value_blk, beta_blk, decay_blk = pieces
        cumulative = jnp.cumsum(decay_blk)
        spread = cumulative[:, None] - cumulative[None, :]
        lower_decay = jnp.where(strict, jnp.exp(jnp.where(strict, spread, 0.0)), 0.0)
        causal_decay = jnp.where(inclusive, jnp.exp(jnp.where(inclusive, spread, 0.0)), 0.0)
        start_decay = jnp.exp(cumulative)
        system = identity + beta_blk[:, None] * exact_dot(key_blk, key_blk.T) * lower_decay
        right_side = jnp.concatenate(
            [beta_blk[:, None] * value_blk, (beta_blk * start_decay)[:, None] * key_blk], axis=1
        )
        solved = jax.scipy.linalg.solve_triangular(
            system, right_side, lower=True, unit_diagonal=True
        )
        fresh_values = solved[:, :head_dim] - exact_dot(solved[:, head_dim:], recurrent_state)
        scores = exact_dot(query_blk, key_blk.T) * causal_decay
        output_vector = start_decay[:, None] * exact_dot(query_blk, recurrent_state) + exact_dot(
            scores, fresh_values
        )
        tail_decay = jnp.exp(cumulative[-1] - cumulative)
        recurrent_state = jnp.exp(cumulative[-1]) * recurrent_state + exact_dot(
            (key_blk * tail_decay[:, None]).T, fresh_values
        )
        return (recurrent_state, output_vector)

    def blocked(series):
        return series.reshape((blocks, BLOCK) + series.shape[1:])

    start_state = jnp.zeros((head_dim, head_dim), jnp.float32)
    last_state, outputs = lax.scan(
        one_block,
        start_state,
        (
            blocked(query_seq),
            blocked(key_seq),
            blocked(value_seq),
            blocked(beta_seq),
            blocked(decay_seq),
        ),
    )
    return outputs.reshape(seq_len, head_dim)


def mixer(projections, conv_taps, decay_log, decay_bias, norm_head):
    proj_query, proj_key, proj_value, proj_gate, proj_beta, proj_alpha = projections
    seq_len = proj_query.shape[0]
    head_count = decay_log.shape[0]
    head_dim = norm_head.shape[0]
    split_shape = (seq_len, head_count, head_dim)
    queries = unit_rows(
        jax.nn.silu(short_conv(proj_query, conv_taps[0])).reshape(split_shape)
    ) / math.sqrt(head_dim)
    key_rows = unit_rows(jax.nn.silu(short_conv(proj_key, conv_taps[1])).reshape(split_shape))
    values = jax.nn.silu(short_conv(proj_value, conv_taps[2])).reshape(split_shape)
    beta_rows = jax.nn.sigmoid(proj_beta)
    decays = -jnp.exp(decay_log) * jax.nn.softplus(proj_alpha + decay_bias)
    mixed_rows = jax.vmap(head_rule, in_axes=1, out_axes=1)(
        queries, key_rows, values, beta_rows, decays
    )
    gated_rows = rms_scale(mixed_rows, norm_head) * jax.nn.silu(proj_gate.reshape(split_shape))
    return gated_rows.reshape(seq_len, head_count * head_dim)


def per_device(
    tokens,
    cotangent,
    lengths,
    norm_in,
    w_query,
    w_key,
    w_value,
    w_gate,
    w_beta,
    w_alpha,
    conv_taps,
    decay_log,
    decay_bias,
    norm_head,
    w_out,
    norm_mid,
    w_up_gate,
    w_up,
    w_down,
):
    micro_count, seq_len, model_dim = tokens.shape
    positions = lax.broadcasted_iota(jnp.int32, (seq_len, 1), 0)
    in_weights = (w_query, w_key, w_value, w_gate, w_beta, w_alpha)
    col_widths = [weight.shape[1] for weight in in_weights] + [
        w_out.shape[0],
        w_up_gate.shape[1],
        w_up.shape[1],
        w_down.shape[0],
    ]

    def forward_reduce(partial_sum):
        return lax.psum(partial_sum, "head")

    def backward_reduce(partial_sum):
        return lax.psum(partial_sum.astype(jnp.bfloat16), "head").astype(jnp.float32)

    def gain_term(normal_rows, partial_sum):
        return jnp.sum(normal_rows * partial_sum, axis=0)

    gain_in = jnp.zeros((model_dim,), jnp.float32)
    gain_mid = jnp.zeros((model_dim,), jnp.float32)
    gain_head = jnp.zeros(norm_head.shape, jnp.float32)
    taps_total = jnp.zeros(conv_taps.shape, jnp.float32)
    decay_log_total = jnp.zeros(decay_log.shape, jnp.float32)
    decay_bias_total = jnp.zeros(decay_bias.shape, jnp.float32)
    out_list = []
    grad_list = []
    for micro in range(micro_count):
        rows = tokens[micro].astype(jnp.float32)
        grad_rows = cotangent[micro].astype(jnp.float32)
        keep = (positions < lengths[micro, 0]).astype(jnp.float32)
        normed_low = rms_scale(rows, norm_in).astype(jnp.bfloat16)
        projections = tuple((bf_dot(normed_low, weight) for weight in in_weights))
        gated, mixer_back = jax.vjp(mixer, projections, conv_taps, decay_log, decay_bias, norm_head)
        gated_low = gated.astype(jnp.bfloat16)
        middle = rows + keep * forward_reduce(bf_dot(gated_low, w_out))
        mid_low = rms_scale(middle, norm_mid).astype(jnp.bfloat16)
        gate_act = bf_dot(mid_low, w_up_gate)
        up_act = bf_dot(mid_low, w_up)
        sig_gate = jax.nn.sigmoid(gate_act)
        hidden_low = (gate_act * sig_gate * up_act).astype(jnp.bfloat16)
        out_own = (middle + keep * forward_reduce(bf_dot(hidden_low, w_down))).astype(jnp.bfloat16)
        out_list.append(out_own)
        down_grad = (keep * grad_rows).astype(jnp.bfloat16)
        grad_hidden = dot_nt(down_grad, w_down)
        grad_gate_low = (
            grad_hidden * up_act * sig_gate * (1.0 + gate_act * (1.0 - sig_gate))
        ).astype(jnp.bfloat16)
        grad_up_low = (grad_hidden * gate_act * sig_gate).astype(jnp.bfloat16)
        mid_part = dot_nt(grad_gate_low, w_up_gate) + dot_nt(grad_up_low, w_up)
        mid_reduced = backward_reduce(mid_part)
        gain_mid = gain_mid + gain_term(rms_scale(middle, 1.0), mid_part)
        grad_middle = grad_rows + rms_back(mid_reduced, middle, norm_mid)
        attn_grad_low = (keep * grad_middle).astype(jnp.bfloat16)
        grad_gated = dot_nt(attn_grad_low, w_out)
        grad_proj, grad_taps, grad_dlog, grad_dbias, grad_nhead = mixer_back(grad_gated)
        grad_proj_low = tuple((entry.astype(jnp.bfloat16) for entry in grad_proj))
        in_part = dot_nt(grad_proj_low[0], in_weights[0])
        for index_in in range(1, len(in_weights)):
            in_part = in_part + dot_nt(grad_proj_low[index_in], in_weights[index_in])
        in_reduced = backward_reduce(in_part)
        gain_in = gain_in + gain_term(rms_scale(rows, 1.0), in_part)
        grad_own = (grad_middle + rms_back(in_reduced, rows, norm_in)).astype(jnp.bfloat16)
        grad_list.append(grad_own)
        gain_head = gain_head + grad_nhead
        taps_total = taps_total + grad_taps
        decay_log_total = decay_log_total + grad_dlog
        decay_bias_total = decay_bias_total + grad_dbias
        micro_big = jnp.concatenate(
            [dot_tn(normed_low, entry) for entry in grad_proj_low]
            + [
                dot_tn(attn_grad_low, gated_low),
                dot_tn(mid_low, grad_gate_low),
                dot_tn(mid_low, grad_up_low),
                dot_tn(down_grad, hidden_low),
            ],
            axis=1,
        )
        collected = micro_big if micro == 0 else collected + micro_big
    big_joined = lax.psum_scatter(
        collected.astype(jnp.bfloat16), "batch", scatter_dimension=0, tiled=True
    ).astype(jnp.float32)
    big_shares = []
    offset = 0
    for width in col_widths:
        big_shares.append(big_joined[:, offset : offset + width])
        offset = offset + width
    gain_totals = lax.psum((gain_in, gain_head, gain_mid), ("batch", "head"))
    small_totals = lax.psum((taps_total, decay_log_total, decay_bias_total), "batch")
    out_tokens = jnp.stack(out_list, axis=0)
    grad_tokens = jnp.stack(grad_list, axis=0)
    return (
        out_tokens,
        grad_tokens,
        gain_totals[0],
        big_shares[0],
        big_shares[1],
        big_shares[2],
        big_shares[3],
        big_shares[4],
        big_shares[5],
        small_totals[0],
        small_totals[1],
        small_totals[2],
        gain_totals[1],
        big_shares[6].T,
        gain_totals[2],
        big_shares[7],
        big_shares[8],
        big_shares[9].T,
    )


def solution(mesh):
    placed = (
        P(None, "batch", None),
        P(None, "batch", None),
        P(None, "batch"),
        P(),
        P(None, "head"),
        P(None, "head"),
        P(None, "head"),
        P(None, "head"),
        P(None, "head"),
        P(None, "head"),
        P(None, None, "head"),
        P("head"),
        P("head"),
        P(),
        P("head", None),
        P(),
        P(None, "head"),
        P(None, "head"),
        P("head", None),
    )
    return jax.shard_map(
        per_device,
        mesh=mesh,
        in_specs=placed,
        out_specs=(
            P(None, "batch", None),
            P(None, "batch", None),
            P(),
            P("batch", "head"),
            P("batch", "head"),
            P("batch", "head"),
            P("batch", "head"),
            P("batch", "head"),
            P("batch", "head"),
            P(None, None, "head"),
            P("head"),
            P("head"),
            P(),
            P("head", "batch"),
            P(),
            P("batch", "head"),
            P("batch", "head"),
            P("head", "batch"),
        ),
        check_vma=False,
    )
```

profile of v0, /device:TPU:0, one launch (start us, length us, event | category | flops | bytes accessed | tf_op | source)
XLA Modules:
  0.0 2596.5 jit_solution(2624721874554976296)
XLA Ops:
  93.3 252.7 %while.190 = (s32[]{:T(128)}, f32[4,128,128]{2,1,0:T(8,128)S(1)}, f32[6,4,64,128]{3,2,0,1:T(8,128)}, f32[6,4,64,64]{3,2,1,0:T(8,128)}, f32[6,4,64,64]{3,2,1,0:T(...) while((s32[]{:T(128)}, f32[4,128,128]{2,1,0:T(8,128)S(1)}, ...), condition=%wide.region_5.8_spmd.clone.clone, body=%wide.region_3.7_spmd.clone.clone.sunk | while | flops 277976128 | bytes 7702909 | solution.py:99
  102.3 21.0 custom-call.22
  144.3 21.0 custom-call.22
  186.4 21.0 custom-call.22
  228.5 21.0 custom-call.22
  270.6 21.0 custom-call.22
  312.8 21.0 custom-call.22
  379.2 239.3 %while.191 = (s32[]{:T(128)}, f32[4,128,128]{2,1,0:T(8,128)S(1)}, f32[6,4,64,128]{3,2,0,1:T(8,128)}, f32[6,4,64,64]{3,2,1,0:T(8,128)}, f32[6,4,64,64]{3,2,1,0:T(...) while((s32[]{:T(128)}, f32[4,128,128]{2,1,0:T(8,128)S(1)}, ...), condition=%wide.region_15.18_spmd.clone.clone, body=%wide.region_13.17_spmd.clone.clone.sunk | while | flops 277976128 | bytes 7753637 | solution.py:99
  386.6 20.3 custom-call.23
  426.5 20.3 custom-call.23
  466.3 20.3 custom-call.23
  506.2 20.3 custom-call.23
  546.1 20.3 custom-call.23
  586.0 20.3 custom-call.23
  635.1 223.5 %all-reduce.81.cloned.1.call-done = (f32[384,2048]{1,0:T(8,128)}, f32[384,2048]{1,0:T(8,128)}) async-done(((f32[384,2048]{1,0:T(8,128)}, f32[384,2048]{1,0:T(8,128)}), (f32[384,2048]{1,0:T(8,128)}, f32[384,2048]{1,0:T(8,128)})) %all-reduce.81.cloned.1.call-update) | async-done | bytes 6291472 | tf_op jit(solution)/shard_map/psum | solution.py:165
  866.3 7.8 fusion.538
  883.3 6.9 multiply_convert_fusion.4
  893.1 8.7 multiply_convert_fusion.6
  913.2 7.3 fusion.546
  920.5 7.0 fusion.539
  928.2 9.2 fusion.564
  955.7 6.2 fusion.462
  968.1 65.6 %all-reduce.85.cloned.1.call-done = (bf16[384,2048]{1,0:T(8,128)(2,1)}, bf16[384,2048]{1,0:T(8,128)(2,1)}) async-done(((bf16[384,2048]{1,0:T(8,128)(2,1)}, bf16[384,2048]{1,0:T(8,128)(2,1)}), (bf16[384,2048]{1,0:T(8,128)(2,1)}, bf16[384,2048]{1,0:T(8,128)(2,1)})) %all-reduce.85.cloned.1.call-update) | async-done | bytes 3145744 | tf_op jit(solution)/shard_map/psum | solution.py:168
  1033.7 7.8 multiply_reduce_fusion.1
  1041.5 216.9 %all-reduce.79.cloned.1.call-done = (f32[384,2048]{1,0:T(8,128)}, f32[384,2048]{1,0:T(8,128)}) async-done(((f32[384,2048]{1,0:T(8,128)}, f32[384,2048]{1,0:T(8,128)}), (f32[384,2048]{1,0:T(8,128)}, f32[384,2048]{1,0:T(8,128)})) %all-reduce.79.cloned.1.call-update) | async-done | bytes 6291472 | tf_op jit(solution)/shard_map/psum | solution.py:165
  1258.3 9.8 convert_add_fusion.1
  1281.3 369.4 %while.193 = (s32[]{:T(128)}, f32[4,128,128]{2,1,0:T(8,128)S(1)}, f32[6,4,64,128]{3,2,0,1:T(8,128)}, f32[6,4,64,128]{3,2,0,1:T(8,128)}, f32[6,4,64,128]{3,2,0,1:...) while((s32[]{:T(128)}, f32[4,128,128]{2,1,0:T(8,128)S(1)}, ...), condition=%wide.region_53.57_spmd.clone.clone, body=%wide.region_42.56_spmd.clone.clone.sunk | while | flops 568064064 | bytes 11613120 | solution.py:99
  1290.3 20.3 custom-call.25
  1351.8 20.3 custom-call.25
  1413.3 20.3 custom-call.25
  1474.9 20.3 custom-call.25
  1536.4 20.3 custom-call.25
  1597.9 20.3 custom-call.25
  1660.6 342.8 %while.192 = (s32[]{:T(128)}, f32[4,128,128]{2,1,0:T(8,128)S(1)}, f32[6,4,64,128]{3,2,0,1:T(8,128)}, f32[6,4,64,128]{3,2,0,1:T(8,128)}, f32[6,4,64,128]{3,2,0,1:...) while((s32[]{:T(128)}, f32[4,128,128]{2,1,0:T(8,128)S(1)}, ...), condition=%wide.region_34.38_spmd.clone.clone, body=%wide.region_23.37_spmd.clone.clone.sunk | while | flops 568064064 | bytes 10818384 | solution.py:99
  1669.6 19.7 custom-call.24
  1726.7 19.7 custom-call.24
  1783.7 19.7 custom-call.24
  1840.8 19.7 custom-call.24
  1897.8 19.7 custom-call.24
  1954.9 19.7 custom-call.24
  2083.5 8.4 fusion.531
  2097.6 129.3 %concatenate.44 = f32[2048,6792]{0,1:T(8,128)} concatenate(f32[2048,512]{0,1:T(8,128)} %fusion.559, f32[2048,512]{0,1:T(8,128)} %fusion.560, f32[2048,512]{0,1:T(8,128)} %fusion.561, f32[2048,512]{0,1:T(8,128)} %fusion.406, f32[2048,4]{0,1:T(4,128)S(1)} %fusion.562, f32[2048,4]{0,1:T(4,128)S(1)} %fusion.495, f32[2048,512]{0,1:T(8,128)} %fusion.498, f32[2048,1408]{0,1:T(8,128)} %fusion.563, ...), dimensions={1} | concatenate | bytes 111280128 | tf_op jit(solution)/shard_map/concatenate | solution.py:222
  2226.9 129.1 %concatenate.45 = f32[2048,6792]{0,1:T(8,128)} concatenate(f32[2048,512]{0,1:T(8,128)} %fusion.565, f32[2048,512]{0,1:T(8,128)} %fusion.566, f32[2048,512]{0,1:T(8,128)} %fusion.567, f32[2048,512]{0,1:T(8,128)} %fusion.402, f32[2048,4]{0,1:T(4,128)S(1)} %copy-done.118, f32[2048,4]{0,1:T(4,128)S(1)} %fusion.492, f32[2048,512]{0,1:T(8,128)} %fusion.500, f32[2048,1408]{0,1:T(8,128)} %fusion.569, ...), dimensions={1} | concatenate | bytes 111280128 | tf_op jit(solution)/shard_map/concatenate | solution.py:222
  2356.1 44.1 %add_convert_fusion = bf16[2048,6792]{0,1:T(8,128)(2,1)} fusion(f32[2048,6792]{0,1:T(8,128)} %concatenate.44, f32[2048,6792]{0,1:T(8,128)} %concatenate.45), kind=kLoop, calls=%fused_computation.520 | loop fusion | flops 27820032 | bytes 139100160 | tf_op jit(solution)/shard_map/convert_element_type | solution.py:234
  2401.2 24.6 all-reduce.69
  2429.7 7.8 fusion.375
  2437.6 39.5 %all-reduce.68 = (f32[2048]{0:T(1024)}, f32[128]{0:T(128)}, f32[2048]{0:T(1024)}) all-reduce(f32[2048]{0:T(1024)S(1)} %add.686, f32[128]{0:T(128)S(1)} %add.691, f32[2048]{0:T(1024)S(1)} %add.692), channel_id=1, replica_groups=mesh['batch'=8,'head'=4] {'batch','head'}, use_global_device_ids=true, to_apply=%region_60.64 | all-reduce | flops 4224 | bytes 33792 | tf_op jit(solution)/shard_map/psum | solution.py:241
  2484.3 87.5 %reduce-scatter.2.cloned.1.call-done = bf16[256,6792]{0,1:T(8,128)(2,1)} async-done(((bf16[2048,6792]{0,1:T(8,128)(2,1)}), bf16[256,6792]{0,1:T(8,128)(2,1)}) %reduce-scatter.2.cloned.1.call-update) | async-done | bytes 3477520 | tf_op jit(solution)/shard_map/reduce_scatter | solution.py:233
  (1701 shorter events, 1042.3 us)
Async XLA Ops:
  7.2 619.9 %copy-start = (bf16[512,2048]{1,0:T(8,128)(2,1)S(1)}, bf16[512,2048]{1,0:T(8,128)(2,1)}, u32[]{:S(2)}) copy-start(bf16[512,2048]{1,0:T(8,128)(2,1)} %param.48) | copy-start | bytes 6291460
  7.2 851.4 %all-reduce.81.cloned.1.call-start = ((), (), s32[]{:S(2)}) async-start(), calls=%async_computation.3 | async-start | bytes 12582912 | tf_op jit(solution)/shard_map/psum | solution.py:165
  10.1 19.9 copy-start.148
  11.4 10.2 copy-start.2
  11.4 12.1 copy-start.4
  12.0 24.4 copy-start.138
  12.5 23.1 copy-start.139
  13.0 21.2 copy-start.132
  14.1 20.1 copy-start.134
  25.4 8.9 copy-start.196
  25.4 11.6 copy-start.176
  25.4 11.6 copy-start.178
  25.4 11.6 copy-start.180
  25.4 11.6 copy-start.182
  25.4 31.4 %copy-start.160 = (f32[1,1,512]{2,1,0:T(1,128)}, f32[1,1,512]{2,1,0:T(1,128)S(1)}, u32[]{:S(2)}) copy-start(f32[1,1,512]{2,1,0:T(1,128)S(1)} %get-tuple-element.5185) | copy-start | bytes 6148
  25.5 31.3 %copy-start.162 = (f32[1,1,512]{2,1,0:T(1,128)}, f32[1,1,512]{2,1,0:T(1,128)S(1)}, u32[]{:S(2)}) copy-start(f32[1,1,512]{2,1,0:T(1,128)S(1)} %get-tuple-element.5186) | copy-start | bytes 6148
  25.5 31.3 %copy-start.164 = (f32[1,1,512]{2,1,0:T(1,128)}, f32[1,1,512]{2,1,0:T(1,128)S(1)}, u32[]{:S(2)}) copy-start(f32[1,1,512]{2,1,0:T(1,128)S(1)} %get-tuple-element.5187) | copy-start | bytes 6148
  25.5 31.3 %copy-start.166 = (f32[1,1,512]{2,1,0:T(1,128)}, f32[1,1,512]{2,1,0:T(1,128)S(1)}, u32[]{:S(2)}) copy-start(f32[1,1,512]{2,1,0:T(1,128)S(1)} %get-tuple-element.5188) | copy-start | bytes 6148
  25.5 35.4 %copy-start.168 = (f32[1,1,512]{2,1,0:T(1,128)}, f32[1,1,512]{2,1,0:T(1,128)S(1)}, u32[]{:S(2)}) copy-start(f32[1,1,512]{2,1,0:T(1,128)S(1)} %get-tuple-element.5183) | copy-start | bytes 6148
  25.5 35.4 %copy-start.170 = (f32[1,1,512]{2,1,0:T(1,128)}, f32[1,1,512]{2,1,0:T(1,128)S(1)}, u32[]{:S(2)}) copy-start(f32[1,1,512]{2,1,0:T(1,128)S(1)} %get-tuple-element.5184) | copy-start | bytes 6148
  25.5 35.4 %copy-start.172 = (f32[1,1,512]{2,1,0:T(1,128)}, f32[1,1,512]{2,1,0:T(1,128)S(1)}, u32[]{:S(2)}) copy-start(f32[1,1,512]{2,1,0:T(1,128)S(1)} %get-tuple-element.5193) | copy-start | bytes 6148
  25.5 35.4 %copy-start.174 = (f32[1,1,512]{2,1,0:T(1,128)}, f32[1,1,512]{2,1,0:T(1,128)S(1)}, u32[]{:S(2)}) copy-start(f32[1,1,512]{2,1,0:T(1,128)S(1)} %get-tuple-element.5194) | copy-start | bytes 6148
  68.7 9.1 copy-start.140
  632.5 401.1 %all-reduce.85.cloned.1.call-start = ((), (), s32[]{:S(2)}) async-start(), calls=%async_computation.5 | async-start | bytes 6291456 | tf_op jit(solution)/shard_map/psum | solution.py:168
  635.0 633.1 %copy-start.125 = (f32[384]{0:T(512)}, f32[384]{0:T(512)S(1)}, u32[]{:S(2)}) copy-start(f32[384]{0:T(512)S(1)} %get-tuple-element.5250) | copy-start | bytes 4612
  635.0 634.7 %copy-start.123 = (f32[384]{0:T(512)}, f32[384]{0:T(512)S(1)}, u32[]{:S(2)}) copy-start(f32[384]{0:T(512)S(1)} %get-tuple-element.5251) | copy-start | bytes 4612
  863.6 10.5 slice-start
  866.3 14.4 copy-start.17
  866.3 11.8 slice-start.2
  890.3 14.2 copy-start.85
  913.1 345.2 %all-reduce.79.cloned.1.call-start = ((), (), s32[]{:S(2)}) async-start(), calls=%async_computation.2 | async-start | bytes 12582912 | tf_op jit(solution)/shard_map/psum | solution.py:165
  927.5 1502.3 %all-reduce.83.cloned.1.call-start = ((), (), s32[]{:S(2)}) async-start(), calls=%async_computation.4 | async-start | bytes 6291456 | tf_op jit(solution)/shard_map/psum | solution.py:168
  928.2 9.2 copy-start.20
  928.2 9.2 copy-start.88
  1281.3 370.9 %copy-start.5 = (bf16[384,2048]{1,0:T(8,128)(2,1)S(1)}, bf16[384,2048]{1,0:T(8,128)(2,1)}, u32[]{:S(2)}) copy-start(bf16[384,2048]{1,0:T(8,128)(2,1)} %copy-done.4) | copy-start | bytes 4718596
  1310.6 8.7 copy-start.31
  1372.1 8.7 copy-start.31
  1433.6 8.7 copy-start.31
  1495.2 8.7 copy-start.31
  1556.7 8.7 copy-start.31
  1618.2 8.7 copy-start.31
  1660.6 344.3 %copy-start.3 = (bf16[384,2048]{1,0:T(8,128)(2,1)S(1)}, bf16[384,2048]{1,0:T(8,128)(2,1)}, u32[]{:S(2)}) copy-start(bf16[384,2048]{1,0:T(8,128)(2,1)} %copy-done.2) | copy-start | bytes 4718596
  2083.5 10.0 copy-start.36
  2083.5 10.9 copy-start.37
  2097.6 129.4 %copy-start.118 = (f32[2048,4]{0,1:T(4,128)S(1)}, f32[2048,4]{0,1:T(4,128)}, u32[]{:S(2)}) copy-start(f32[2048,4]{0,1:T(4,128)} %fusion.568) | copy-start | bytes 98308
  2097.6 474.2 %reduce-scatter.2.cloned.1.call-start = ((), (), s32[]{:S(2)}) async-start(), calls=%async_computation.1 | async-start | bytes 31297536 | tf_op jit(solution)/shard_map/reduce_scatter | solution.py:233
  2400.3 25.5 copy-start.59
  2429.7 47.4 %copy-start.58 = (bf16[384,2048]{1,0:T(8,128)(2,1)S(1)}, bf16[384,2048]{1,0:T(8,128)(2,1)}, u32[]{:S(2)}) copy-start(bf16[384,2048]{1,0:T(8,128)(2,1)} %get-tuple-element.5001) | copy-start | bytes 4718596
  (324 other events, 1583.5 us)
Sparse Core Ops, SparseCore 0:
  632.6 225.9 all-reduce.80
  913.2 120.3 all-reduce.84
  1036.1 222.2 all-reduce.78
  2097.7 120.3 all-reduce.82
  2400.5 171.3 reduce-scatter.1
where the time goes:
time: 2620 us; the launch traced here: 2600 us
  other arithmetic  839 us (32%)
  matrix products  597 us (23%)
  waiting for transfers between devices  594 us (23%)
  local copies, waits for them, and re-layouts  482 us (18%)
  blocking collectives  64.1 us (2%)
    another operation x108, other arithmetic, one_block(): jax.scipy.linalg.solve_triangular(system, right_side, lower=True, unit_di...  511 us
    psum x2, waiting for transfers between devices, forward_reduce(): return lax.psum(partial_sum, 'head')  440 us
    dot_general x216, matrix products, exact_dot(): return jnp.dot(left, right, precision=FULL_PRECISION)  318 us
    concatenate x2, local copies, waits for them, and re-layouts, per_device(): jnp.concatenate([dot_tn(normed_low, entry) for entry in grad_proj_low] +...  258 us
    reduce_scatter x1, waiting for transfers between devices, per_device(): lax.psum_scatter(collected.astype(jnp.bfloat16), 'batch', scatter_dimensi...  87.5 us
    dot_general x20, matrix products, dot_tn(): lax.dot_general(left, right, (((0,), (0,)), ((), ())), preferred_element_...  76.5 us
    dot_general x20, matrix products, dot_nt(): lax.dot_general(left, right, (((1,), (1,)), ((), ())), preferred_element_...  71.7 us
    dynamic_update_slice x72, other arithmetic, head_rule(): lax.scan(one_block, start_state, (blocked(query_seq), blocked(key_seq), b...  70 us
  transfers between devices with their start and end apart: 5, of which 4 were waited for; matrix products, arithmetic and copies ran while one was open for 15% of the time, Pallas kernels for 0%

commit v1 on v0

v1 whole, which is shorter than its diff:
```python
import math

import jax
import jax.numpy as jnp
from jax import lax
from jax.experimental import pallas as pl
from jax.experimental.pallas import tpu as pltpu
from jax.sharding import PartitionSpec as P

EPSILON = 1e-06
CHUNK = 128
LOW = jnp.bfloat16
FULL = jnp.float32


def mm(left, right, dims=((1,), (0,))):
    return lax.dot_general(
        left.astype(LOW), right.astype(LOW), (dims, ((), ())), preferred_element_type=FULL
    )


NN = ((1,), (0,))
NT = ((1,), (1,))
TN = ((0,), (0,))


def mm3(left, right, dims):
    left_high = left.astype(LOW)
    left_rest = (left - left_high.astype(FULL)).astype(LOW)
    right_high = right.astype(LOW)
    right_rest = (right - right_high.astype(FULL)).astype(LOW)
    return (
        mm(left_high, right_high, dims)
        + mm(left_high, right_rest, dims)
        + mm(left_rest, right_high, dims)
    )


def row_sum(value):
    return jnp.sum(value, axis=-1, keepdims=True)


def shift_down(value, count):
    if count == 0:
        return value
    row = lax.broadcasted_iota(jnp.int32, value.shape, 0)
    return jnp.where(row >= count, pltpu.roll(value, count, 0), 0.0)


def shift_up(value, count):
    if count == 0:
        return value
    rows = value.shape[0]
    row = lax.broadcasted_iota(jnp.int32, value.shape, 0)
    return jnp.where(row < rows - count, pltpu.roll(value, rows - count, 0), 0.0)


def conv_rows(projected, taps):
    count = taps.shape[0]
    total = projected * taps[count - 1 : count]
    for tap in range(count - 1):
        total = total + shift_down(projected, count - 1 - tap) * taps[tap : tap + 1]
    return total


def conv_back(grad, projected, taps):
    count = taps.shape[0]
    grad_in = grad * taps[count - 1 : count]
    grad_taps = [None] * count
    grad_taps[count - 1] = jnp.sum(grad * projected, axis=0, keepdims=True)
    for tap in range(count - 1):
        grad_in = grad_in + shift_up(grad, count - 1 - tap) * taps[tap : tap + 1]
        grad_taps[tap] = jnp.sum(
            grad * shift_down(projected, count - 1 - tap), axis=0, keepdims=True
        )
    return grad_in, grad_taps


def column_of(matrix, index):
    lane = lax.broadcasted_iota(jnp.int32, matrix.shape, 1)
    return row_sum(jnp.where(lane == index, matrix, 0.0))


def chunk_parts(rows):
    return [slice(start, start + CHUNK) for start in range(0, rows, CHUNK)]


def masks():
    row = lax.broadcasted_iota(jnp.int32, (CHUNK, CHUNK), 0)
    col = lax.broadcasted_iota(jnp.int32, (CHUNK, CHUNK), 1)
    return row, col


def sigmoid(value):
    return 1.0 / (1.0 + jnp.exp(-value))


def softplus(value):
    return jnp.maximum(value, 0.0) + jnp.log1p(jnp.exp(-jnp.abs(value)))


def full_dot(left, right):
    return lax.dot_general(
        left,
        right,
        (((1,), (0,)), ((), ())),
        precision=lax.Precision.HIGHEST,
        preferred_element_type=FULL,
    )


def decay_tables(alpha_ref, beta_ref, dlog_ref, dbias_ref, first_head, head_count, parts):
    row, col = masks()
    lower = jnp.where(row >= col, 1.0, 0.0)
    shifted = alpha_ref[...] + dbias_ref[...]
    decays = -jnp.exp(dlog_ref[...]) * softplus(shifted)
    running = [full_dot(lower, decays[part]) for part in parts]
    betas = sigmoid(beta_ref[...])
    tables = []
    for head in range(head_count):
        beta_col = column_of(betas, first_head + head)
        per_chunk = []
        for index, part in enumerate(parts):
            gamma = column_of(running[index], first_head + head)
            spread = jnp.broadcast_to(gamma, (CHUNK, CHUNK))
            spread = spread - spread.T
            causal = jnp.where(row >= col, jnp.exp(jnp.where(row >= col, spread, 0.0)), 0.0)
            last = gamma[CHUNK - 1 : CHUNK]
            per_chunk.append(
                (beta_col[part], jnp.exp(gamma), jnp.exp(last - gamma), jnp.exp(last), causal)
            )
        tables.append(per_chunk)
    return decays, betas, shifted, tables


def unit_inverse(value):
    return lax.rsqrt(row_sum(value * value) + EPSILON)


def mixer_forward_body(
    query_ref, key_ref, value_ref, gate_ref, beta_ref, alpha_ref, taps_ref, dlog_ref, dbias_ref,
    gain_ref, gated_ref, mixed_ref, fresh_ref, inverse_ref, state_ref,
):
    rows, width = query_ref.shape
    head_dim = gain_ref.shape[1]
    head_count = width // head_dim
    parts = chunk_parts(rows)
    first_head = pl.program_id(0) * head_count
    row, col = masks()
    tables = decay_tables(
        alpha_ref, beta_ref, dlog_ref, dbias_ref, first_head, head_count, parts
    )[3]
    units = [(head, index) for head in range(head_count) for index in range(len(parts))]
    queries, key_rows, values = {}, {}, {}
    for head in range(head_count):
        cols = slice(head * head_dim, (head + 1) * head_dim)
        conv_q = conv_rows(query_ref[:, cols], taps_ref[0, :, cols])
        conv_k = conv_rows(key_ref[:, cols], taps_ref[1, :, cols])
        conv_v = conv_rows(value_ref[:, cols], taps_ref[2, :, cols])
        act_q = conv_q * sigmoid(conv_q)
        act_k = conv_k * sigmoid(conv_k)
        query = (act_q * (unit_inverse(act_q) * (1.0 / math.sqrt(head_dim)))).astype(LOW)
        key_low = (act_k * unit_inverse(act_k)).astype(LOW)
        value = conv_v * sigmoid(conv_v)
        for index, part in enumerate(parts):
            queries[head, index] = query[part]
            key_rows[head, index] = key_low[part]
            values[head, index] = value[part]
    system, scores, inverse = {}, {}, {}
    for head, index in units:
        beta, _, _, _, causal = tables[head][index]
        key_blk = key_rows[head, index]
        system[head, index] = jnp.where(row > col, beta * mm(key_blk, key_blk, NT) * causal, 0.0)
        scores[head, index] = (mm(queries[head, index], key_blk, NT) * causal).astype(LOW)
    size = 1
    while size < CHUNK:
        own = (row // (2 * size) == col // (2 * size)) & (row // size != col // size)
        for unit in units:
            part = jnp.where(own, system[unit], 0.0)
            if size == 1:
                inverse[unit] = jnp.where(row == col, 1.0, 0.0) - part
            else:
                inverse_low = inverse[unit].astype(LOW)
                inverse[unit] = inverse[unit] - mm(mm(inverse_low, part), inverse_low)
        size *= 2
    gain = gain_ref[...]
    states = {head: jnp.zeros((head_dim, head_dim), FULL) for head in range(head_count)}
    for index, part in enumerate(parts):
        for head in range(head_count):
            unit = (head, index)
            cols = slice(head * head_dim, (head + 1) * head_dim)
            beta, start, tail, last, _ = tables[head][index]
            state = states[head]
            state_ref[head, index] = state.astype(LOW)
            inverse_low = inverse[unit].astype(LOW)
            inverse_ref[head, index] = inverse_low
            right = values[unit]
            if index:
                right = right - start * mm(key_rows[unit], state)
            fresh = mm(inverse_low, beta * right)
            fresh_low = fresh.astype(LOW)
            fresh_ref[part, cols] = fresh_low
            mixed = mm(scores[unit], fresh_low)
            if index:
                mixed = mixed + start * mm(queries[unit], state)
            mixed_ref[part, cols] = mixed
            if index + 1 < len(parts):
                grown = mm(key_rows[unit].astype(FULL) * tail, fresh_low, TN)
                states[head] = last * state + grown if index else grown
            gate = gate_ref[part, cols]
            scale = lax.rsqrt(jnp.mean(mixed * mixed, axis=-1, keepdims=True) + EPSILON)
            gated_ref[part, cols] = (mixed * scale * gain * (gate * sigmoid(gate))).astype(LOW)


def mixer_backward_body(
    grad_ref, query_ref, key_ref, value_ref, gate_ref, beta_ref, alpha_ref, taps_ref, dlog_ref,
    dbias_ref, gain_ref, mixed_ref, fresh_ref, inverse_ref, state_ref,
    dquery_ref, dkey_ref, dvalue_ref, dgate_ref, dbeta_ref, dalpha_ref, dtaps_ref, ddlog_ref,
    ddbias_ref, dgain_ref,
):
    rows, width = query_ref.shape
    head_dim = gain_ref.shape[1]
    head_count = width // head_dim
    parts = chunk_parts(rows)
    step = pl.program_id(0)
    first_head = step * head_count
    row, col = masks()
    decays, betas, shifted, tables = decay_tables(
        alpha_ref, beta_ref, dlog_ref, dbias_ref, first_head, head_count, parts
    )
    upper = jnp.where(row <= col, 1.0, 0.0)
    units = [(head, index) for head in range(head_count) for index in range(len(parts))]
    gain = gain_ref[...]
    root = 1.0 / math.sqrt(head_dim)

    @pl.when(step == 0)
    def _():
        dbeta_ref[...] = jnp.zeros_like(dbeta_ref)
        dalpha_ref[...] = jnp.zeros_like(dalpha_ref)
        ddlog_ref[...] = jnp.zeros_like(ddlog_ref)
        ddbias_ref[...] = jnp.zeros_like(ddbias_ref)
        dgain_ref[...] = jnp.zeros_like(dgain_ref)

    queries, key_rows, values, grads, acts, convs = {}, {}, {}, {}, {}, {}
    for head in range(head_count):
        cols = slice(head * head_dim, (head + 1) * head_dim)
        conv_q = conv_rows(query_ref[:, cols], taps_ref[0, :, cols])
        conv_k = conv_rows(key_ref[:, cols], taps_ref[1, :, cols])
        conv_v = conv_rows(value_ref[:, cols], taps_ref[2, :, cols])
        act_q = conv_q * sigmoid(conv_q)
        act_k = conv_k * sigmoid(conv_k)
        value = conv_v * sigmoid(conv_v)
        norm_q, norm_k = unit_inverse(act_q), unit_inverse(act_k)
        query, key_full = act_q * norm_q, act_k * norm_k
        convs[head] = (conv_q, conv_k, conv_v)
        acts[head] = (query, norm_q, key_full, norm_k)
        mixed = mixed_ref[:, cols]
        gate = gate_ref[:, cols]
        sig = sigmoid(gate)
        grad = grad_ref[:, cols]
        scale = lax.rsqrt(jnp.mean(mixed * mixed, axis=-1, keepdims=True) + EPSILON)
        normal = mixed * scale
        opened = gate * sig
        dgain_ref[...] += jnp.sum(grad * normal * opened, axis=0, keepdims=True)
        dgate_ref[:, cols] = (
            grad * normal * gain * (sig * (1.0 + gate * (1.0 - sig)))
        ).astype(LOW)
        grad_normal = grad * gain * opened
        grad_mixed = scale * (
            grad_normal - normal * jnp.mean(grad_normal * normal, axis=-1, keepdims=True)
        )
        for index, part in enumerate(parts):
            queries[head, index] = query[part] * root
            key_rows[head, index] = key_full[part]
            values[head, index] = value[part]
            grads[head, index] = grad_mixed[part]
    cross, scores, system, strict = {}, {}, {}, {}
    for unit in units:
        head, index = unit
        beta, _, _, _, causal = tables[head][index]
        cross[unit] = mm3(queries[unit], key_rows[unit], NT)
        scores[unit] = (cross[unit] * causal).astype(LOW)
        strict[unit] = jnp.where(row > col, beta * causal, 0.0)
        system[unit] = mm3(key_rows[unit], key_rows[unit], NT)
    grad_states = {head: None for head in range(head_count)}
    grad_q, grad_k, grad_v, gamma_grads = {}, {}, {}, {}
    grad_beta = {}
    for index in reversed(range(len(parts))):
        part = parts[index]
        for head in range(head_count):
            unit = (head, index)
            cols = slice(head * head_dim, (head + 1) * head_dim)
            beta, start, tail, last, causal = tables[head][index]
            query, key_full = queries[unit], key_rows[unit]
            query_low, key_low = query.astype(LOW), key_full.astype(LOW)
            grad = grads[unit]
            grad_low = grad.astype(LOW)
            fresh_low = fresh_ref[part, cols]
            fresh = fresh_low.astype(FULL)
            state = state_ref[head, index]
            grad_state = grad_states[head]
            grad_fresh = mm(scores[unit], grad_low, TN)
            if grad_state is not None:
                grad_state_low = grad_state.astype(LOW)
                grad_fresh = grad_fresh + mm(key_full * tail, grad_state_low)
            grad_right = mm(inverse_ref[head, index], grad_fresh, TN)
            grad_right_low = grad_right.astype(LOW)
            grad_cross = mm(grad_low, fresh_low, NT) * causal
            grad_system = -(mm(grad_right_low, fresh_low, NT) * strict[unit])
            turned = grad_cross * cross[unit] + grad_system * system[unit]
            gamma = row_sum(turned) - row_sum(turned.T)
            grad_cross_low = grad_cross.astype(LOW)
            grad_system_low = grad_system.astype(LOW)
            dquery = mm(grad_cross_low, key_low)
            dkey = (
                mm(grad_system_low, key_low)
                + mm(grad_system_low, key_low, TN)
                + mm(grad_cross_low, query_low, TN)
            )
            back = -beta * start * grad_right
            if index:
                back_low = back.astype(LOW)
                dquery = dquery + start * mm(grad_low, state, NT)
                dkey = dkey + mm(back_low, state, NT)
                gamma = gamma + row_sum(grad * start * mm(query_low, state))
                gamma = gamma + row_sum(back * mm(key_low, state))
            final = None
            if grad_state is not None:
                grad_tail = mm(fresh_low, grad_state_low, NT) * tail
                dkey = dkey + grad_tail
                tail_term = row_sum(grad_tail * key_full)
                gamma = gamma - tail_term
                final = jnp.sum(tail_term, axis=0, keepdims=True)
                if index:
                    final = final + last * jnp.sum(
                        row_sum(state.astype(FULL) * grad_state), axis=0, keepdims=True
                    )
                is_last = lax.broadcasted_iota(jnp.int32, gamma.shape, 0) == CHUNK - 1
                gamma = gamma + jnp.where(is_last, final, 0.0)
            gamma_grads[unit] = gamma
            grad_beta[unit] = (1.0 - beta) * row_sum(grad_right * fresh)
            grad_q[unit], grad_k[unit], grad_v[unit] = dquery, dkey, beta * grad_right
            if index:
                grown = mm(query * start, grad_low, TN) + mm(key_low, back_low, TN)
                if grad_state is not None:
                    grown = grown + last * grad_state
                grad_states[head] = grown
    lane = lax.broadcasted_iota(jnp.int32, (CHUNK, alpha_ref.shape[1]), 1)
    for index, part in enumerate(parts):
        gamma_cols = jnp.zeros(lane.shape, FULL)
        beta_cols = jnp.zeros(lane.shape, FULL)
        for head in range(head_count):
            gamma_cols = jnp.where(lane == first_head + head, gamma_grads[head, index], gamma_cols)
            beta_cols = jnp.where(lane == first_head + head, grad_beta[head, index], beta_cols)
        grad_decay = full_dot(upper, gamma_cols)
        grad_alpha = grad_decay * -jnp.exp(dlog_ref[...]) * sigmoid(shifted[part])
        dbeta_ref[part] += beta_cols
        dalpha_ref[part] += grad_alpha
        ddbias_ref[...] += jnp.sum(grad_alpha, axis=0, keepdims=True)
        ddlog_ref[...] += jnp.sum(grad_decay * decays[part], axis=0, keepdims=True)
    for head in range(head_count):
        cols = slice(head * head_dim, (head + 1) * head_dim)
        query, norm_q, key_full, norm_k = acts[head]
        dquery = jnp.concatenate([grad_q[head, index] for index in range(len(parts))], axis=0)
        dkey = jnp.concatenate([grad_k[head, index] for index in range(len(parts))], axis=0)
        dvalue = jnp.concatenate([grad_v[head, index] for index in range(len(parts))], axis=0)
        act_grads = (
            norm_q * root * (dquery - query * row_sum(query * dquery)),
            norm_k * (dkey - key_full * row_sum(key_full * dkey)),
            dvalue,
        )
        projected = (query_ref, key_ref, value_ref)
        for which, out_ref in enumerate((dquery_ref, dkey_ref, dvalue_ref)):
            conv = convs[head][which]
            sig = sigmoid(conv)
            grad_conv = act_grads[which] * sig * (1.0 + conv * (1.0 - sig))
            grad_in, grad_taps = conv_back(
                grad_conv, projected[which][:, cols], taps_ref[which, :, cols]
            )
            out_ref[:, cols] = grad_in.astype(LOW)
            for tap, entry in enumerate(grad_taps):
                dtaps_ref[which, tap : tap + 1, cols] = entry


def mixer_specs(rows, heads, group, head_dim, taps_shape):
    width = group * head_dim
    wide = pl.BlockSpec((rows, width), lambda step: (0, step))
    narrow = pl.BlockSpec((rows, heads), lambda step: (0, 0))
    taps = pl.BlockSpec(taps_shape[:2] + (width,), lambda step: (0, 0, step))
    small = pl.BlockSpec((1, heads), lambda step: (0, 0))
    gain = pl.BlockSpec((1, head_dim), lambda step: (0, 0))
    chunks = rows // CHUNK
    square = pl.BlockSpec((group, chunks, CHUNK, CHUNK), lambda step: (step, 0, 0, 0))
    state = pl.BlockSpec((group, chunks, head_dim, head_dim), lambda step: (step, 0, 0, 0))
    return wide, narrow, taps, small, gain, square, state


def mixer_forward(projections, conv_taps, decay_log, decay_bias, norm_head):
    query, key_rows, value, gate, beta, alpha = projections
    rows, width = query.shape
    heads, head_dim = decay_log.shape[0], norm_head.shape[0]
    group = 2 if heads % 2 == 0 else 1
    chunks = rows // CHUNK
    wide, narrow, taps, small, gain, square, state = mixer_specs(
        rows, heads, group, head_dim, conv_taps.shape
    )
    return pl.pallas_call(
        mixer_forward_body,
        grid=(heads // group,),
        in_specs=[wide] * 4 + [narrow] * 2 + [taps, small, small, gain],
        out_specs=[wide, wide, wide, square, state],
        out_shape=[
            jax.ShapeDtypeStruct((rows, width), LOW),
            jax.ShapeDtypeStruct((rows, width), FULL),
            jax.ShapeDtypeStruct((rows, width), LOW),
            jax.ShapeDtypeStruct((heads, chunks, CHUNK, CHUNK), LOW),
            jax.ShapeDtypeStruct((heads, chunks, head_dim, head_dim), LOW),
        ],
        compiler_params=pltpu.CompilerParams(
            vmem_limit_bytes=48 * 1024 * 1024, dimension_semantics=("arbitrary",)
        ),
        name="mixer_forward",
    )(
        query, key_rows, value, gate, beta, alpha, conv_taps,
        decay_log.reshape(1, heads), decay_bias.reshape(1, heads), norm_head.reshape(1, head_dim),
    )


def mixer_backward(grad, projections, conv_taps, decay_log, decay_bias, norm_head, kept):
    query, key_rows, value, gate, beta, alpha = projections
    mixed, fresh, inverse, states = kept
    rows, width = query.shape
    heads, head_dim = decay_log.shape[0], norm_head.shape[0]
    group = 2 if heads % 2 == 0 else 1
    wide, narrow, taps, small, gain, square, state = mixer_specs(
        rows, heads, group, head_dim, conv_taps.shape
    )
    return pl.pallas_call(
        mixer_backward_body,
        grid=(heads // group,),
        in_specs=[wide] * 5
        + [narrow] * 2
        + [taps, small, small, gain, wide, wide, square, state],
        out_specs=[wide] * 4 + [narrow] * 2 + [taps, small, small, gain],
        out_shape=[jax.ShapeDtypeStruct((rows, width), LOW)] * 4
        + [jax.ShapeDtypeStruct((rows, heads), FULL)] * 2
        + [
            jax.ShapeDtypeStruct(conv_taps.shape, FULL),
            jax.ShapeDtypeStruct((1, heads), FULL),
            jax.ShapeDtypeStruct((1, heads), FULL),
            jax.ShapeDtypeStruct((1, head_dim), FULL),
        ],
        compiler_params=pltpu.CompilerParams(
            vmem_limit_bytes=48 * 1024 * 1024, dimension_semantics=("arbitrary",)
        ),
        name="mixer_backward",
    )(
        grad, query, key_rows, value, gate, beta, alpha, conv_taps,
        decay_log.reshape(1, heads), decay_bias.reshape(1, heads), norm_head.reshape(1, head_dim),
        mixed, fresh, inverse, states,
    )


def rms_scale(vector, gain):
    return vector * lax.rsqrt(jnp.mean(vector * vector, axis=-1, keepdims=True) + EPSILON) * gain


def rms_back(grad_norm, vector, gain):
    inverse = lax.rsqrt(jnp.mean(vector * vector, axis=-1, keepdims=True) + EPSILON)
    normal = vector * inverse
    scaled = grad_norm * gain
    return inverse * (scaled - normal * jnp.mean(scaled * normal, axis=-1, keepdims=True))


def scatter_sum(partial_sum):
    return lax.psum_scatter(
        partial_sum.astype(LOW), "head", scatter_dimension=0, tiled=True
    ).astype(FULL)


def gather(own):
    return lax.all_gather(own, "head", axis=0, tiled=True)


def per_device(
    tokens, cotangent, lengths, norm_in, w_query, w_key, w_value, w_gate, w_beta, w_alpha,
    conv_taps, decay_log, decay_bias, norm_head, w_out, norm_mid, w_up_gate, w_up, w_down,
):
    micro_count, seq_len, model_dim = tokens.shape
    head_parts = lax.axis_size("head")
    batch_parts = lax.axis_size("batch")
    own_len = seq_len // head_parts
    first_row = lax.axis_index("head") * own_len
    positions = lax.broadcasted_iota(jnp.int32, (seq_len, 1), 0)
    in_weights = (w_query, w_key, w_value, w_gate, w_beta, w_alpha)

    def own_of(value):
        return lax.dynamic_slice_in_dim(value, first_row, own_len, 0)

    micros = []
    for micro in range(micro_count):
        rows = tokens[micro].astype(FULL)
        keep = (positions < lengths[micro, 0]).astype(FULL)
        normed = rms_scale(rows, norm_in).astype(LOW)
        projections = tuple(mm(normed, weight) for weight in in_weights)
        gated, *kept = mixer_forward(projections, conv_taps, decay_log, decay_bias, norm_head)
        out_part = scatter_sum(mm(gated, w_out))
        micros.append(
            dict(rows=own_of(rows), keep=keep, keep_own=own_of(keep), normed=normed,
                 projections=projections, gated=gated, kept=kept, out_part=out_part)
        )
    for micro in range(micro_count):
        held = micros[micro]
        middle = held["rows"] + held["keep_own"] * held["out_part"]
        mid = gather(rms_scale(middle, norm_mid).astype(LOW))
        grad_rows = cotangent[micro].astype(FULL)
        down_grad = (held["keep"] * grad_rows).astype(LOW)
        gate_act = mm(mid, w_up_gate)
        up_act = mm(mid, w_up)
        sig = jax.nn.sigmoid(gate_act)
        hidden = (gate_act * sig * up_act).astype(LOW)
        grad_hidden = mm(down_grad, w_down, NT)
        grad_gate = (grad_hidden * up_act * sig * (1.0 + gate_act * (1.0 - sig))).astype(LOW)
        grad_up = (grad_hidden * gate_act * sig).astype(LOW)
        mid_part = scatter_sum(mm(grad_gate, w_up_gate, NT) + mm(grad_up, w_up, NT))
        down_part = scatter_sum(mm(hidden, w_down))
        out_own = (middle + held["keep_own"] * down_part).astype(LOW)
        held.update(
            middle=middle, mid=mid, down_grad=down_grad, hidden=hidden, grad_gate=grad_gate,
            grad_up=grad_up, mid_part=mid_part, grad_rows=own_of(grad_rows), out=gather(out_own),
        )

    def both(name):
        return jnp.concatenate([held[name] for held in micros], axis=0)

    def shared(left, right):
        return lax.psum_scatter(
            mm(left, right, TN).astype(LOW), "batch", scatter_dimension=0, tiled=True
        ).astype(FULL)

    mid_both, down_both = both("mid"), both("down_grad")
    share_up_gate = shared(mid_both, both("grad_gate"))
    share_up = shared(mid_both, both("grad_up"))
    share_down = shared(down_both, both("hidden")).T
    gain_in = jnp.zeros((model_dim,), FULL)
    gain_mid = jnp.zeros((model_dim,), FULL)
    small = None
    for micro in range(micro_count):
        held = micros[micro]
        middle = held["middle"]
        gain_mid = gain_mid + jnp.sum(rms_scale(middle, 1.0) * held["mid_part"], axis=0)
        grad_middle = held["grad_rows"] + rms_back(held["mid_part"], middle, norm_mid)
        attn = gather((held["keep_own"] * grad_middle).astype(LOW))
        *grads, grad_taps, grad_dlog, grad_dbias, grad_gain = mixer_backward(
            mm(attn, w_out, NT), held["projections"], conv_taps, decay_log, decay_bias,
            norm_head, held["kept"],
        )
        grads = [entry.astype(LOW) for entry in grads]
        in_part = mm(grads[0], in_weights[0], NT)
        for index in range(1, len(in_weights)):
            in_part = in_part + mm(grads[index], in_weights[index], NT)
        in_part = scatter_sum(in_part)
        gain_in = gain_in + jnp.sum(rms_scale(held["rows"], 1.0) * in_part, axis=0)
        grad_own = (grad_middle + rms_back(in_part, held["rows"], norm_in)).astype(LOW)
        entries = (grad_taps, grad_dlog, grad_dbias, grad_gain)
        small = entries if small is None else tuple(a + b for a, b in zip(small, entries))
        held.update(attn=attn, grads=grads, grad_tokens=gather(grad_own))
    normed_both = both("normed")
    grads_both = [
        jnp.concatenate([held["grads"][index] for held in micros], axis=0) for index in range(6)
    ]
    share_in = [shared(normed_both, grads_both[index]) for index in range(4)]
    share_out = shared(both("attn"), both("gated")).T
    tiny = mm(jnp.concatenate(grads_both[4:], axis=1), normed_both, TN)
    grad_taps, grad_dlog, grad_dbias, grad_gain = small
    gains = lax.psum((gain_in, grad_gain[0], gain_mid), ("batch", "head"))
    tiny, grad_taps, grad_dlog, grad_dbias = lax.psum(
        (tiny, grad_taps, grad_dlog[0], grad_dbias[0]), "batch"
    )
    width = model_dim // batch_parts
    tiny = lax.dynamic_slice_in_dim(tiny, lax.axis_index("batch") * width, width, 1).T
    count = w_beta.shape[1]
    return (
        jnp.stack([held["out"] for held in micros]),
        jnp.stack([held["grad_tokens"] for held in micros]),
        gains[0],
        share_in[0], share_in[1], share_in[2], share_in[3],
        tiny[:, :count], tiny[:, count:],
        grad_taps, grad_dlog, grad_dbias, gains[1],
        share_out, gains[2], share_up_gate, share_up, share_down,
    )


def solution(mesh):
    tokens, column, row = P(None, "batch", None), P(None, "head"), P("head", None)
    placed = (
        tokens, tokens, P(None, "batch"), P(), column, column, column, column, column, column,
        P(None, None, "head"), P("head"), P("head"), P(), row, P(), column, column, row,
    )
    block, turned = P("batch", "head"), P("head", "batch")
    return jax.shard_map(
        per_device,
        mesh=mesh,
        in_specs=placed,
        out_specs=(
            tokens, tokens, P(), block, block, block, block, block, block,
            P(None, None, "head"), P("head"), P("head"), P(), turned, P(), block, block, turned,
        ),
        check_vma=False,
    )
```

time: 2620 us -> 1200 us (0.46)
  other arithmetic: 839 us -> 70.4 us
  local copies, waits for them, and re-layouts: 482 us -> 31.4 us
  matrix products: 597 us -> 157 us
  waiting for transfers between devices: 594 us -> 798 us
  Pallas kernels: 0 us -> 46.7 us
    another operation x153 -> x2, other arithmetic: 554 us -> 7.66 us  [the longest x1 3.83 us: per_device(): jnp.stack([held['out'] for held in micros])]
    reduce_scatter x1 -> x16, waiting for transfers between devices: 87.5 us -> 584 us  [the longest x8 392 us: shared(): lax.psum_scatter(mm(left, right, TN).astype(LOW), 'batch', scatter_dimens...]
    psum x4 -> x1, waiting for transfers between devices: 506 us -> 50.4 us  [per_device(): lax.psum((tiny, grad_taps, grad_dlog[0], grad_dbias[0]), 'batch')]
    dot_general x288 -> x49, matrix products: 542 us -> 157 us  [mm(): lax.dot_general(left.astype(LOW), right.astype(LOW), (dims, ((), ())), pr...]
    concatenate x2 -> x1, local copies, waits for them, and re-layouts: 258 us -> 0.16 us  [both(): return jnp.concatenate([held[name] for held in micros], axis=0)]
    all_gather x0 -> x8, waiting for transfers between devices: none -> 162 us  [gather(): return lax.all_gather(own, 'head', axis=0, tiled=True)]
    reduce_sum x66 -> x4, other arithmetic: 89.3 us -> 7.66 us  [the longest x2 3.94 us: per_device(): jnp.sum(rms_scale(middle, 1.0) * held['mid_part'], axis=0)]
    dynamic_update_slice x72 -> x0, other arithmetic: 70 us -> none  [head_rule(): lax.scan(one_block, start_state, (blocked(query_seq), blocked(key_seq), b...]
  transfers between devices with their start and end apart: 5 -> 25, of which waited for: 4 -> 22; matrix products, arithmetic and copies ran while one was open for 15% -> 12% of each run, Pallas kernels for 0% -> 2%
where the time goes in v1:
time: 1200 us; the launch traced here: 1190 us
  waiting for transfers between devices  798 us (66%)
  matrix products  157 us (13%)
  other arithmetic  70.4 us (6%)
  blocking collectives  67 us (6%)
  Pallas kernels  46.7 us (4%)
  local copies, waits for them, and re-layouts  31.4 us (3%)
  between operations  16.3 us (1%)
    reduce_scatter x8, waiting for transfers between devices, shared(): lax.psum_scatter(mm(left, right, TN).astype(LOW), 'batch', scatter_dimens...  392 us
    reduce_scatter x8, waiting for transfers between devices, scatter_sum(): lax.psum_scatter(partial_sum.astype(LOW), 'head', scatter_dimension=0, ti...  191 us
    all_gather x8, waiting for transfers between devices, gather(): return lax.all_gather(own, 'head', axis=0, tiled=True)  162 us
    dot_general x49, matrix products, mm(): lax.dot_general(left.astype(LOW), right.astype(LOW), (dims, ((), ())), pr...  157 us
    psum x1, waiting for transfers between devices, per_device(): lax.psum((tiny, grad_taps, grad_dlog[0], grad_dbias[0]), 'batch')  50.4 us
    psum x1, blocking collectives, per_device(): gains = lax.psum((gain_in, grad_gain[0], gain_mid), ('batch', 'head'))  42 us
    unnamed x275, local copies, waits for them, and re-layouts  29 us
    pallas_call x2, Pallas kernels, mixer_backward(): pl.pallas_call(mixer_backward_body, grid=(heads // group,), in_specs=[wid...  28.7 us
  transfers between devices with their start and end apart: 25, of which 22 were waited for; matrix products, arithmetic and copies ran while one was open for 12% of the time, Pallas kernels for 2%

profile of v1, /device:TPU:0, one launch (start us, length us, event | category | flops | bytes accessed | tf_op | source)
XLA Modules:
  0.0 1189.8 jit_solution(10747554911275172579)
XLA Ops:
  20.2 9.0 mixer_forward.2
  35.8 5.4 slice_convert_fusion.3
  41.3 31.4 %reduce-scatter.17.cloned.1.call-done = bf16[96,2048]{1,0:T(8,128)(2,1)} async-done(((bf16[384,2048]{1,0:T(8,128)(2,1)}), bf16[96,2048]{1,0:T(8,128)(2,1)}) %reduce-scatter.17.cloned.1.call-update) | async-done | bytes 393232 | tf_op jit(solution)/shard_map/reduce_scatter | solution.py:476
  77.6 4.1 fusion.8
  81.7 30.3 %all-gather.9.cloned.1.call-done = bf16[384,2048]{1,0:T(8,128)(2,1)} async-done(((bf16[96,2048]{1,0:T(8,128)(2,1)}), bf16[384,2048]{1,0:T(8,128)(2,1)}) %all-gather.9.cloned.1.call-update) | async-done | bytes 1572880 | tf_op jit(solution)/shard_map/all_gather | solution.py:482
  112.0 5.8 fusion.100
  117.9 6.7 fusion.99
  124.7 7.0 multiply_convert_fusion.2
  134.4 3.9 add_convert_fusion.3
  138.3 6.8 convolution_convert_fusion.8
  145.1 5.6 slice_convert_fusion.1
  150.7 21.8 %reduce-scatter.25.cloned.1.call-done = bf16[96,2048]{1,0:T(8,128)(2,1)} async-done(((bf16[384,2048]{1,0:T(8,128)(2,1)}), bf16[96,2048]{1,0:T(8,128)(2,1)}) %reduce-scatter.25.cloned.1.call-update) | async-done | bytes 393232 | tf_op jit(solution)/shard_map/reduce_scatter | solution.py:476
  174.4 34.6 %reduce-scatter.19.cloned.1.call-done = bf16[96,2048]{1,0:T(8,128)(2,1)} async-done(((bf16[384,2048]{1,0:T(8,128)(2,1)}), bf16[96,2048]{1,0:T(8,128)(2,1)}) %reduce-scatter.19.cloned.1.call-update) | async-done | bytes 393232 | tf_op jit(solution)/shard_map/reduce_scatter | solution.py:476
  223.3 9.0 mixer_forward.3
  238.7 9.2 all-gather.17.cloned.1.call-done
  250.5 14.4 %mixer_backward.2 = (bf16[384,512]{1,0:T(8,128)(2,1)S(1)}, bf16[384,512]{1,0:T(8,128)(2,1)S(1)}, bf16[384,512]{1,0:T(8,128)(2,1)S(1)}, bf16[384,512]{1,0:T(8,128...) custom-call(f32[384,512]{1,0:T(8,128)S(1)} %fusion.110.grad_ref, ...), custom_call_target="tpu_custom_call" | custom-call | tf_op jit(solution)/shard_map/mixer_backward/pallas_call | solution.py:438
  276.1 8.2 reduce-scatter.21.cloned.1.call-done
  287.2 33.6 %reduce-scatter.27.cloned.1.call-done = bf16[96,2048]{1,0:T(8,128)(2,1)} async-done(((bf16[384,2048]{1,0:T(8,128)(2,1)}), bf16[96,2048]{1,0:T(8,128)(2,1)}) %reduce-scatter.27.cloned.1.call-update) | async-done | bytes 393232 | tf_op jit(solution)/shard_map/reduce_scatter | solution.py:476
  326.4 36.1 %all-gather.13.cloned.1.call-done = bf16[384,2048]{1,0:T(8,128)(2,1)} async-done(((bf16[96,2048]{1,0:T(8,128)(2,1)}), bf16[384,2048]{1,0:T(8,128)(2,1)}) %all-gather.13.cloned.1.call-update) | async-done | bytes 1572880 | tf_op jit(solution)/shard_map/all_gather | solution.py:482
  362.6 5.8 fusion.107
  368.5 6.7 fusion.108
  375.3 7.0 multiply_convert_fusion
  388.8 6.8 convolution_convert_fusion.7
  395.6 27.4 %reduce-scatter.29.cloned.1.call-done = bf16[96,2048]{1,0:T(8,128)(2,1)} async-done(((bf16[384,2048]{1,0:T(8,128)(2,1)}), bf16[96,2048]{1,0:T(8,128)(2,1)}) %reduce-scatter.29.cloned.1.call-update) | async-done | bytes 393232 | tf_op jit(solution)/shard_map/reduce_scatter | solution.py:476
  425.2 34.3 %reduce-scatter.23.cloned.1.call-done = bf16[96,2048]{1,0:T(8,128)(2,1)} async-done(((bf16[384,2048]{1,0:T(8,128)(2,1)}), bf16[96,2048]{1,0:T(8,128)(2,1)}) %reduce-scatter.23.cloned.1.call-update) | async-done | bytes 393232 | tf_op jit(solution)/shard_map/reduce_scatter | solution.py:476
  462.6 36.0 %all-gather.21.cloned.1.call-done = bf16[384,2048]{1,0:T(8,128)(2,1)} async-done(((bf16[96,2048]{1,0:T(8,128)(2,1)}), bf16[384,2048]{1,0:T(8,128)(2,1)}) %all-gather.21.cloned.1.call-update) | async-done | bytes 1572880 | tf_op jit(solution)/shard_map/all_gather | solution.py:482
  501.8 14.3 %mixer_backward.3 = (bf16[384,512]{1,0:T(8,128)(2,1)S(1)}, bf16[384,512]{1,0:T(8,128)(2,1)S(1)}, bf16[384,512]{1,0:T(8,128)(2,1)S(1)}, bf16[384,512]{1,0:T(8,128...) custom-call(f32[384,512]{1,0:T(8,128)S(1)} %fusion.117.grad_ref, ...), custom_call_target="tpu_custom_call" | custom-call | tf_op jit(solution)/shard_map/mixer_backward/pallas_call | solution.py:438
  531.2 5.1 fusion.15
  536.3 9.0 convolution_convert_fusion
  550.0 7.1 convolution_convert_fusion.1
  558.4 8.6 convolution_convert_fusion.2
  568.0 5.3 convolution_convert_fusion.3
  573.7 5.0 convolution_convert_fusion.4
  578.8 5.2 convolution_convert_fusion.5
  584.1 5.1 convolution_convert_fusion.6
  594.5 25.1 %all-reduce.1 = (f32[3,4,512]{2,1,0:T(4,128)}, f32[4]{0:T(128)}, f32[4]{0:T(128)}) all-reduce(f32[3,4,512]{2,1,0:T(4,128)S(1)} %add.234, f32[4]{0:T(128)S(1)} %add_bitcast_fusion.2, f32[4]{0:T(128)S(1)} %add_bitcast_fusion.1), channel_id=1, replica_groups=mesh['batch'=8,'head'=4] {'batch'}, use_global_device_ids=true, to_apply=%region_26.0 | all-reduce | flops 6152 | bytes 49216 | tf_op jit(solution)/shard_map/psum | solution.py:577
  619.6 16.9 %all-gather.15.cloned.1.call-done = bf16[384,2048]{1,0:T(8,128)(2,1)} async-done(((bf16[96,2048]{1,0:T(8,128)(2,1)}), bf16[384,2048]{1,0:T(8,128)(2,1)}) %all-gather.15.cloned.1.call-update) | async-done | bytes 1572880 | tf_op jit(solution)/shard_map/all_gather | solution.py:482
  640.3 50.4 %all-reduce.4.cloned.1.call-done = f32[8,2048]{1,0:T(8,128)} async-done(((f32[8,2048]{1,0:T(8,128)}), f32[8,2048]{1,0:T(8,128)}) %all-reduce.4.cloned.1.call-update) | async-done | bytes 65552 | tf_op jit(solution)/shard_map/psum | solution.py:577
  692.0 42.9 %reduce-scatter.41.cloned.1.call-done = bf16[256,512]{1,0:T(8,128)(2,1)} async-done(((bf16[2048,512]{1,0:T(8,128)(2,1)}), bf16[256,512]{1,0:T(8,128)(2,1)}) %reduce-scatter.41.cloned.1.call-update) | async-done | bytes 262160 | tf_op jit(solution)/shard_map/reduce_scatter | solution.py:537
  736.9 60.4 %reduce-scatter.47.cloned.1.call-done = bf16[256,1408]{1,0:T(8,128)(2,1)} async-done(((bf16[2048,1408]{1,0:T(8,128)(2,1)}), bf16[256,1408]{1,0:T(8,128)(2,1)}) %reduce-scatter.47.cloned.1.call-update) | async-done | bytes 720912 | tf_op jit(solution)/shard_map/reduce_scatter | solution.py:537
  802.4 57.5 %reduce-scatter.45.cloned.1.call-done = bf16[256,1408]{1,0:T(8,128)(2,1)} async-done(((bf16[2048,1408]{1,0:T(8,128)(2,1)}), bf16[256,1408]{1,0:T(8,128)(2,1)}) %reduce-scatter.45.cloned.1.call-update) | async-done | bytes 720912 | tf_op jit(solution)/shard_map/reduce_scatter | solution.py:537
  862.3 60.2 %reduce-scatter.43.cloned.1.call-done = bf16[256,1408]{1,0:T(8,128)(2,1)} async-done(((bf16[2048,1408]{1,0:T(8,128)(2,1)}), bf16[256,1408]{1,0:T(8,128)(2,1)}) %reduce-scatter.43.cloned.1.call-update) | async-done | bytes 720912 | tf_op jit(solution)/shard_map/reduce_scatter | solution.py:537
  924.8 42.4 %reduce-scatter.39.cloned.1.call-done = bf16[256,512]{1,0:T(8,128)(2,1)} async-done(((bf16[2048,512]{1,0:T(8,128)(2,1)}), bf16[256,512]{1,0:T(8,128)(2,1)}) %reduce-scatter.39.cloned.1.call-update) | async-done | bytes 262160 | tf_op jit(solution)/shard_map/reduce_scatter | solution.py:537
  969.0 42.7 %reduce-scatter.37.cloned.1.call-done = bf16[256,512]{1,0:T(8,128)(2,1)} async-done(((bf16[2048,512]{1,0:T(8,128)(2,1)}), bf16[256,512]{1,0:T(8,128)(2,1)}) %reduce-scatter.37.cloned.1.call-update) | async-done | bytes 262160 | tf_op jit(solution)/shard_map/reduce_scatter | solution.py:537
  1013.5 43.1 %reduce-scatter.35.cloned.1.call-done = bf16[256,512]{1,0:T(8,128)(2,1)} async-done(((bf16[2048,512]{1,0:T(8,128)(2,1)}), bf16[256,512]{1,0:T(8,128)(2,1)}) %reduce-scatter.35.cloned.1.call-update) | async-done | bytes 262160 | tf_op jit(solution)/shard_map/reduce_scatter | solution.py:537
  1058.4 43.3 %reduce-scatter.33.cloned.1.call-done = bf16[256,512]{1,0:T(8,128)(2,1)} async-done(((bf16[2048,512]{1,0:T(8,128)(2,1)}), bf16[256,512]{1,0:T(8,128)(2,1)}) %reduce-scatter.33.cloned.1.call-update) | async-done | bytes 262160 | tf_op jit(solution)/shard_map/reduce_scatter | solution.py:537
  1103.5 42.0 %all-reduce = (f32[2048]{0:T(1024)}, f32[128]{0:T(128)}, f32[2048]{0:T(1024)}) all-reduce(f32[2048]{0:T(1024)S(1)} %add.232, f32[128]{0:T(128)S(1)} %add_bitcast_fusion, f32[2048]{0:T(1024)S(1)} %add.238), channel_id=1, replica_groups=mesh['batch'=8,'head'=4] {'batch','head'}, use_global_device_ids=true, to_apply=%region_20.0 | all-reduce | flops 4224 | bytes 33792 | tf_op jit(solution)/shard_map/psum | solution.py:576
  1145.5 33.5 %all-gather.23.cloned.1.call-done = bf16[384,2048]{1,0:T(8,128)(2,1)} async-done(((bf16[96,2048]{1,0:T(8,128)(2,1)}), bf16[384,2048]{1,0:T(8,128)(2,1)}) %all-gather.23.cloned.1.call-update) | async-done | bytes 1572880 | tf_op jit(solution)/shard_map/all_gather | solution.py:482
  (419 shorter events, 141.5 us)
Async XLA Ops:
  7.2 25.2 %copy-start = (bf16[512,2048]{1,0:T(8,128)(2,1)S(1)}, bf16[512,2048]{1,0:T(8,128)(2,1)}, u32[]{:S(2)}) copy-start(bf16[512,2048]{1,0:T(8,128)(2,1)} %param.33) | copy-start | bytes 6291460
  7.2 65.5 %reduce-scatter.17.cloned.1.call-start = ((), (), s32[]{:S(2)}) async-start(), calls=%async_computation.16 | async-start | bytes 1966080 | tf_op jit(solution)/shard_map/reduce_scatter | solution.py:476
  18.9 10.3 copy-start.10
  20.1 11.5 copy-start.11
  34.5 77.5 %all-gather.9.cloned.1.call-start = ((), (), s32[]{:S(2)}) async-start(), calls=%async_computation.17 | async-start | bytes 1966080 | tf_op jit(solution)/shard_map/all_gather | solution.py:482
  35.8 39.0 %copy-start.92 = (f32[2048]{0:T(1024)S(1)}, f32[2048]{0:T(1024)}, u32[]{:S(2)}) copy-start(f32[2048]{0:T(1024)} %param.34) | copy-start | bytes 24580
  74.8 134.3 %copy-start.64 = (f32[96,2048]{1,0:T(8,128)}, f32[96,2048]{1,0:T(8,128)S(1)}, u32[]{:S(2)}) copy-start(f32[96,2048]{1,0:T(8,128)S(1)} %get-tuple-element.131) | copy-start | bytes 2359300
  74.8 134.2 %copy-start.108 = (f32[96]{0:T(128)}, f32[96]{0:T(128)S(1)}, u32[]{:S(2)}) copy-start(f32[96]{0:T(128)S(1)} %add_rsqrt_fusion.5) | copy-start | bytes 1156
  75.8 96.8 %reduce-scatter.25.cloned.1.call-start = ((), (), s32[]{:S(2)}) async-start(), calls=%async_computation.24 | async-start | bytes 1966080 | tf_op jit(solution)/shard_map/reduce_scatter | solution.py:476
  112.0 12.6 %slice-start.8 = ((s8[5767168]{0:T(1024)(128)(4,1)}), s8[4194304]{0:T(1024)(128)(4,1)S(1)}, s32[]{:S(2)}) async-start(s8[5767168]{0:T(1024)(128)(4,1)} %bitcast.195), calls=%async_computation.49 | async-start | bytes 8388608
  117.9 13.7 %slice-start = ((s8[5767168]{0:T(1024)(128)(4,1)}), s8[4194304]{0:T(1024)(128)(4,1)S(1)}, s32[]{:S(2)}) async-start(s8[5767168]{0:T(1024)(128)(4,1)} %bitcast.187), calls=%async_computation.41 | async-start | bytes 8388608
  117.9 16.4 %slice-start.4 = ((s8[5767168]{0:T(1024)(128)(4,1)}), s8[4194304]{0:T(1024)(128)(4,1)S(1)}, s32[]{:S(2)}) async-start(s8[5767168]{0:T(1024)(128)(4,1)} %bitcast.191), calls=%async_computation.45 | async-start | bytes 8388608
  138.3 70.8 %reduce-scatter.19.cloned.1.call-start = ((), (), s32[]{:S(2)}) async-start(), calls=%async_computation.18 | async-start | bytes 1966080 | tf_op jit(solution)/shard_map/reduce_scatter | solution.py:476
  145.1 102.8 %all-gather.17.cloned.1.call-start = ((), (), s32[]{:S(2)}) async-start(), calls=%async_computation.25 | async-start | bytes 1966080 | tf_op jit(solution)/shard_map/all_gather | solution.py:482
  174.4 39.6 %copy-start.113 = (f32[96]{0:T(128)}, f32[96]{0:T(128)S(1)}, u32[]{:S(2)}) copy-start(f32[96]{0:T(128)S(1)} %broadcast_multiply_fusion.3) | copy-start | bytes 1156
  211.7 72.6 %reduce-scatter.21.cloned.1.call-start = ((), (), s32[]{:S(2)}) async-start(), calls=%async_computation.20 | async-start | bytes 1966080 | tf_op jit(solution)/shard_map/reduce_scatter | solution.py:476
  238.4 82.4 %reduce-scatter.27.cloned.1.call-start = ((), (), s32[]{:S(2)}) async-start(), calls=%async_computation.26 | async-start | bytes 1966080 | tf_op jit(solution)/shard_map/reduce_scatter | solution.py:476
  250.5 14.5 %copy-start.98 = (bf16[2048,4]{0,1:T(4,128)(2,1)S(1)}, bf16[2048,4]{0,1:T(4,128)(2,1)}, u32[]{:S(2)}) copy-start(bf16[2048,4]{0,1:T(4,128)(2,1)} %param.27) | copy-start | bytes 49156
  274.9 45.9 %copy-start.95 = (f32[2048]{0:T(1024)S(1)}, f32[2048]{0:T(1024)}, u32[]{:S(2)}) copy-start(f32[2048]{0:T(1024)} %param.22) | copy-start | bytes 24580
  274.9 48.0 %copy-start.109 = (f32[96]{0:T(128)S(1)}, f32[96]{0:T(128)}, u32[]{:S(2)}) copy-start(f32[96]{0:T(128)} %copy-done.108) | copy-start | bytes 1156
  274.9 48.0 %copy-start.114 = (f32[96]{0:T(128)S(1)}, f32[96]{0:T(128)}, u32[]{:S(2)}) copy-start(f32[96]{0:T(128)} %copy-done.113) | copy-start | bytes 1156
  274.9 87.6 %all-gather.13.cloned.1.call-start = ((), (), s32[]{:S(2)}) async-start(), calls=%async_computation.21 | async-start | bytes 1966080 | tf_op jit(solution)/shard_map/all_gather | solution.py:482
  287.2 172.3 %copy-start.106 = (f32[96]{0:T(128)}, f32[96]{0:T(128)S(1)}, u32[]{:S(2)}) copy-start(f32[96]{0:T(128)S(1)} %add_rsqrt_fusion.4) | copy-start | bytes 1156
  326.4 96.7 %reduce-scatter.29.cloned.1.call-start = ((), (), s32[]{:S(2)}) async-start(), calls=%async_computation.28 | async-start | bytes 1966080 | tf_op jit(solution)/shard_map/reduce_scatter | solution.py:476
  362.6 12.6 %slice-start.10 = ((s8[5767168]{0:T(1024)(128)(4,1)}), s8[4194304]{0:T(1024)(128)(4,1)S(1)}, s32[]{:S(2)}) async-start(s8[5767168]{0:T(1024)(128)(4,1)} %bitcast.197), calls=%async_computation.51 | async-start | bytes 8388608
  368.5 13.8 %slice-start.2 = ((s8[5767168]{0:T(1024)(128)(4,1)}), s8[4194304]{0:T(1024)(128)(4,1)S(1)}, s32[]{:S(2)}) async-start(s8[5767168]{0:T(1024)(128)(4,1)} %bitcast.189), calls=%async_computation.43 | async-start | bytes 8388608
  368.5 16.4 %slice-start.6 = ((s8[5767168]{0:T(1024)(128)(4,1)}), s8[4194304]{0:T(1024)(128)(4,1)S(1)}, s32[]{:S(2)}) async-start(s8[5767168]{0:T(1024)(128)(4,1)} %bitcast.193), calls=%async_computation.47 | async-start | bytes 8388608
  388.7 70.8 %reduce-scatter.23.cloned.1.call-start = ((), (), s32[]{:S(2)}) async-start(), calls=%async_computation.22 | async-start | bytes 1966080 | tf_op jit(solution)/shard_map/reduce_scatter | solution.py:476
  395.6 103.0 %all-gather.21.cloned.1.call-start = ((), (), s32[]{:S(2)}) async-start(), calls=%async_computation.29 | async-start | bytes 1966080 | tf_op jit(solution)/shard_map/all_gather | solution.py:482
  425.2 76.0 %copy-start.111 = (f32[96]{0:T(128)}, f32[96]{0:T(128)S(1)}, u32[]{:S(2)}) copy-start(f32[96]{0:T(128)S(1)} %broadcast_multiply_fusion.1) | copy-start | bytes 1156
  462.4 127.6 %reduce-scatter.31.cloned.1.call-start = ((), (), s32[]{:S(2)}) async-start(), calls=%async_computation.30 | async-start | bytes 1966080 | tf_op jit(solution)/shard_map/reduce_scatter | solution.py:476
  501.8 14.4 %copy-start.99 = (bf16[2048,4]{0,1:T(4,128)(2,1)S(1)}, bf16[2048,4]{0,1:T(4,128)(2,1)}, u32[]{:S(2)}) copy-start(bf16[2048,4]{0,1:T(4,128)(2,1)} %param.27) | copy-start | bytes 49156
  526.0 93.6 %all-gather.11.cloned.1.call-start = ((), (), s32[]{:S(2)}) async-start(), calls=%async_computation.19 | async-start | bytes 1966080 | tf_op jit(solution)/shard_map/all_gather | solution.py:482
  526.7 109.8 %all-gather.15.cloned.1.call-start = ((), (), s32[]{:S(2)}) async-start(), calls=%async_computation.23 | async-start | bytes 1966080 | tf_op jit(solution)/shard_map/all_gather | solution.py:482
  527.3 163.4 %all-reduce.4.cloned.1.call-start = ((), (), s32[]{:S(2)}) async-start(), calls=%async_computation.36 | async-start | bytes 131072 | tf_op jit(solution)/shard_map/psum | solution.py:577
  531.1 203.7 %reduce-scatter.41.cloned.1.call-start = ((), (), s32[]{:S(2)}) async-start(), calls=%async_computation.37 | async-start | bytes 2359296 | tf_op jit(solution)/shard_map/reduce_scatter | solution.py:537
  536.3 260.9 %reduce-scatter.47.cloned.1.call-start = ((), (), s32[]{:S(2)}) async-start(), calls=%async_computation.40 | async-start | bytes 6488064 | tf_op jit(solution)/shard_map/reduce_scatter | solution.py:537
  545.4 314.6 %reduce-scatter.45.cloned.1.call-start = ((), (), s32[]{:S(2)}) async-start(), calls=%async_computation.39 | async-start | bytes 6488064 | tf_op jit(solution)/shard_map/reduce_scatter | solution.py:537
  557.1 365.3 %reduce-scatter.43.cloned.1.call-start = ((), (), s32[]{:S(2)}) async-start(), calls=%async_computation.38 | async-start | bytes 6488064 | tf_op jit(solution)/shard_map/reduce_scatter | solution.py:537
  567.0 400.2 %reduce-scatter.39.cloned.1.call-start = ((), (), s32[]{:S(2)}) async-start(), calls=%async_computation.35 | async-start | bytes 2359296 | tf_op jit(solution)/shard_map/reduce_scatter | solution.py:537
  573.4 438.4 %reduce-scatter.37.cloned.1.call-start = ((), (), s32[]{:S(2)}) async-start(), calls=%async_computation.34 | async-start | bytes 2359296 | tf_op jit(solution)/shard_map/reduce_scatter | solution.py:537
  578.8 477.9 %reduce-scatter.35.cloned.1.call-start = ((), (), s32[]{:S(2)}) async-start(), calls=%async_computation.33 | async-start | bytes 2359296 | tf_op jit(solution)/shard_map/reduce_scatter | solution.py:537
  584.1 517.7 %reduce-scatter.33.cloned.1.call-start = ((), (), s32[]{:S(2)}) async-start(), calls=%async_computation.32 | async-start | bytes 2359296 | tf_op jit(solution)/shard_map/reduce_scatter | solution.py:537
  589.3 556.3 %all-gather.19.cloned.1.call-start = ((), (), s32[]{:S(2)}) async-start(), calls=%async_computation.27 | async-start | bytes 1966080 | tf_op jit(solution)/shard_map/all_gather | solution.py:482
  589.8 589.2 %all-gather.23.cloned.1.call-start = ((), (), s32[]{:S(2)}) async-start(), calls=%async_computation.31 | async-start | bytes 1966080 | tf_op jit(solution)/shard_map/all_gather | solution.py:482
  591.6 27.9 %copy-start.51 = (f32[1,128]{1,0:T(1,128)S(1)}, f32[1,128]{1,0:T(1,128)}, u32[]{:S(2)}) copy-start(f32[1,128]{1,0:T(1,128)} %copy-done.50) | copy-start | bytes 1540
  591.6 27.9 %copy-start.57 = (f32[1,128]{1,0:T(1,128)S(1)}, f32[1,128]{1,0:T(1,128)}, u32[]{:S(2)}) copy-start(f32[1,128]{1,0:T(1,128)} %copy-done.56) | copy-start | bytes 1540
  736.9 65.6 %copy-start.104 = (f32[2048]{0:T(1024)S(1)}, f32[2048]{0:T(1024)}, u32[]{:S(2)}) copy-start(f32[2048]{0:T(1024)} %get-tuple-element.116) | copy-start | bytes 24580
  (113 other events, 328.1 us)
Sparse Core Ops, SparseCore 0:
  34.6 37.9 reduce-scatter.16
  75.9 36.0 all-gather.8
  138.4 34.1 reduce-scatter.24
  174.7 34.2 reduce-scatter.18
  211.8 36.0 all-gather.16
  250.0 34.1 reduce-scatter.20
  286.5 34.2 reduce-scatter.26
  326.5 36.0 all-gather.12
  388.8 34.1 reduce-scatter.28
  425.2 34.2 reduce-scatter.22
  462.5 36.0 all-gather.20
  526.1 34.1 reduce-scatter.30
  562.4 36.0 all-gather.10
  600.5 35.9 all-gather.14
  639.4 51.2 all-reduce.3
  694.2 40.6 reduce-scatter.40
  738.1 59.0 reduce-scatter.46
  800.9 58.9 reduce-scatter.44
  863.4 59.0 reduce-scatter.42
  925.9 41.2 reduce-scatter.38
  970.5 41.1 reduce-scatter.36
  1015.4 41.2 reduce-scatter.34
  1060.5 41.1 reduce-scatter.32
  1103.2 38.1 all-gather.18
  1143.1 35.9 all-gather.22

commit v2 on v1

--- a/solution.py
+++ b/solution.py
@@ -215,8 +215,7 @@
 def mixer_backward_body(
     grad_ref, query_ref, key_ref, value_ref, gate_ref, beta_ref, alpha_ref, taps_ref, dlog_ref,
     dbias_ref, gain_ref, mixed_ref, fresh_ref, inverse_ref, state_ref,
-    dquery_ref, dkey_ref, dvalue_ref, dgate_ref, dbeta_ref, dalpha_ref, dtaps_ref, ddlog_ref,
-    ddbias_ref, dgain_ref,
+    dproj_ref, dbeta_ref, dalpha_ref, dtaps_ref, ddlog_ref, ddbias_ref, dgain_ref,
 ):
     rows, width = query_ref.shape
     head_dim = gain_ref.shape[1]
@@ -232,6 +231,11 @@
     units = [(head, index) for head in range(head_count) for index in range(len(parts))]
     gain = gain_ref[...]
     root = 1.0 / math.sqrt(head_dim)
+    all_cols = dproj_ref.shape[1] // 4
+
+    def proj_cols(which, head):
+        start = which * all_cols + (first_head + head) * head_dim
+        return pl.ds(pl.multiple_of(start, head_dim), head_dim)
 
     @pl.when(step == 0)
     def _():
@@ -262,7 +266,7 @@
         normal = mixed * scale
         opened = gate * sig
         dgain_ref[...] += jnp.sum(grad * normal * opened, axis=0, keepdims=True)
-        dgate_ref[:, cols] = (
+        dproj_ref[:, proj_cols(3, head)] = (
             grad * normal * gain * (sig * (1.0 + gate * (1.0 - sig)))
         ).astype(LOW)
         grad_normal = grad * gain * opened
@@ -370,14 +374,14 @@
             dvalue,
         )
         projected = (query_ref, key_ref, value_ref)
-        for which, out_ref in enumerate((dquery_ref, dkey_ref, dvalue_ref)):
+        for which in range(3):
             conv = convs[head][which]
             sig = sigmoid(conv)
             grad_conv = act_grads[which] * sig * (1.0 + conv * (1.0 - sig))
             grad_in, grad_taps = conv_back(
                 grad_conv, projected[which][:, cols], taps_ref[which, :, cols]
             )
-            out_ref[:, cols] = grad_in.astype(LOW)
+            dproj_ref[:, proj_cols(which, head)] = grad_in.astype(LOW)
             for tap, entry in enumerate(grad_taps):
                 dtaps_ref[which, tap : tap + 1, cols] = entry
 
@@ -441,8 +445,10 @@
         in_specs=[wide] * 5
         + [narrow] * 2
         + [taps, small, small, gain, wide, wide, square, state],
-        out_specs=[wide] * 4 + [narrow] * 2 + [taps, small, small, gain],
-        out_shape=[jax.ShapeDtypeStruct((rows, width), LOW)] * 4
+        out_specs=[pl.BlockSpec((rows, 4 * width), lambda step: (0, 0))]
+        + [narrow] * 2
+        + [taps, small, small, gain],
+        out_shape=[jax.ShapeDtypeStruct((rows, 4 * width), LOW)]
         + [jax.ShapeDtypeStruct((rows, heads), FULL)] * 2
         + [
             jax.ShapeDtypeStruct(conv_taps.shape, FULL),
@@ -472,14 +478,93 @@
     return inverse * (scaled - normal * jnp.mean(scaled * normal, axis=-1, keepdims=True))
 
 
-def scatter_sum(partial_sum):
+def chain_scatter(partial_sum):
+    parts = lax.axis_size("head")
+    place = lax.axis_index("head")
+    own_len = partial_sum.shape[0] // parts
+
+    def share(index):
+        start = jnp.clip(index, 0, parts - 1) * own_len
+        return lax.dynamic_slice_in_dim(partial_sum, start, own_len, 0).astype(FULL)
+
+    right = left = 0.0
+    for step in range(1, parts):
+        right = lax.ppermute(
+            (share(parts - step + place) + right).astype(LOW),
+            "head",
+            [(source, source + 1) for source in range(step)],
+        ).astype(FULL)
+        left = lax.ppermute(
+            (share(step - parts + place) + left).astype(LOW),
+            "head",
+            [(source, source - 1) for source in range(parts - step, parts)],
+        ).astype(FULL)
+    return share(place) + right + left
+
+
+def chain_gather(own):
+    parts = lax.axis_size("head")
+    place = lax.axis_index("head")
+    own_len = own.shape[0]
+    right = left = own
+    before, after = [], []
+    for step in range(1, parts):
+        right = lax.ppermute(
+            right, "head", [(source, source + 1) for source in range(step - 1, parts - 1)]
+        )
+        left = lax.ppermute(
+            left, "head", [(source, source - 1) for source in range(1, parts - step + 1)]
+        )
+        before.append(right)
+        after.append(left)
+    joined = jnp.concatenate(before[::-1] + [own] + after, axis=0)
+    return lax.dynamic_slice_in_dim(
+        joined, (parts - 1 - place) * own_len, parts * own_len, 0
+    )
+
+
+def offload_scatter(partial_sum):
     return lax.psum_scatter(
         partial_sum.astype(LOW), "head", scatter_dimension=0, tiled=True
     ).astype(FULL)
 
 
-def gather(own):
+def offload_gather(own):
     return lax.all_gather(own, "head", axis=0, tiled=True)
+
+
+def butterfly(value, axis):
+    size = lax.axis_size(axis)
+    bit = 1
+    while bit < size:
+        value = value + lax.ppermute(value, axis, [(place, place ^ bit) for place in range(size)])
+        bit *= 2
+    return value
+
+
+def packed(entries):
+    flat = jnp.concatenate([entry.reshape(-1) for entry in entries])
+    pad = -flat.shape[0] % 1024
+    return jnp.pad(flat, (0, pad)).reshape(-1, 128)
+
+
+def unpacked(matrix, entries):
+    flat = matrix.reshape(-1)
+    outs, start = [], 0
+    for entry in entries:
+        outs.append(flat[start : start + entry.size].reshape(entry.shape))
+        start += entry.size
+    return outs
+
+
+def after(value, *others):
+    return lax.optimization_barrier((value,) + others)[0]
+
+
+scatter_out, gather_mid = chain_scatter, chain_gather
+scatter_down, gather_out = offload_scatter, offload_gather
+scatter_mid, gather_attn = chain_scatter, chain_gather
+scatter_in, gather_in = chain_scatter, chain_gather
 
 
 def per_device(
@@ -492,7 +577,9 @@
     own_len = seq_len // head_parts
     first_row = lax.axis_index("head") * own_len
     positions = lax.broadcasted_iota(jnp.int32, (seq_len, 1), 0)
-    in_weights = (w_query, w_key, w_value, w_gate, w_beta, w_alpha)
+    in_weights = (w_query, w_key, w_value, w_gate)
+    hidden_width = w_up.shape[1]
+    head_width = w_query.shape[1]
 
     def own_of(value):
         return lax.dynamic_slice_in_dim(value, first_row, own_len, 0)
@@ -500,83 +587,83 @@
     micros = []
     for micro in range(micro_count):
         rows = tokens[micro].astype(FULL)
+        grad_rows = cotangent[micro].astype(FULL)
         keep = (positions < lengths[micro, 0]).astype(FULL)
         normed = rms_scale(rows, norm_in).astype(LOW)
-        projections = tuple(mm(normed, weight) for weight in in_weights)
+        projections = tuple(mm(normed, weight) for weight in in_weights + (w_beta, w_alpha))
         gated, *kept = mixer_forward(projections, conv_taps, decay_log, decay_bias, norm_head)
-        out_part = scatter_sum(mm(gated, w_out))
+        out_part = scatter_out(mm(gated, w_out).astype(LOW))
         micros.append(
-            dict(rows=own_of(rows), keep=keep, keep_own=own_of(keep), normed=normed,
+            dict(rows=own_of(rows), grad_rows=own_of(grad_rows), keep_own=own_of(keep),
+                 down_grad=(keep * grad_rows).astype(LOW), normed=normed,
                  projections=projections, gated=gated, kept=kept, out_part=out_part)
         )
-    for micro in range(micro_count):
-        held = micros[micro]
+    for held in micros:
         middle = held["rows"] + held["keep_own"] * held["out_part"]
-        mid = gather(rms_scale(middle, norm_mid).astype(LOW))
-        grad_rows = cotangent[micro].astype(FULL)
-        down_grad = (held["keep"] * grad_rows).astype(LOW)
+        mid = gather_mid(rms_scale(middle, norm_mid).astype(LOW))
         gate_act = mm(mid, w_up_gate)
         up_act = mm(mid, w_up)
         sig = jax.nn.sigmoid(gate_act)
         hidden = (gate_act * sig * up_act).astype(LOW)
-        grad_hidden = mm(down_grad, w_down, NT)
+        grad_hidden = mm(held["down_grad"], w_down, NT)
         grad_gate = (grad_hidden * up_act * sig * (1.0 + gate_act * (1.0 - sig))).astype(LOW)
         grad_up = (grad_hidden * gate_act * sig).astype(LOW)
-        mid_part = scatter_sum(mm(grad_gate, w_up_gate, NT) + mm(grad_up, w_up, NT))
-        down_part = scatter_sum(mm(hidden, w_down))
+        mid_part = scatter_mid((mm(grad_gate, w_up_gate, NT) + mm(grad_up, w_up, NT)).astype(LOW))
+        down_part = scatter_down(mm(hidden, w_down).astype(LOW))
         out_own = (middle + held["keep_own"] * down_part).astype(LOW)
         held.update(
-            middle=middle, mid=mid, down_grad=down_grad, hidden=hidden, grad_gate=grad_gate,
-            grad_up=grad_up, mid_part=mid_part, grad_rows=own_of(grad_rows), out=gather(out_own),
-        )
-
-    def both(name):
-        return jnp.concatenate([held[name] for held in micros], axis=0)
+            middle=middle, mid=mid, hidden=hidden, grad_gate=grad_gate, grad_up=grad_up,
+            mid_part=mid_part, out=gather_out(out_own),
+        )
+
+    def both(*names):
+        return jnp.concatenate(
+            [jnp.concatenate([held[name] for name in names], axis=1) for held in micros], axis=0
+        )
 
     def shared(left, right):
         return lax.psum_scatter(
             mm(left, right, TN).astype(LOW), "batch", scatter_dimension=0, tiled=True
         ).astype(FULL)
 
-    mid_both, down_both = both("mid"), both("down_grad")
-    share_up_gate = shared(mid_both, both("grad_gate"))
-    share_up = shared(mid_both, both("grad_up"))
-    share_down = shared(down_both, both("hidden")).T
+    share_ups = shared(both("mid"), both("grad_gate", "grad_up"))
+    share_down = shared(both("down_grad"), both("hidden")).T
     gain_in = jnp.zeros((model_dim,), FULL)
     gain_mid = jnp.zeros((model_dim,), FULL)
     small = None
-    for micro in range(micro_count):
-        held = micros[micro]
+    for held in micros:
         middle = held["middle"]
         gain_mid = gain_mid + jnp.sum(rms_scale(middle, 1.0) * held["mid_part"], axis=0)
         grad_middle = held["grad_rows"] + rms_back(held["mid_part"], middle, norm_mid)
-        attn = gather((held["keep_own"] * grad_middle).astype(LOW))
-        *grads, grad_taps, grad_dlog, grad_dbias, grad_gain = mixer_backward(
+        attn = gather_attn((held["keep_own"] * grad_middle).astype(LOW))
+        grads, grad_beta, grad_alpha, grad_taps, grad_dlog, grad_dbias, grad_gain = mixer_backward(
             mm(attn, w_out, NT), held["projections"], conv_taps, decay_log, decay_bias,
             norm_head, held["kept"],
         )
-        grads = [entry.astype(LOW) for entry in grads]
-        in_part = mm(grads[0], in_weights[0], NT)
-        for index in range(1, len(in_weights)):
-            in_part = in_part + mm(grads[index], in_weights[index], NT)
-        in_part = scatter_sum(in_part)
+        narrow = (grad_beta.astype(LOW), grad_alpha.astype(LOW))
+        in_part = mm(narrow[0], w_beta, NT) + mm(narrow[1], w_alpha, NT)
+        for index, weight in enumerate(in_weights):
+            in_part = in_part + mm(
+                grads[:, index * head_width : (index + 1) * head_width], weight, NT
+            )
+        in_part = scatter_in(in_part.astype(LOW))
         gain_in = gain_in + jnp.sum(rms_scale(held["rows"], 1.0) * in_part, axis=0)
         grad_own = (grad_middle + rms_back(in_part, held["rows"], norm_in)).astype(LOW)
         entries = (grad_taps, grad_dlog, grad_dbias, grad_gain)
         small = entries if small is None else tuple(a + b for a, b in zip(small, entries))
-        held.update(attn=attn, grads=grads, grad_tokens=gather(grad_own))
+        held.update(attn=attn, grads=grads, beta=narrow[0], alpha=narrow[1],
+                    grad_tokens=gather_in(grad_own))
+    share_out = shared(both("attn"), both("gated")).T
     normed_both = both("normed")
-    grads_both = [
-        jnp.concatenate([held["grads"][index] for held in micros], axis=0) for index in range(6)
-    ]
-    share_in = [shared(normed_both, grads_both[index]) for index in range(4)]
-    share_out = shared(both("attn"), both("gated")).T
-    tiny = mm(jnp.concatenate(grads_both[4:], axis=1), normed_both, TN)
+    share_in = shared(normed_both, both("grads"))
+    tiny = mm(both("beta", "alpha"), normed_both, TN)
     grad_taps, grad_dlog, grad_dbias, grad_gain = small
-    gains = lax.psum((gain_in, grad_gain[0], gain_mid), ("batch", "head"))
-    tiny, grad_taps, grad_dlog, grad_dbias = lax.psum(
-        (tiny, grad_taps, grad_dlog[0], grad_dbias[0]), "batch"
-    )
+    entries = (tiny, grad_taps, grad_dlog[0], grad_dbias[0])
+    tiny, grad_taps, grad_dlog, grad_dbias = unpacked(
+        butterfly(packed(entries), "batch"), entries
+    )
+    entries = (gain_in, grad_gain[0], gain_mid)
+    gains = unpacked(butterfly(butterfly(packed(entries), "batch"), "head"), entries)
     width = model_dim // batch_parts
     tiny = lax.dynamic_slice_in_dim(tiny, lax.axis_index("batch") * width, width, 1).T
     count = w_beta.shape[1]
@@ -584,10 +671,10 @@
         jnp.stack([held["out"] for held in micros]),
         jnp.stack([held["grad_tokens"] for held in micros]),
         gains[0],
-        share_in[0], share_in[1], share_in[2], share_in[3],
+        *(share_in[:, index * head_width : (index + 1) * head_width] for index in range(4)),
         tiny[:, :count], tiny[:, count:],
         grad_taps, grad_dlog, grad_dbias, gains[1],
-        share_out, gains[2], share_up_gate, share_up, share_down,
+        share_out, gains[2], share_ups[:, :hidden_width], share_ups[:, hidden_width:], share_down,
     )
 
 

time: 1200 us -> 751 us (0.63)
  waiting for transfers between devices: 798 us -> 244 us
  starting transfers between devices: 2.92 us -> 169 us
  blocking collectives: 67 us -> 0 us
  matrix products: 157 us -> 118 us
  local copies, waits for them, and re-layouts: 31.4 us -> 68.4 us
    reduce_scatter x8 -> x4, waiting for transfers between devices: 392 us -> 23.2 us  [shared(): lax.psum_scatter(mm(left, right, TN).astype(LOW), 'batch', scatter_dimens...]
    ppermute x0 -> x80, waiting for transfers between devices: none -> 220 us  [the longest x18 73.6 us: chain_gather(): lax.ppermute(left, 'head', [(source, source - 1) for source in range(1, p...]
    reduce_scatter x8 -> x2, waiting for transfers between devices: 191 us -> 0.01 us  [offload_scatter(): lax.psum_scatter(partial_sum.astype(LOW), 'head', scatter_dimension=0, ti...]
    ppermute x0 -> x80, starting transfers between devices: none -> 169 us  [the longest x18 79.5 us: chain_scatter(): lax.ppermute((share(parts - step + place) + right).astype(LOW), 'head', [...]
    all_gather x8 -> x2, waiting for transfers between devices: 162 us -> 0.01 us  [offload_gather(): return lax.all_gather(own, 'head', axis=0, tiled=True)]
    psum x2 -> x0, blocking collectives: 67 us -> none  [the longest x1 42 us: per_device(): gains = lax.psum((gain_in, grad_gain[0], gain_mid), ('batch', 'head'))]
    psum x1 -> x0, waiting for transfers between devices: 50.4 us -> none  [per_device(): lax.psum((tiny, grad_taps, grad_dlog[0], grad_dbias[0]), 'batch')]
    dot_general x49 -> x45, matrix products: 157 us -> 118 us  [mm(): lax.dot_general(left.astype(LOW), right.astype(LOW), (dims, ((), ())), pr...]
  transfers between devices with their start and end apart: 25 -> 88, of which waited for: 22 -> 37; matrix products, arithmetic and copies ran while one was open for 12% -> 27% of each run, Pallas kernels for 2% -> 5%
where the time goes in v2:
time: 751 us; the launch traced here: 741 us
  waiting for transfers between devices  244 us (32%)
  starting transfers between devices  169 us (23%)
  matrix products  118 us (16%)
  other arithmetic  75.2 us (10%)
  local copies, waits for them, and re-layouts  68.4 us (9%)
  Pallas kernels  49 us (7%)
  between operations  17.4 us (2%)
    dot_general x45, matrix products, mm(): lax.dot_general(left.astype(LOW), right.astype(LOW), (dims, ((), ())), pr...  118 us
    ppermute x18, starting transfers between devices, chain_scatter(): lax.ppermute((share(parts - step + place) + right).astype(LOW), 'head', [...  79.5 us
    ppermute x18, waiting for transfers between devices, chain_gather(): lax.ppermute(left, 'head', [(source, source - 1) for source in range(1, p...  73.6 us
    ppermute x18, waiting for transfers between devices, chain_scatter(): lax.ppermute((share(parts - step + place) + right).astype(LOW), 'head', [...  60.9 us
    ppermute x18, waiting for transfers between devices, chain_scatter(): lax.ppermute((share(step - parts + place) + left).astype(LOW), 'head', [(...  53.9 us
    unnamed x319, local copies, waits for them, and re-layouts  49.6 us
    ppermute x18, starting transfers between devices, chain_gather(): lax.ppermute(right, 'head', [(source, source + 1) for source in range(ste...  36.2 us
    pallas_call x2, Pallas kernels, mixer_backward(): pl.pallas_call(mixer_backward_body, grid=(heads // group,), in_specs=[wid...  31 us
  transfers between devices with their start and end apart: 88, of which 37 were waited for; matrix products, arithmetic and copies ran while one was open for 27% of the time, Pallas kernels for 5%

profile of v2, /device:TPU:0, one launch (start us, length us, event | category | flops | bytes accessed | tf_op | source)
XLA Modules:
  0.0 740.8 jit_solution(12668309245380466629)
XLA Ops:
  19.9 9.0 %mixer_forward.2 = (bf16[384,512]{1,0:T(8,128)(2,1)S(1)}, f32[384,512]{1,0:T(8,128)S(1)}, bf16[384,512]{1,0:T(8,128)(2,1)S(1)}, bf16[4,3,128,128]{3,2,1,0:T(8,128)(2,1)S(1)}, bf16[4,3,128,128]{3,2,1,0:T(8,128)(2,1)S(1)}) custom-call(f32[384,512]{1,0:T(8,128)S(1)} %fusion.80.query_ref, f32[384,512]{1,0:T(8,128)S(1)} %fusion.81.key_ref, ...), custom_call_target="tpu_custom_call" | custom-call | tf_op jit(solution)/shard_map/mixer_forward/pallas_call | solution.py:411
  37.1 5.7 collective-permute-start
  61.4 9.0 %mixer_forward.3 = (bf16[384,512]{1,0:T(8,128)(2,1)S(1)}, f32[384,512]{1,0:T(8,128)S(1)}, bf16[384,512]{1,0:T(8,128)(2,1)S(1)}, bf16[4,3,128,128]{3,2,1,0:T(8,128)(2,1)S(1)}, bf16[4,3,128,128]{3,2,1,0:T(8,128)(2,1)S(1)}) custom-call(f32[384,512]{1,0:T(8,128)S(1)} %copy-done.7, f32[384,512]{1,0:T(8,128)S(1)} %copy-done.9, f32[384,512]{1,0:T(8,128)S(1)} %copy-done.11, ...), custom_call_target="tpu_custom_call" | custom-call | tf_op jit(solution)/shard_map/mixer_forward/pallas_call | solution.py:411
  88.0 4.5 slice_convert_fusion.3
  92.5 5.3 collective-permute-start.2
  104.1 4.9 collective-permute-done.5
  111.6 4.8 collective-permute-start.6
  123.1 5.6 slice_convert_fusion.1
  134.9 6.0 collective-permute-start.13
  143.9 7.0 collective-permute-done.11
  183.9 12.6 %collective-permute-done.25 = bf16[96,2048]{1,0:T(8,128)(2,1)S(1)} collective-permute-done((bf16[96,2048]{1,0:T(8,128)(2,1)S(1)}, bf16[96,2048]{1,0:T(8,128)(2,1)S(1)}, u32[]{:S(2)}, u32[]{:S(2)}) %collective-permute-start.25) | collective-permute-done | bytes 393248 | tf_op jit(solution)/shard_map/ppermute | solution.py:492
  199.9 15.5 %collective-permute-start.26 = (bf16[96,2048]{1,0:T(8,128)(2,1)S(1)}, bf16[96,2048]{1,0:T(8,128)(2,1)S(1)}, u32[]{:S(2)}, u32[]{:S(2)}) collective-permute-start(bf16[96,2048]{1,0:T(8,128)(2,1)S(1)} %get-tuple-element.140), channel_id=1, source_target_pairs={{0,1},{1,2},{2,3},{4,5},{5,6},{6,7},{8,9},{9,10},{10,11},{12,13},{... | collective-permute-start | bytes 1179656 | tf_op jit(solution)/shard_map/ppermute | solution.py:492
  216.9 6.3 collective-permute-done.17
  226.1 5.8 collective-permute-done.29
  236.5 7.2 collective-permute-start.18
  249.6 4.3 collective-permute-done.21
  255.9 5.4 fusion.99
  267.0 7.9 %collective-permute-done.23 = bf16[96,2048]{1,0:T(8,128)(2,1)S(1)} collective-permute-done((bf16[96,2048]{1,0:T(8,128)(2,1)S(1)}, bf16[96,2048]{1,0:T(8,128)(2,1)S(1)}, u32[]{:S(2)}, u32[]{:S(2)}) %collective-permute-start.23) | collective-permute-done | bytes 393248 | tf_op jit(solution)/shard_map/ppermute | solution.py:515
  290.5 6.6 add_convert_fusion.1
  302.7 13.8 %collective-permute-done.48 = bf16[96,2048]{1,0:T(8,128)(2,1)S(1)} collective-permute-done((bf16[96,2048]{1,0:T(8,128)(2,1)S(1)}, bf16[96,2048]{1,0:T(8,128)(2,1)S(1)}, u32[]{:S(2)}, u32[]{:S(2)}) %collective-permute-start.48) | collective-permute-done | bytes 393248 | tf_op jit(solution)/shard_map/ppermute | solution.py:492
  316.6 4.4 collective-permute-start.49
  321.0 12.0 %collective-permute-done.30 = bf16[96,2048]{1,0:T(8,128)(2,1)} collective-permute-done((bf16[96,2048]{1,0:T(8,128)(2,1)S(1)}, bf16[96,2048]{1,0:T(8,128)(2,1)}, u32[]{:S(2)}, u32[]{:S(2)}) %collective-permute-start.30) | collective-permute-done | bytes 393248 | tf_op jit(solution)/shard_map/ppermute | solution.py:512
  335.7 6.6 collective-permute-done.49
  350.7 5.3 collective-permute-start.50
  361.1 8.9 %collective-permute-done.50 = bf16[96,2048]{1,0:T(8,128)(2,1)S(1)} collective-permute-done((bf16[96,2048]{1,0:T(8,128)(2,1)}, bf16[96,2048]{1,0:T(8,128)(2,1)S(1)}, u32[]{:S(2)}, u32[]{:S(2)}) %collective-permute-start.50) | collective-permute-done | bytes 393248 | tf_op jit(solution)/shard_map/ppermute | solution.py:492
  370.0 20.4 %collective-permute-done.53 = bf16[96,2048]{1,0:T(8,128)(2,1)S(1)} collective-permute-done((bf16[96,2048]{1,0:T(8,128)(2,1)S(1)}, bf16[96,2048]{1,0:T(8,128)(2,1)S(1)}, u32[]{:S(2)}, u32[]{:S(2)}) %collective-permute-start.53) | collective-permute-done | bytes 393248 | tf_op jit(solution)/shard_map/ppermute | solution.py:497
  416.7 5.4 collective-permute-done.58
  427.7 13.1 %collective-permute-done.59 = bf16[96,2048]{1,0:T(8,128)(2,1)S(1)} collective-permute-done((bf16[96,2048]{1,0:T(8,128)(2,1)}, bf16[96,2048]{1,0:T(8,128)(2,1)S(1)}, u32[]{:S(2)}, u32[]{:S(2)}) %collective-permute-start.59) | collective-permute-done | bytes 393248 | tf_op jit(solution)/shard_map/ppermute | solution.py:515
  445.4 9.0 %convolution_convert_fusion.1 = bf16[2048,1408]{1,0:T(8,128)(2,1)} fusion(bf16[384,2048]{1,0:T(8,128)(2,1)} %get-tuple-element.132, bf16[384,2048]{1,0:T(8,128)(2,1)} %copy-done.84, bf16[384,1408]{1,0:T(8,128)(2,1)} %copy-done.125, bf16[384,1408]{1,0:T(8,128)(2,1)} %copy-done.124), kind=kOutput, calls=%fused_computation.1 | convolution fusion | flops 4442685440 | bytes 11075584 | tf_op jit(solution)/shard_map/dot_general | solution.py:17
  457.2 15.4 %mixer_backward.2 = (bf16[384,2048]{1,0:T(8,128)(2,1)}, f32[384,4]{1,0:T(8,128)S(1)}, f32[384,4]{1,0:T(8,128)S(1)}, f32[3,4,512]{2,1,0:T(4,128)S(1)}, f32[1,4]{1...) custom-call(f32[384,512]{1,0:T(8,128)S(1)} %fusion.96.grad_ref, f32[384,512]{1,0:T(8,128)S(1)} %fusion.80.query_ref, ...), custom_call_target="tpu_custom_call" | custom-call | tf_op jit(solution)/shard_map/mixer_backward/pallas_call | solution.py:442
  475.0 15.6 %mixer_backward.3 = (bf16[384,2048]{1,0:T(8,128)(2,1)}, f32[384,4]{1,0:T(8,128)S(1)}, f32[384,4]{1,0:T(8,128)S(1)}, f32[3,4,512]{2,1,0:T(4,128)S(1)}, f32[1,4]{1...) custom-call(f32[384,512]{1,0:T(8,128)S(1)} %fusion.101.grad_ref, f32[384,512]{1,0:T(8,128)S(1)} %copy-done.8, ...), custom_call_target="tpu_custom_call" | custom-call | tf_op jit(solution)/shard_map/mixer_backward/pallas_call | solution.py:442
  490.6 10.5 %convolution_convert_fusion.2 = bf16[2048,2048]{1,0:T(8,128)(2,1)} fusion(bf16[384,2048]{1,0:T(8,128)(2,1)} %get-tuple-element.57, bf16[384,2048]{1,0:T(8,128)(2,1)S(1)} %copy-done.100, bf16[384,2048]{1,0:T(8,128)(2,1)S(1)} %copy-done.82, bf16[384,2048]{1,0:T(8,128)(2,1)S(1)} %copy-done.79), kind=kOutput, calls=%fused_computation.2 | convolution fusion | flops 6459228160 | bytes 14680064 | tf_op jit(solution)/shard_map/dot_general | solution.py:17
  514.6 14.6 %convolution_convert_fusion = bf16[2048,2816]{1,0:T(8,128)(2,1)} fusion(bf16[384,1408]{1,0:T(8,128)(2,1)} %get-tuple-element.123, bf16[384,1408]{1,0:T(8,128)(2,1)} %copy-done.123, bf16[384,1408]{1,0:T(8,128)(2,1)S(1)} %copy-done.121, bf16[384,1408]{1,0:T(8,128)(2,1)} %copy-done.122, bf16[384,2048]{1,0:T(8,128)(2,1)S(1)} %copy-done.89, ...), kind=kOutput, calls=%fused_computation | convolution fusion | flops 8887730176 | bytes 19005440 | tf_op jit(solution)/shard_map/dot_general | solution.py:17
  532.5 5.2 collective-permute-done.37
  551.3 11.1 %collective-permute-done.41 = bf16[96,2048]{1,0:T(8,128)(2,1)} collective-permute-done((bf16[96,2048]{1,0:T(8,128)(2,1)}, bf16[96,2048]{1,0:T(8,128)(2,1)}, u32[]{:S(2)}, u32[]{:S(2)}) %collective-permute-start.41) | collective-permute-done | bytes 393248 | tf_op jit(solution)/shard_map/ppermute | solution.py:497
  573.8 4.3 collective-permute-start.60
  584.2 5.1 collective-permute-start.61
  599.3 5.0 collective-permute-start.62
  607.6 6.5 collective-permute-done.79
  614.2 5.3 collective-permute-done.65
  624.0 4.7 collective-permute-start.42
  636.0 4.6 collective-permute-start.66
  647.2 5.7 collective-permute-done.75
  654.6 4.8 pad_maximum_fusion
  664.6 9.0 %collective-permute-done.46 = bf16[96,2048]{1,0:T(8,128)(2,1)S(1)} collective-permute-done((bf16[96,2048]{1,0:T(8,128)(2,1)}, bf16[96,2048]{1,0:T(8,128)(2,1)S(1)}, u32[]{:S(2)}, u32[]{:S(2)}) %collective-permute-start.46) | collective-permute-done | bytes 393248 | tf_op jit(solution)/shard_map/ppermute | solution.py:515
  675.6 6.4 collective-permute-done.70
  690.5 4.6 collective-permute-done.71
  707.2 23.2 %reduce-scatter.15.cloned.1.call-done = bf16[256,2816]{1,0:T(8,128)(2,1)} async-done(((bf16[2048,2816]{1,0:T(8,128)(2,1)}), bf16[256,2816]{1,0:T(8,128)(2,1)}) %reduce-scatter.15.cloned.1.call-update) | async-done | bytes 1441808 | tf_op jit(solution)/shard_map/reduce_scatter | solution.py:625
  (616 shorter events, 329.3 us)
Async XLA Ops:
  7.2 225.5 %reduce-scatter.7.cloned.1.call-start = ((), (), s32[]{:S(2)}) async-start(), calls=%async_computation.6 | async-start | bytes 1966080 | tf_op jit(solution)/shard_map/reduce_scatter | solution.py:527
  37.1 34.7 %collective-permute-start = (bf16[96,2048]{1,0:T(8,128)(2,1)}, bf16[96,2048]{1,0:T(8,128)(2,1)}, u32[]{:S(2)}, u32[]{:S(2)}) collective-permute-start(bf16[96,2048]{1,0:T(8,128)(2,1)} %get-tuple-element.154), channel_id=1, source_target_pairs={{0,1},{4,5},{8,9},{12,13},{16,17},{20,21},{24,25},{28,29}} | collective-permute-start | bytes 1179656 | tf_op jit(solution)/shard_map/ppermute | solution.py:492
  42.8 41.3 %collective-permute-start.3 = (bf16[96,2048]{1,0:T(8,128)(2,1)}, bf16[96,2048]{1,0:T(8,128)(2,1)}, u32[]{:S(2)}, u32[]{:S(2)}) collective-permute-start(bf16[96,2048]{1,0:T(8,128)(2,1)} %get-tuple-element.155), channel_id=1, source_target_pairs={{3,2},{7,6},{11,10},{15,14},{19,18},{23,22},{27,26},{31,30}} | collective-permute-start | bytes 1179656 | tf_op jit(solution)/shard_map/ppermute | solution.py:497
  77.4 55.6 %collective-permute-start.12 = (bf16[96,2048]{1,0:T(8,128)(2,1)}, bf16[96,2048]{1,0:T(8,128)(2,1)}, u32[]{:S(2)}, u32[]{:S(2)}) collective-permute-start(bf16[96,2048]{1,0:T(8,128)(2,1)} %get-tuple-element.158), channel_id=1, source_target_pairs={{0,1},{4,5},{8,9},{12,13},{16,17},{20,21},{24,25},{28,29}} | collective-permute-start | bytes 1179656 | tf_op jit(solution)/shard_map/ppermute | solution.py:492
  80.1 98.8 %collective-permute-start.15 = (bf16[96,2048]{1,0:T(8,128)(2,1)}, bf16[96,2048]{1,0:T(8,128)(2,1)}, u32[]{:S(2)}, u32[]{:S(2)}) collective-permute-start(bf16[96,2048]{1,0:T(8,128)(2,1)} %get-tuple-element.159), channel_id=1, source_target_pairs={{3,2},{7,6},{11,10},{15,14},{19,18},{23,22},{27,26},{31,30}} | collective-permute-start | bytes 1179656 | tf_op jit(solution)/shard_map/ppermute | solution.py:497
  134.9 44.0 %collective-permute-start.13 = (bf16[96,2048]{1,0:T(8,128)(2,1)}, bf16[96,2048]{1,0:T(8,128)(2,1)}, u32[]{:S(2)}, u32[]{:S(2)}) collective-permute-start(bf16[96,2048]{1,0:T(8,128)(2,1)} %add_convert_fusion.26), channel_id=1, source_target_pairs={{0,1},{1,2},{4,5},{5,6},{8,9},{9,10},{12,13},{13,14},{16,17},{17,1... | collective-permute-start | bytes 1179656 | tf_op jit(solution)/shard_map/ppermute | solution.py:492
  167.9 16.0 %collective-permute-start.27 = (bf16[96,2048]{1,0:T(8,128)(2,1)}, bf16[96,2048]{1,0:T(8,128)(2,1)}, u32[]{:S(2)}, u32[]{:S(2)}) collective-permute-start(bf16[96,2048]{1,0:T(8,128)(2,1)} %get-tuple-element.143), channel_id=1, source_target_pairs={{3,2},{7,6},{11,10},{15,14},{19,18},{23,22},{27,26},{31,30}} | collective-permute-start | bytes 1179656 | tf_op jit(solution)/shard_map/ppermute | solution.py:497
  173.3 219.3 %reduce-scatter.9.cloned.1.call-start = ((), (), s32[]{:S(2)}) async-start(), calls=%async_computation.8 | async-start | bytes 1966080 | tf_op jit(solution)/shard_map/reduce_scatter | solution.py:527
  174.7 21.8 %collective-permute-start.25 = (bf16[96,2048]{1,0:T(8,128)(2,1)S(1)}, bf16[96,2048]{1,0:T(8,128)(2,1)S(1)}, u32[]{:S(2)}, u32[]{:S(2)}) collective-permute-start(bf16[96,2048]{1,0:T(8,128)(2,1)S(1)} %add_convert_fusion.21), channel_id=1, source_target_pairs={{0,1},{1,2},{4,5},{5,6},{8,9},{9,10},{12,13},{13,14},{16,17},{17,1... | collective-permute-start | bytes 1179656 | tf_op jit(solution)/shard_map/ppermute | solution.py:492
  180.5 17.9 %collective-permute-start.16 = (bf16[96,2048]{1,0:T(8,128)(2,1)S(1)}, bf16[96,2048]{1,0:T(8,128)(2,1)S(1)}, u32[]{:S(2)}, u32[]{:S(2)}) collective-permute-start(bf16[96,2048]{1,0:T(8,128)(2,1)S(1)} %get-tuple-element.157), channel_id=1, source_target_pairs={{2,1},{3,2},{6,5},{7,6},{10,9},{11,10},{14,13},{15,14},{18,17},{19... | collective-permute-start | bytes 1179656 | tf_op jit(solution)/shard_map/ppermute | solution.py:497
  181.2 35.6 %collective-permute-start.14 = (bf16[96,2048]{1,0:T(8,128)(2,1)S(1)}, bf16[96,2048]{1,0:T(8,128)(2,1)S(1)}, u32[]{:S(2)}, u32[]{:S(2)}) collective-permute-start(bf16[96,2048]{1,0:T(8,128)(2,1)S(1)} %get-tuple-element.156), channel_id=1, source_target_pairs={{0,1},{1,2},{2,3},{4,5},{5,6},{6,7},{8,9},{9,10},{10,11},{12,13},{... | collective-permute-start | bytes 1179656 | tf_op jit(solution)/shard_map/ppermute | solution.py:492
  197.7 17.8 %collective-permute-start.28 = (bf16[96,2048]{1,0:T(8,128)(2,1)S(1)}, bf16[96,2048]{1,0:T(8,128)(2,1)S(1)}, u32[]{:S(2)}, u32[]{:S(2)}) collective-permute-start(bf16[96,2048]{1,0:T(8,128)(2,1)S(1)} %get-tuple-element.141), channel_id=1, source_target_pairs={{2,1},{3,2},{6,5},{7,6},{10,9},{11,10},{14,13},{15,14},{18,17},{19... | collective-permute-start | bytes 1179656 | tf_op jit(solution)/shard_map/ppermute | solution.py:497
  198.5 24.7 %collective-permute-start.17 = (bf16[96,2048]{1,0:T(8,128)(2,1)S(1)}, bf16[96,2048]{1,0:T(8,128)(2,1)S(1)}, u32[]{:S(2)}, u32[]{:S(2)}) collective-permute-start(bf16[96,2048]{1,0:T(8,128)(2,1)S(1)} %add_convert_fusion.23), channel_id=1, source_target_pairs={{1,0},{2,1},{3,2},{5,4},{6,5},{7,6},{9,8},{10,9},{11,10},{13,12},{... | collective-permute-start | bytes 1179656 | tf_op jit(solution)/shard_map/ppermute | solution.py:497
  199.9 26.2 %collective-permute-start.26 = (bf16[96,2048]{1,0:T(8,128)(2,1)S(1)}, bf16[96,2048]{1,0:T(8,128)(2,1)S(1)}, u32[]{:S(2)}, u32[]{:S(2)}) collective-permute-start(bf16[96,2048]{1,0:T(8,128)(2,1)S(1)} %get-tuple-element.140), channel_id=1, source_target_pairs={{0,1},{1,2},{2,3},{4,5},{5,6},{6,7},{8,9},{9,10},{10,11},{12,13},{... | collective-permute-start | bytes 1179656 | tf_op jit(solution)/shard_map/ppermute | solution.py:492
  215.5 16.4 %collective-permute-start.29 = (bf16[96,2048]{1,0:T(8,128)(2,1)S(1)}, bf16[96,2048]{1,0:T(8,128)(2,1)S(1)}, u32[]{:S(2)}, u32[]{:S(2)}) collective-permute-start(bf16[96,2048]{1,0:T(8,128)(2,1)S(1)} %add_convert_fusion.18), channel_id=1, source_target_pairs={{1,0},{2,1},{3,2},{5,4},{6,5},{7,6},{9,8},{10,9},{11,10},{13,12},{... | collective-permute-start | bytes 1179656 | tf_op jit(solution)/shard_map/ppermute | solution.py:497
  290.5 364.1 %all-gather.3.cloned.1.call-start = ((), (), s32[]{:S(2)}) async-start(), calls=%async_computation.7 | async-start | bytes 1966080 | tf_op jit(solution)/shard_map/all_gather | solution.py:533
  297.2 19.3 %collective-permute-start.48 = (bf16[96,2048]{1,0:T(8,128)(2,1)S(1)}, bf16[96,2048]{1,0:T(8,128)(2,1)S(1)}, u32[]{:S(2)}, u32[]{:S(2)}) collective-permute-start(bf16[96,2048]{1,0:T(8,128)(2,1)S(1)} %get-tuple-element.150), channel_id=1, source_target_pairs={{0,1},{4,5},{8,9},{12,13},{16,17},{20,21},{24,25},{28,29}} | collective-permute-start | bytes 1179656 | tf_op jit(solution)/shard_map/ppermute | solution.py:492
  298.7 34.3 %collective-permute-start.30 = (bf16[96,2048]{1,0:T(8,128)(2,1)S(1)}, bf16[96,2048]{1,0:T(8,128)(2,1)}, u32[]{:S(2)}, u32[]{:S(2)}) collective-permute-start(bf16[96,2048]{1,0:T(8,128)(2,1)S(1)} %copy-done.74), channel_id=1, source_target_pairs={{0,1},{1,2},{2,3},{4,5},{5,6},{6,7},{8,9},{9,10},{10,11},{12,13},{... | collective-permute-start | bytes 1179656 | tf_op jit(solution)/shard_map/ppermute | solution.py:512
  300.7 33.7 %collective-permute-start.33 = (bf16[96,2048]{1,0:T(8,128)(2,1)S(1)}, bf16[96,2048]{1,0:T(8,128)(2,1)}, u32[]{:S(2)}, u32[]{:S(2)}) collective-permute-start(bf16[96,2048]{1,0:T(8,128)(2,1)S(1)} %copy-done.74), channel_id=1, source_target_pairs={{1,0},{2,1},{3,2},{5,4},{6,5},{7,6},{9,8},{10,9},{11,10},{13,12},{... | collective-permute-start | bytes 1179656 | tf_op jit(solution)/shard_map/ppermute | solution.py:515
  302.0 33.7 %collective-permute-start.51 = (bf16[96,2048]{1,0:T(8,128)(2,1)S(1)}, bf16[96,2048]{1,0:T(8,128)(2,1)S(1)}, u32[]{:S(2)}, u32[]{:S(2)}) collective-permute-start(bf16[96,2048]{1,0:T(8,128)(2,1)S(1)} %get-tuple-element.151), channel_id=1, source_target_pairs={{3,2},{7,6},{11,10},{15,14},{19,18},{23,22},{27,26},{31,30}} | collective-permute-start | bytes 1179656 | tf_op jit(solution)/shard_map/ppermute | solution.py:497
  316.6 25.7 %collective-permute-start.49 = (bf16[96,2048]{1,0:T(8,128)(2,1)S(1)}, bf16[96,2048]{1,0:T(8,128)(2,1)S(1)}, u32[]{:S(2)}, u32[]{:S(2)}) collective-permute-start(bf16[96,2048]{1,0:T(8,128)(2,1)S(1)} %add_convert_fusion.12), channel_id=1, source_target_pairs={{0,1},{1,2},{4,5},{5,6},{8,9},{9,10},{12,13},{13,14},{16,17},{17,1... | collective-permute-start | bytes 1179656 | tf_op jit(solution)/shard_map/ppermute | solution.py:492
  334.4 15.0 %collective-permute-start.34 = (bf16[96,2048]{1,0:T(8,128)(2,1)}, bf16[96,2048]{1,0:T(8,128)(2,1)}, u32[]{:S(2)}, u32[]{:S(2)}) collective-permute-start(bf16[96,2048]{1,0:T(8,128)(2,1)} %collective-permute-done.33), channel_id=1, source_target_pairs={{1,0},{2,1},{5,4},{6,5},{9,8},{10,9},{13,12},{14,13},{17,16},{18,1... | collective-permute-start | bytes 1179656 | tf_op jit(solution)/shard_map/ppermute | solution.py:515
  343.5 12.6 %collective-permute-start.52 = (bf16[96,2048]{1,0:T(8,128)(2,1)}, bf16[96,2048]{1,0:T(8,128)(2,1)}, u32[]{:S(2)}, u32[]{:S(2)}) collective-permute-start(bf16[96,2048]{1,0:T(8,128)(2,1)} %get-tuple-element.149), channel_id=1, source_target_pairs={{2,1},{3,2},{6,5},{7,6},{10,9},{11,10},{14,13},{15,14},{18,17},{19... | collective-permute-start | bytes 1179656 | tf_op jit(solution)/shard_map/ppermute | solution.py:497
  344.9 309.7 %all-gather.5.cloned.1.call-start = ((), (), s32[]{:S(2)}) async-start(), calls=%async_computation.9 | async-start | bytes 1966080 | tf_op jit(solution)/shard_map/all_gather | solution.py:533
  345.0 13.6 %collective-permute-start.32 = (bf16[96,2048]{1,0:T(8,128)(2,1)}, bf16[96,2048]{1,0:T(8,128)(2,1)S(1)}, u32[]{:S(2)}, u32[]{:S(2)}) collective-permute-start(bf16[96,2048]{1,0:T(8,128)(2,1)} %collective-permute-done.31), channel_id=1, source_target_pairs={{2,3},{6,7},{10,11},{14,15},{18,19},{22,23},{26,27},{30,31}} | collective-permute-start | bytes 1179656 | tf_op jit(solution)/shard_map/ppermute | solution.py:512
  349.4 63.8 %collective-permute-start.35 = (bf16[96,2048]{1,0:T(8,128)(2,1)}, bf16[96,2048]{1,0:T(8,128)(2,1)}, u32[]{:S(2)}, u32[]{:S(2)}) collective-permute-start(bf16[96,2048]{1,0:T(8,128)(2,1)} %collective-permute-done.34), channel_id=1, source_target_pairs={{1,0},{5,4},{9,8},{13,12},{17,16},{21,20},{25,24},{29,28}} | collective-permute-start | bytes 1179656 | tf_op jit(solution)/shard_map/ppermute | solution.py:515
  350.7 19.3 %collective-permute-start.50 = (bf16[96,2048]{1,0:T(8,128)(2,1)}, bf16[96,2048]{1,0:T(8,128)(2,1)S(1)}, u32[]{:S(2)}, u32[]{:S(2)}) collective-permute-start(bf16[96,2048]{1,0:T(8,128)(2,1)} %get-tuple-element.148), channel_id=1, source_target_pairs={{0,1},{1,2},{2,3},{4,5},{5,6},{6,7},{8,9},{9,10},{10,11},{12,13},{... | collective-permute-start | bytes 1179656 | tf_op jit(solution)/shard_map/ppermute | solution.py:492
  357.3 33.1 %collective-permute-start.53 = (bf16[96,2048]{1,0:T(8,128)(2,1)S(1)}, bf16[96,2048]{1,0:T(8,128)(2,1)S(1)}, u32[]{:S(2)}, u32[]{:S(2)}) collective-permute-start(bf16[96,2048]{1,0:T(8,128)(2,1)S(1)} %add_convert_fusion.9), channel_id=1, source_target_pairs={{1,0},{2,1},{3,2},{5,4},{6,5},{7,6},{9,8},{10,9},{11,10},{13,12},{... | collective-permute-start | bytes 1179656 | tf_op jit(solution)/shard_map/ppermute | solution.py:497
  415.0 282.2 %reduce-scatter.13.cloned.1.call-start = ((), (), s32[]{:S(2)}) async-start(), calls=%async_computation.11 | async-start | bytes 2359296 | tf_op jit(solution)/shard_map/reduce_scatter | solution.py:625
  422.2 18.7 %collective-permute-start.59 = (bf16[96,2048]{1,0:T(8,128)(2,1)}, bf16[96,2048]{1,0:T(8,128)(2,1)S(1)}, u32[]{:S(2)}, u32[]{:S(2)}) collective-permute-start(bf16[96,2048]{1,0:T(8,128)(2,1)} %collective-permute-done.58), channel_id=1, source_target_pairs={{1,0},{5,4},{9,8},{13,12},{17,16},{21,20},{25,24},{29,28}} | collective-permute-start | bytes 1179656 | tf_op jit(solution)/shard_map/ppermute | solution.py:515
  445.4 253.9 %reduce-scatter.17.cloned.1.call-start = ((), (), s32[]{:S(2)}) async-start(), calls=%async_computation.13 | async-start | bytes 6488064 | tf_op jit(solution)/shard_map/reduce_scatter | solution.py:625
  454.5 250.1 %reduce-scatter.11.cloned.1.call-start = ((), (), s32[]{:S(2)}) async-start(), calls=%async_computation.10 | async-start | bytes 9437184 | tf_op jit(solution)/shard_map/reduce_scatter | solution.py:625
  501.2 229.2 %reduce-scatter.15.cloned.1.call-start = ((), (), s32[]{:S(2)}) async-start(), calls=%async_computation.12 | async-start | bytes 12976128 | tf_op jit(solution)/shard_map/reduce_scatter | solution.py:625
  512.6 17.4 %collective-permute-start.36 = (bf16[96,2048]{1,0:T(8,128)(2,1)}, bf16[96,2048]{1,0:T(8,128)(2,1)}, u32[]{:S(2)}, u32[]{:S(2)}) collective-permute-start(bf16[96,2048]{1,0:T(8,128)(2,1)} %get-tuple-element.138), channel_id=1, source_target_pairs={{0,1},{4,5},{8,9},{12,13},{16,17},{20,21},{24,25},{28,29}} | collective-permute-start | bytes 1179656 | tf_op jit(solution)/shard_map/ppermute | solution.py:492
  547.8 14.7 %collective-permute-start.41 = (bf16[96,2048]{1,0:T(8,128)(2,1)}, bf16[96,2048]{1,0:T(8,128)(2,1)}, u32[]{:S(2)}, u32[]{:S(2)}) collective-permute-start(bf16[96,2048]{1,0:T(8,128)(2,1)} %add_convert_fusion.14), channel_id=1, source_target_pairs={{1,0},{2,1},{3,2},{5,4},{6,5},{7,6},{9,8},{10,9},{11,10},{13,12},{... | collective-permute-start | bytes 1179656 | tf_op jit(solution)/shard_map/ppermute | solution.py:497
  599.3 14.9 %collective-permute-start.62 = (bf16[96,2048]{1,0:T(8,128)(2,1)}, bf16[96,2048]{1,0:T(8,128)(2,1)S(1)}, u32[]{:S(2)}, u32[]{:S(2)}) collective-permute-start(bf16[96,2048]{1,0:T(8,128)(2,1)} %get-tuple-element.144), channel_id=1, source_target_pairs={{0,1},{1,2},{2,3},{4,5},{5,6},{6,7},{8,9},{9,10},{10,11},{12,13},{... | collective-permute-start | bytes 1179656 | tf_op jit(solution)/shard_map/ppermute | solution.py:492
  606.2 13.3 %collective-permute-start.65 = (bf16[96,2048]{1,0:T(8,128)(2,1)}, bf16[96,2048]{1,0:T(8,128)(2,1)}, u32[]{:S(2)}, u32[]{:S(2)}) collective-permute-start(bf16[96,2048]{1,0:T(8,128)(2,1)} %add_convert_fusion.5), channel_id=1, source_target_pairs={{1,0},{2,1},{3,2},{5,4},{6,5},{7,6},{9,8},{10,9},{11,10},{13,12},{... | collective-permute-start | bytes 1179656 | tf_op jit(solution)/shard_map/ppermute | solution.py:497
  624.0 20.7 %collective-permute-start.42 = (bf16[96,2048]{1,0:T(8,128)(2,1)}, bf16[96,2048]{1,0:T(8,128)(2,1)}, u32[]{:S(2)}, u32[]{:S(2)}) collective-permute-start(bf16[96,2048]{1,0:T(8,128)(2,1)} %get-tuple-element.174), channel_id=1, source_target_pairs={{0,1},{1,2},{2,3},{4,5},{5,6},{6,7},{8,9},{9,10},{10,11},{12,13},{... | collective-permute-start | bytes 1179656 | tf_op jit(solution)/shard_map/ppermute | solution.py:512
  628.6 30.8 %collective-permute-start.45 = (bf16[96,2048]{1,0:T(8,128)(2,1)}, bf16[96,2048]{1,0:T(8,128)(2,1)}, u32[]{:S(2)}, u32[]{:S(2)}) collective-permute-start(bf16[96,2048]{1,0:T(8,128)(2,1)} %get-tuple-element.174), channel_id=1, source_target_pairs={{1,0},{2,1},{3,2},{5,4},{6,5},{7,6},{9,8},{10,9},{11,10},{13,12},{... | collective-permute-start | bytes 1179656 | tf_op jit(solution)/shard_map/ppermute | solution.py:515
  636.0 24.7 %collective-permute-start.66 = (bf16[96,2048]{1,0:T(8,128)(2,1)S(1)}, bf16[96,2048]{1,0:T(8,128)(2,1)S(1)}, u32[]{:S(2)}, u32[]{:S(2)}) collective-permute-start(bf16[96,2048]{1,0:T(8,128)(2,1)S(1)} %add_convert_fusion.4), channel_id=1, source_target_pairs={{0,1},{1,2},{2,3},{4,5},{5,6},{6,7},{8,9},{9,10},{10,11},{12,13},{... | collective-permute-start | bytes 1179656 | tf_op jit(solution)/shard_map/ppermute | solution.py:512
  640.6 20.8 %collective-permute-start.69 = (bf16[96,2048]{1,0:T(8,128)(2,1)S(1)}, bf16[96,2048]{1,0:T(8,128)(2,1)S(1)}, u32[]{:S(2)}, u32[]{:S(2)}) collective-permute-start(bf16[96,2048]{1,0:T(8,128)(2,1)S(1)} %add_convert_fusion.4), channel_id=1, source_target_pairs={{1,0},{2,1},{3,2},{5,4},{6,5},{7,6},{9,8},{10,9},{11,10},{13,12},{... | collective-permute-start | bytes 1179656 | tf_op jit(solution)/shard_map/ppermute | solution.py:515
  644.6 18.1 %collective-permute-start.43 = (bf16[96,2048]{1,0:T(8,128)(2,1)}, bf16[96,2048]{1,0:T(8,128)(2,1)}, u32[]{:S(2)}, u32[]{:S(2)}) collective-permute-start(bf16[96,2048]{1,0:T(8,128)(2,1)} %collective-permute-done.42), channel_id=1, source_target_pairs={{1,2},{2,3},{5,6},{6,7},{9,10},{10,11},{13,14},{14,15},{17,18},{18... | collective-permute-start | bytes 1179656 | tf_op jit(solution)/shard_map/ppermute | solution.py:512
  659.4 14.2 %collective-permute-start.46 = (bf16[96,2048]{1,0:T(8,128)(2,1)}, bf16[96,2048]{1,0:T(8,128)(2,1)S(1)}, u32[]{:S(2)}, u32[]{:S(2)}) collective-permute-start(bf16[96,2048]{1,0:T(8,128)(2,1)} %collective-permute-done.45), channel_id=1, source_target_pairs={{1,0},{2,1},{5,4},{6,5},{9,8},{10,9},{13,12},{14,13},{17,16},{18,1... | collective-permute-start | bytes 1179656 | tf_op jit(solution)/shard_map/ppermute | solution.py:515
  660.7 14.1 %collective-permute-start.67 = (bf16[96,2048]{1,0:T(8,128)(2,1)S(1)}, bf16[96,2048]{1,0:T(8,128)(2,1)S(1)}, u32[]{:S(2)}, u32[]{:S(2)}) collective-permute-start(bf16[96,2048]{1,0:T(8,128)(2,1)S(1)} %collective-permute-done.66), channel_id=1, source_target_pairs={{1,2},{2,3},{5,6},{6,7},{9,10},{10,11},{13,14},{14,15},{17,18},{18... | collective-permute-start | bytes 1179656 | tf_op jit(solution)/shard_map/ppermute | solution.py:512
  661.4 20.6 %collective-permute-start.70 = (bf16[96,2048]{1,0:T(8,128)(2,1)S(1)}, bf16[96,2048]{1,0:T(8,128)(2,1)S(1)}, u32[]{:S(2)}, u32[]{:S(2)}) collective-permute-start(bf16[96,2048]{1,0:T(8,128)(2,1)S(1)} %collective-permute-done.69), channel_id=1, source_target_pairs={{1,0},{2,1},{5,4},{6,5},{9,8},{10,9},{13,12},{14,13},{17,16},{18,1... | collective-permute-start | bytes 1179656 | tf_op jit(solution)/shard_map/ppermute | solution.py:515
  662.8 20.6 %collective-permute-start.44 = (bf16[96,2048]{1,0:T(8,128)(2,1)}, bf16[96,2048]{1,0:T(8,128)(2,1)S(1)}, u32[]{:S(2)}, u32[]{:S(2)}) collective-permute-start(bf16[96,2048]{1,0:T(8,128)(2,1)} %collective-permute-done.43), channel_id=1, source_target_pairs={{2,3},{6,7},{10,11},{14,15},{18,19},{22,23},{26,27},{30,31}} | collective-permute-start | bytes 1179656 | tf_op jit(solution)/shard_map/ppermute | solution.py:512
  673.6 16.9 %collective-permute-start.47 = (bf16[96,2048]{1,0:T(8,128)(2,1)S(1)}, bf16[96,2048]{1,0:T(8,128)(2,1)S(1)}, u32[]{:S(2)}, u32[]{:S(2)}) collective-permute-start(bf16[96,2048]{1,0:T(8,128)(2,1)S(1)} %collective-permute-done.46), channel_id=1, source_target_pairs={{1,0},{5,4},{9,8},{13,12},{17,16},{21,20},{25,24},{29,28}} | collective-permute-start | bytes 1179656 | tf_op jit(solution)/shard_map/ppermute | solution.py:515
  682.0 13.1 %collective-permute-start.71 = (bf16[96,2048]{1,0:T(8,128)(2,1)S(1)}, bf16[96,2048]{1,0:T(8,128)(2,1)S(1)}, u32[]{:S(2)}, u32[]{:S(2)}) collective-permute-start(bf16[96,2048]{1,0:T(8,128)(2,1)S(1)} %collective-permute-done.70), channel_id=1, source_target_pairs={{1,0},{5,4},{9,8},{13,12},{17,16},{21,20},{25,24},{29,28}} | collective-permute-start | bytes 1179656 | tf_op jit(solution)/shard_map/ppermute | solution.py:515
  (180 other events, 1519.3 us)
Sparse Core Ops, SparseCore 0:
  173.4 48.1 reduce-scatter.6
  290.6 51.0 reduce-scatter.8
  345.0 46.5 all-gather.2
  415.2 42.4 all-gather.4
  460.8 39.2 reduce-scatter.12
  503.8 59.0 reduce-scatter.16
  566.3 73.3 reduce-scatter.10
  643.6 86.7 reduce-scatter.14

commit v3 on v2

--- a/solution.py
+++ b/solution.py
@@ -478,7 +478,7 @@
     return inverse * (scaled - normal * jnp.mean(scaled * normal, axis=-1, keepdims=True))
 
 
-def chain_scatter(partial_sum):
+def scatter_steps(partial_sum):
     parts = lax.axis_size("head")
     place = lax.axis_index("head")
     own_len = partial_sum.shape[0] // parts
@@ -489,57 +489,159 @@
 
     right = left = 0.0
     for step in range(1, parts):
-        right = lax.ppermute(
-            (share(parts - step + place) + right).astype(LOW),
-            "head",
-            [(source, source + 1) for source in range(step)],
-        ).astype(FULL)
-        left = lax.ppermute(
-            (share(step - parts + place) + left).astype(LOW),
-            "head",
-            [(source, source - 1) for source in range(parts - step, parts)],
-        ).astype(FULL)
+        right, left = yield [
+            (
+                (share(parts - step + place) + right).astype(LOW),
+                "head",
+                [(source, source + 1) for source in range(step)],
+            ),
+            (
+                (share(step - parts + place) + left).astype(LOW),
+                "head",
+                [(source, source - 1) for source in range(parts - step, parts)],
+            ),
+        ]
+        right, left = right.astype(FULL), left.astype(FULL)
     return share(place) + right + left
 
 
-def chain_gather(own):
+def gather_steps(own, buffer, micro):
+    parts = lax.axis_size("head")
+    place = lax.axis_index("head")
+    right = left = own
+    before, behind = [None] * parts, [None] * parts
+    for step in range(1, parts):
+        right, left = yield [
+            (right, "head", [(source, source + 1) for source in range(step - 1, parts - 1)]),
+            (left, "head", [(source, source - 1) for source in range(1, parts - step + 1)]),
+        ]
+        before[step], behind[step] = right, left
+    pieces = [(own, place)]
+    for step in range(1, parts):
+        piece = jnp.where(place >= step, before[step], behind[parts - step])
+        pieces.append((piece, lax.rem(place - step + parts, parts)))
+    return placed_pieces(pieces, buffer, micro)
+
+
+def offload_scatter_steps(partial_sum):
+    yield from ()
+    return lax.psum_scatter(partial_sum, "head", scatter_dimension=0, tiled=True).astype(FULL)
+
+
+def offload_gather_steps(own, buffer, micro):
+    yield from ()
+    whole = lax.all_gather(own, "head", axis=0, tiled=True)
+    if buffer is None:
+        return whole
+    buffer[0] = lax.dynamic_update_slice(buffer[0], whole[None], (micro, 0, 0))
+    return buffer
+
+
+def spans(size):
+    masks = []
+    while 1 << len(masks) < size:
+        masks.append((2 << len(masks)) - 1)
+    rest = [[0]]
+    for mask in masks[::-1]:
+        rest.append(rest[-1] + [mask ^ value for value in rest[-1]])
+    return masks, rest[::-1][1:]
+
+
+def pair_scatter_steps(partial_sum):
+    parts = lax.axis_size("head")
+    place = lax.axis_index("head")
+    own_len = partial_sum.shape[0] // parts
+    masks, rests = spans(parts)
+    kept = {
+        code: lax.dynamic_slice_in_dim(partial_sum, (place ^ code) * own_len, own_len, 0)
+        for code in range(parts)
+    }
+    for mask, rest in zip(masks, rests):
+        payload = jnp.concatenate([kept[mask ^ code].astype(LOW) for code in rest], axis=0)
+        (other,) = yield [(payload, "head", [(at, at ^ mask) for at in range(parts)])]
+        kept = {
+            code: kept[code].astype(FULL)
+            + other[index * own_len : (index + 1) * own_len].astype(FULL)
+            for index, code in enumerate(rest)
+        }
+    return kept[0]
+
+
+def pair_gather_steps(own, buffer, micro):
     parts = lax.axis_size("head")
     place = lax.axis_index("head")
     own_len = own.shape[0]
-    right = left = own
-    before, after = [], []
-    for step in range(1, parts):
-        right = lax.ppermute(
-            right, "head", [(source, source + 1) for source in range(step - 1, parts - 1)]
+    masks, rests = spans(parts)
+    kept = {0: own}
+    for mask, rest in zip(masks[::-1], rests[::-1]):
+        payload = jnp.concatenate([kept[code] for code in rest], axis=0)
+        (other,) = yield [(payload, "head", [(at, at ^ mask) for at in range(parts)])]
+        for index, code in enumerate(rest):
+            kept[mask ^ code] = other[index * own_len : (index + 1) * own_len]
+    return placed_pieces(
+        [(kept[code], place ^ code) for code in range(parts)], buffer, micro
+    )
+
+
+def placed_pieces(pieces, buffer, micro):
+    own_len, width = pieces[0][0].shape
+    if buffer is None:
+        whole = jnp.zeros((len(pieces) * own_len, width), pieces[0][0].dtype)
+        for piece, index in pieces:
+            whole = lax.dynamic_update_slice_in_dim(whole, piece, index * own_len, 0)
+        return whole
+    for piece, index in pieces:
+        buffer[0] = lax.dynamic_update_slice(
+            buffer[0], piece[None], (micro, index * own_len, 0)
         )
-        left = lax.ppermute(
-            left, "head", [(source, source - 1) for source in range(1, parts - step + 1)]
-        )
-        before.append(right)
-        after.append(left)
-    joined = jnp.concatenate(before[::-1] + [own] + after, axis=0)
-    return lax.dynamic_slice_in_dim(
-        joined, (parts - 1 - place) * own_len, parts * own_len, 0
-    )
-
-
-def offload_scatter(partial_sum):
-    return lax.psum_scatter(
-        partial_sum.astype(LOW), "head", scatter_dimension=0, tiled=True
-    ).astype(FULL)
-
-
-def offload_gather(own):
-    return lax.all_gather(own, "head", axis=0, tiled=True)
-
-
-def butterfly(value, axis):
-    size = lax.axis_size(axis)
-    bit = 1
-    while bit < size:
-        value = value + lax.ppermute(value, axis, [(place, place ^ bit) for place in range(size)])
-        bit *= 2
+    return buffer
+
+
+def butterfly_steps(value, *axes):
+    for axis in axes:
+        size = lax.axis_size(axis)
+        bit = 1
+        while bit < size:
+            (other,) = yield [(value, axis, [(place, place ^ bit) for place in range(size)])]
+            value = value + other
+            bit *= 2
     return value
+
+
+SCATTERS = dict(C=scatter_steps, P=pair_scatter_steps, S=offload_scatter_steps)
+GATHERS = dict(C=gather_steps, P=pair_gather_steps, S=offload_gather_steps)
+PLAN = dict(
+    out="PP", mid="PP", down="PP", result="PP", grad="PP", attn="PP", inner="PP", final="PP"
+)
+
+
+class Flow:
+    def __init__(self, steps):
+        self.steps = steps
+        self.result = None
+        self.advance(None)
+
+    def advance(self, received):
+        try:
+            self.pending = self.steps.send(received)
+        except StopIteration as stop:
+            self.pending = None
+            self.result = stop.value
+
+
+def tick(flows, work=None):
+    flows[:] = [flow for flow in flows if flow.pending is not None]
+    payloads = [request[0] for flow in flows for request in flow.pending]
+    token = ()
+    if work is not None:
+        token = work(lambda value: after(value, *payloads) if payloads else value)
+        token = tuple(token) if isinstance(token, (tuple, list)) else (token,)
+    for flow in flows:
+        received = [lax.ppermute(*request) for request in flow.pending]
+        if token:
+            received = lax.optimization_barrier(tuple(received) + token)[: len(received)]
+        flow.advance(received)
+    flows[:] = [flow for flow in flows if flow.pending is not None]
 
 
 def packed(entries):
@@ -559,12 +661,6 @@
 
 def after(value, *others):
     return lax.optimization_barrier((value,) + others)[0]
-
-
-scatter_out, gather_mid = chain_scatter, chain_gather
-scatter_down, gather_out = offload_scatter, offload_gather
-scatter_mid, gather_attn = chain_scatter, chain_gather
-scatter_in, gather_in = chain_scatter, chain_gather
 
 
 def per_device(
@@ -584,97 +680,225 @@
     def own_of(value):
         return lax.dynamic_slice_in_dim(value, first_row, own_len, 0)
 
-    micros = []
-    for micro in range(micro_count):
-        rows = tokens[micro].astype(FULL)
-        grad_rows = cotangent[micro].astype(FULL)
-        keep = (positions < lengths[micro, 0]).astype(FULL)
-        normed = rms_scale(rows, norm_in).astype(LOW)
-        projections = tuple(mm(normed, weight) for weight in in_weights + (w_beta, w_alpha))
-        gated, *kept = mixer_forward(projections, conv_taps, decay_log, decay_bias, norm_head)
-        out_part = scatter_out(mm(gated, w_out).astype(LOW))
-        micros.append(
-            dict(rows=own_of(rows), grad_rows=own_of(grad_rows), keep_own=own_of(keep),
-                 down_grad=(keep * grad_rows).astype(LOW), normed=normed,
-                 projections=projections, gated=gated, kept=kept, out_part=out_part)
-        )
-    for held in micros:
-        middle = held["rows"] + held["keep_own"] * held["out_part"]
-        mid = gather_mid(rms_scale(middle, norm_mid).astype(LOW))
-        gate_act = mm(mid, w_up_gate)
-        up_act = mm(mid, w_up)
-        sig = jax.nn.sigmoid(gate_act)
-        hidden = (gate_act * sig * up_act).astype(LOW)
-        grad_hidden = mm(held["down_grad"], w_down, NT)
-        grad_gate = (grad_hidden * up_act * sig * (1.0 + gate_act * (1.0 - sig))).astype(LOW)
-        grad_up = (grad_hidden * gate_act * sig).astype(LOW)
-        mid_part = scatter_mid((mm(grad_gate, w_up_gate, NT) + mm(grad_up, w_up, NT)).astype(LOW))
-        down_part = scatter_down(mm(hidden, w_down).astype(LOW))
-        out_own = (middle + held["keep_own"] * down_part).astype(LOW)
-        held.update(
-            middle=middle, mid=mid, hidden=hidden, grad_gate=grad_gate, grad_up=grad_up,
-            mid_part=mid_part, out=gather_out(out_own),
-        )
+    class Micro:
+        def __init__(self, micro):
+            self.micro = micro
+            keep = (positions < lengths[micro, 0]).astype(LOW)
+            self.rows = own_of(tokens[micro]).astype(FULL)
+            self.grad_rows = own_of(cotangent[micro]).astype(FULL)
+            self.keep_own = own_of(keep).astype(FULL)
+            self.down_grad = keep * cotangent[micro]
+
+        def scatter(self, name, value):
+            return join(Flow(SCATTERS[PLAN[name][self.micro]](value)))
+
+        def gather(self, name, value, buffer=None):
+            return join(Flow(GATHERS[PLAN[name][self.micro]](value, buffer, self.micro)))
+
+        def project(self, tie):
+            rows = tie(tokens[self.micro]).astype(FULL)
+            self.normed = rms_scale(rows, norm_in).astype(LOW)
+            self.projections = tuple(
+                mm(self.normed, weight) for weight in in_weights + (w_beta, w_alpha)
+            )
+            return self.projections
+
+        def mix(self, tie):
+            query, *others = self.projections
+            self.projections = (tie(query), *others)
+            self.gated, *self.kept = mixer_forward(
+                self.projections, conv_taps, decay_log, decay_bias, norm_head
+            )
+            return self.gated
+
+        def project_out(self, tie):
+            self.out_part = mm(tie(self.gated), w_out).astype(LOW)
+            return self.out_part
+
+        def after_mixer(self, out_sum):
+            self.middle = self.rows + self.keep_own * out_sum
+            return self.gather("mid", rms_scale(self.middle, norm_mid).astype(LOW))
+
+        def up(self, tie):
+            mid = tie(self.mid)
+            self.gate_act, self.up_act = mm(mid, w_up_gate), mm(mid, w_up)
+            return self.gate_act, self.up_act
+
+        def activate(self, tie):
+            gate_act, up_act = tie(self.gate_act), self.up_act
+            grad_hidden = mm(self.down_grad, w_down, NT)
+            sig = jax.nn.sigmoid(gate_act)
+            opened = gate_act * sig
+            self.hidden = (opened * up_act).astype(LOW)
+            self.grad_gate = (
+                grad_hidden * up_act * sig * (1.0 + gate_act * (1.0 - sig))
+            ).astype(LOW)
+            self.grad_up = (grad_hidden * opened).astype(LOW)
+            return self.hidden, self.grad_gate, self.grad_up
+
+        def up_back(self, tie):
+            self.mid_part = (
+                mm(tie(self.grad_gate), w_up_gate, NT) + mm(self.grad_up, w_up, NT)
+            ).astype(LOW)
+            return self.mid_part
+
+        def down(self, tie):
+            self.down_part = mm(tie(self.hidden), w_down).astype(LOW)
+            return self.down_part
+
+        def after_down(self, down_sum):
+            own = (self.middle + self.keep_own * down_sum).astype(LOW)
+            return self.gather("result", own, out_buffer)
+
+        def after_up_back(self, mid_sum):
+            self.gain_mid = jnp.sum(rms_scale(self.middle, 1.0) * mid_sum, axis=0)
+            self.grad_middle = self.grad_rows + rms_back(mid_sum, self.middle, norm_mid)
+            return self.gather("attn", (self.keep_own * self.grad_middle).astype(LOW))
+
+        def mix_back(self, tie):
+            grad_gated = mm(tie(self.attn), w_out, NT)
+            self.grads, grad_beta, grad_alpha, *self.small = mixer_backward(
+                grad_gated, self.projections, conv_taps, decay_log, decay_bias,
+                norm_head, self.kept,
+            )
+            self.beta, self.alpha = grad_beta.astype(LOW), grad_alpha.astype(LOW)
+            return self.grads
+
+        def project_back(self, tie):
+            grads = tie(self.grads)
+            in_part = mm(self.beta, w_beta, NT) + mm(self.alpha, w_alpha, NT)
+            for index, weight in enumerate(in_weights):
+                in_part = in_part + mm(
+                    grads[:, index * head_width : (index + 1) * head_width], weight, NT
+                )
+            self.in_part = in_part.astype(LOW)
+            return self.in_part
+
+        def after_project_back(self, in_sum):
+            self.gain_in = jnp.sum(rms_scale(self.rows, 1.0) * in_sum, axis=0)
+            own = (self.grad_middle + rms_back(in_sum, self.rows, norm_in)).astype(LOW)
+            return self.gather("final", own, grad_buffer)
+
+    flows = []
+    out_buffer, grad_buffer = [jnp.zeros_like(tokens)], [jnp.zeros_like(tokens)]
+    one, two = Micro(0), Micro(1)
+    held = (one, two)
 
     def both(*names):
         return jnp.concatenate(
-            [jnp.concatenate([held[name] for name in names], axis=1) for held in micros], axis=0
+            [jnp.concatenate([getattr(h, name) for name in names], axis=1) for h in held], axis=0
         )
 
-    def shared(left, right):
-        return lax.psum_scatter(
-            mm(left, right, TN).astype(LOW), "batch", scatter_dimension=0, tiled=True
-        ).astype(FULL)
-
-    share_ups = shared(both("mid"), both("grad_gate", "grad_up"))
-    share_down = shared(both("down_grad"), both("hidden")).T
-    gain_in = jnp.zeros((model_dim,), FULL)
-    gain_mid = jnp.zeros((model_dim,), FULL)
-    small = None
-    for held in micros:
-        middle = held["middle"]
-        gain_mid = gain_mid + jnp.sum(rms_scale(middle, 1.0) * held["mid_part"], axis=0)
-        grad_middle = held["grad_rows"] + rms_back(held["mid_part"], middle, norm_mid)
-        attn = gather_attn((held["keep_own"] * grad_middle).astype(LOW))
-        grads, grad_beta, grad_alpha, grad_taps, grad_dlog, grad_dbias, grad_gain = mixer_backward(
-            mm(attn, w_out, NT), held["projections"], conv_taps, decay_log, decay_bias,
-            norm_head, held["kept"],
-        )
-        narrow = (grad_beta.astype(LOW), grad_alpha.astype(LOW))
-        in_part = mm(narrow[0], w_beta, NT) + mm(narrow[1], w_alpha, NT)
-        for index, weight in enumerate(in_weights):
-            in_part = in_part + mm(
-                grads[:, index * head_width : (index + 1) * head_width], weight, NT
-            )
-        in_part = scatter_in(in_part.astype(LOW))
-        gain_in = gain_in + jnp.sum(rms_scale(held["rows"], 1.0) * in_part, axis=0)
-        grad_own = (grad_middle + rms_back(in_part, held["rows"], norm_in)).astype(LOW)
-        entries = (grad_taps, grad_dlog, grad_dbias, grad_gain)
-        small = entries if small is None else tuple(a + b for a, b in zip(small, entries))
-        held.update(attn=attn, grads=grads, beta=narrow[0], alpha=narrow[1],
-                    grad_tokens=gather_in(grad_own))
-    share_out = shared(both("attn"), both("gated")).T
-    normed_both = both("normed")
-    share_in = shared(normed_both, both("grads"))
-    tiny = mm(both("beta", "alpha"), normed_both, TN)
-    grad_taps, grad_dlog, grad_dbias, grad_gain = small
-    entries = (tiny, grad_taps, grad_dlog[0], grad_dbias[0])
-    tiny, grad_taps, grad_dlog, grad_dbias = unpacked(
-        butterfly(packed(entries), "batch"), entries
-    )
-    entries = (gain_in, grad_gain[0], gain_mid)
-    gains = unpacked(butterfly(butterfly(packed(entries), "batch"), "head"), entries)
+    def shared(product):
+        return lax.psum_scatter(product, "batch", scatter_dimension=0, tiled=True).astype(FULL)
+
+    def together(*works):
+        return lambda tie: sum((as_tuple(work(tie)) for work in works), ())
+
+    def as_tuple(value):
+        return tuple(value) if isinstance(value, (tuple, list)) else (value,)
+
+    def join(flow):
+        flows.append(flow)
+        return flow
+
+    def until(flow, *works):
+        for work in works:
+            tick(flows, work)
+        while flow.result is None:
+            tick(flows)
+        return flow.result
+
+    product = {}
+
+    def ff_products(tie):
+        ups = mm(tie(both("mid")), both("grad_gate", "grad_up"), TN).astype(LOW)
+        downs = mm(both("down_grad"), both("hidden"), TN).astype(LOW)
+        product["ff"] = jnp.concatenate([ups, downs], axis=1)
+        return product["ff"]
+
+    def out_product(tie):
+        product["out"] = mm(tie(both("attn")), both("gated"), TN).astype(LOW)
+        return product["out"]
+
+    def in_product(tie):
+        normed = after(tie(both("normed")), share_ff)
+        product["in"] = mm(normed, both("grads"), TN).astype(LOW)
+        product["tiny"] = mm(both("beta", "alpha"), normed, TN)
+        return product["in"], product["tiny"]
+
+    def free(value):
+        return value
+
+    one.project(free), one.mix(free), one.project_out(free)
+    flow = one.scatter("out", one.out_part)
+    until(
+        flow,
+        lambda tie: two.project(lambda value: after(tie(value), one.out_part)),
+        two.mix,
+        two.project_out,
+    )
+    flow_two = two.scatter("out", two.out_part)
+    one.mid = until(one.after_mixer(flow.result))
+    flow = two.after_mixer(until(flow_two))
+    tick(flows, one.up)
+    tick(flows, one.activate)
+    tick(flows, one.up_back)
+    sum_one = one.scatter("grad", one.mid_part)
+    two.mid = until(flow)
+    tick(flows, one.down)
+    down_one = one.scatter("down", one.down_part)
+    until(sum_one, two.up, two.activate, two.up_back)
+    attn_one = one.after_up_back(sum_one.result)
+    sum_two = two.scatter("grad", two.mid_part)
+    tick(flows, two.down)
+    out_one = one.after_down(until(down_one))
+    down_two = two.scatter("down", two.down_part)
+    tick(flows, ff_products)
+    share_ff = shared(product["ff"])
+    one.attn = until(attn_one)
+    attn_two = two.after_up_back(until(sum_two))
+    tick(flows, one.mix_back)
+    tick(flows, one.project_back)
+    sum_one = one.scatter("inner", one.in_part)
+    two.attn = until(attn_two)
+    until(out_one)
+    out_two = two.after_down(until(down_two))
+    tick(flows, lambda tie: two.mix_back(lambda value: after(tie(value), one.in_part)))
+    tick(flows, two.project_back)
+    sum_two = two.scatter("inner", two.in_part)
+    tick(flows, together(in_product, out_product))
+    share_in = shared(jnp.concatenate([product["in"], product["out"]], axis=1))
+    small = [a + b for a, b in zip(one.small, two.small)]
+    local = (product["tiny"], small[0], small[1][0], small[2][0])
+    local_flow = join(Flow(butterfly_steps(packed(local), "batch")))
+    grad_one = one.after_project_back(until(sum_one))
+    grad_two = two.after_project_back(until(sum_two))
+    wide = (one.gain_in + two.gain_in, small[3][0], one.gain_mid + two.gain_mid)
+    wide_flow = join(Flow(butterfly_steps(packed(wide), "batch", "head")))
+    while flows:
+        tick(flows)
+    tiny, grad_taps, grad_dlog, grad_dbias = unpacked(local_flow.result, local)
+    gains = unpacked(wide_flow.result, wide)
     width = model_dim // batch_parts
     tiny = lax.dynamic_slice_in_dim(tiny, lax.axis_index("batch") * width, width, 1).T
     count = w_beta.shape[1]
+
+    def pieces(matrix, *widths):
+        outs, start = [], 0
+        for extent in widths:
+            outs.append(matrix[:, start : start + extent])
+            start += extent
+        return outs
+
+    *share_in, share_out = pieces(share_in, *([head_width] * 5))
+    share_gate, share_up, share_down = pieces(share_ff, *([hidden_width] * 3))
     return (
-        jnp.stack([held["out"] for held in micros]),
-        jnp.stack([held["grad_tokens"] for held in micros]),
-        gains[0],
-        *(share_in[:, index * head_width : (index + 1) * head_width] for index in range(4)),
-        tiny[:, :count], tiny[:, count:],
+        out_buffer[0],
+        grad_buffer[0],
+        gains[0], *share_in, tiny[:, :count], tiny[:, count:],
         grad_taps, grad_dlog, grad_dbias, gains[1],
-        share_out, gains[2], share_ups[:, :hidden_width], share_ups[:, hidden_width:], share_down,
+        share_out.T, gains[2], share_gate, share_up, share_down.T,
     )
 
 

time: 751 us -> 583 us (0.78)
  starting transfers between devices: 169 us -> 51.2 us
  waiting for transfers between devices: 244 us -> 196 us
    ppermute x80 -> x40, starting transfers between devices: 169 us -> 50.9 us  [tick(): received = [lax.ppermute(*request) for request in flow.pending]]
    concatenate x0 -> x21, other arithmetic: none -> 39.2 us  [the longest x1 12.6 us: per_device(): share_in = shared(jnp.concatenate([product['in'], product['out']], axis=1))]
    convert_element_type x31 -> x18, other arithmetic: 48.1 us -> 15.9 us  [the longest x8 6.64 us: pair_scatter_steps(): kept[mask ^ code].astype(LOW)]
    ppermute x80 -> x40, waiting for transfers between devices: 220 us -> 196 us  [tick(): received = [lax.ppermute(*request) for request in flow.pending]]
    reduce_scatter x6 -> x2, waiting for transfers between devices: 23.2 us -> 0.01 us  [shared(): lax.psum_scatter(product, 'batch', scatter_dimension=0, tiled=True)]
    unnamed x319 -> x245, local copies, waits for them, and re-layouts: 49.6 us -> 30.2 us
    dynamic_update_slice x0 -> x23, local copies, waits for them, and re-layouts: none -> 13.2 us  [the longest x11 10.6 us: placed_pieces(): lax.dynamic_update_slice(buffer[0], piece[None], (micro, index * own_len,...]
    dynamic_update_slice x0 -> x8, other arithmetic: none -> 9.77 us  [the longest x4 5.6 us: placed_pieces(): lax.dynamic_update_slice(buffer[0], piece[None], (micro, index * own_len,...]
  transfers between devices with their start and end apart: 88 -> 42, of which waited for: 37 -> 15; matrix products, arithmetic and copies ran while one was open for 27% -> 30% of each run, Pallas kernels for 5% -> 7%
where the time goes in v3:
time: 583 us; the launch traced here: 578 us
  waiting for transfers between devices  196 us (34%)
  matrix products  123 us (21%)
  other arithmetic  79 us (14%)
  local copies, waits for them, and re-layouts  62.5 us (11%)
  starting transfers between devices  51.2 us (9%)
  Pallas kernels  49.9 us (9%)
  between operations  16.4 us (3%)
    ppermute x40, waiting for transfers between devices, tick(): received = [lax.ppermute(*request) for request in flow.pending]  196 us
    dot_general x45, matrix products, mm(): lax.dot_general(left.astype(LOW), right.astype(LOW), (dims, ((), ())), pr...  123 us
    ppermute x40, starting transfers between devices, tick(): received = [lax.ppermute(*request) for request in flow.pending]  50.9 us
    pallas_call x2, Pallas kernels, mixer_backward(): pl.pallas_call(mixer_backward_body, grid=(heads // group,), in_specs=[wid...  31.1 us
    unnamed x245, local copies, waits for them, and re-layouts  30.2 us
    pallas_call x2, Pallas kernels, mixer_forward(): pl.pallas_call(mixer_forward_body, grid=(heads // group,), in_specs=[wide...  18.8 us
    concatenate x1, other arithmetic, per_device(): share_in = shared(jnp.concatenate([product['in'], product['out']], axis=1))  12.6 us
  transfers between devices with their start and end apart: 42, of which 15 were waited for; matrix products, arithmetic and copies ran while one was open for 30% of the time, Pallas kernels for 7%

profile of v3, /device:TPU:0, one launch (start us, length us, event | category | flops | bytes accessed | tf_op | source)
XLA Modules:
  0.0 577.8 jit_solution(16711618617432632065)
XLA Ops:
  19.3 9.6 %mixer_forward.2 = (bf16[384,512]{1,0:T(8,128)(2,1)S(1)}, f32[384,512]{1,0:T(8,128)S(1)}, bf16[384,512]{1,0:T(8,128)(2,1)S(1)}, bf16[4,3,128,128]{3,2,1,0:T(8,128)(2,1)S(1)}, bf16[4,3,128,128]{3,2,1,0:T(8,128)(2,1)S(1)}) custom-call(f32[384,512]{1,0:T(8,128)S(1)} %fusion.97.query_ref, f32[384,512]{1,0:T(8,128)S(1)} %fusion.98.key_ref, ...), custom_call_target="tpu_custom_call" | custom-call | tf_op jit(solution)/shard_map/mixer_forward/pallas_call | solution.py:411
  36.5 3.0 collective-permute-start
  58.8 3.6 collective-permute-start.1
  62.3 9.2 %mixer_forward.3 = (bf16[384,512]{1,0:T(8,128)(2,1)S(1)}, f32[384,512]{1,0:T(8,128)S(1)}, bf16[384,512]{1,0:T(8,128)(2,1)S(1)}, bf16[4,3,128,128]{3,2,1,0:T(8,128)(2,1)S(1)}, bf16[4,3,128,128]{3,2,1,0:T(8,128)(2,1)S(1)}) custom-call(f32[384,512]{1,0:T(8,128)S(1)} %fusion.103.query_ref, f32[384,512]{1,0:T(8,128)S(1)} %copy-done.1, f32[384,512]{1,0:T(8,128)S(1)} %copy-done.3, ...), custom_call_target="tpu_custom_call" | custom-call | tf_op jit(solution)/shard_map/mixer_forward/pallas_call | solution.py:411
  76.7 27.6 %collective-permute-done.4 = bf16[192,2048]{1,0:T(8,128)(2,1)S(1)} collective-permute-done((bf16[192,2048]{1,0:T(8,128)(2,1)S(1)}, bf16[192,2048]{1,0:T(8,128)(2,1)S(1)}, u32[]{:S(2)}, u32[]{:S(2)}) %collective-permute-start.4) | collective-permute-done | bytes 786464 | tf_op jit(solution)/shard_map/ppermute | solution.py:640
  106.8 11.6 %collective-permute-done.5 = bf16[96,2048]{1,0:T(8,128)(2,1)S(1)} collective-permute-done((bf16[96,2048]{1,0:T(8,128)(2,1)S(1)}, bf16[96,2048]{1,0:T(8,128)(2,1)S(1)}, u32[]{:S(2)}, u32[]{:S(2)}) %collective-permute-start.5) | collective-permute-done | bytes 393248 | tf_op jit(solution)/shard_map/ppermute | solution.py:640
  120.9 12.3 %collective-permute-done.3 = bf16[192,2048]{1,0:T(8,128)(2,1)S(1)} collective-permute-done((bf16[192,2048]{1,0:T(8,128)(2,1)S(1)}, bf16[192,2048]{1,0:T(8,128)(2,1)S(1)}, u32[]{:S(2)}, u32[]{:S(2)}) %collective-permute-start.3) | collective-permute-done | bytes 786464 | tf_op jit(solution)/shard_map/ppermute | solution.py:640
  133.5 2.6 fusion.109
  136.1 2.6 fusion.110
  138.9 6.0 %multiply_convert_fusion.3 = (bf16[384,1408]{1,0:T(8,128)(2,1)S(1)}, bf16[384,1408]{1,0:T(8,128)(2,1)S(1)}, bf16[384,1408]{1,0:T(8,128)(2,1)S(1)}) fusion(f32[384,1408]{1,0:T(8,128)S(1)} %fusion.109, f32[384,1408]{1,0:T(8,128)S(1)} %fusion.110, bf16[384,2048]{1,0:T(8,128)(2,1)S(1)} %get-tuple-element.223, bf16[1408,2048]{1,0:T(8,128)(2,1)} %param.37), kind=kOutput, calls=%fused_computation.48 | convolution fusion | flops 2222702592 | bytes 14909440 | tf_op jit(solution)/shard_map/dot_general | solution.py:17
  145.0 5.9 %fusion.111 = f32[384,2048]{1,0:T(8,128)S(1)} fusion(bf16[384,1408]{1,0:T(8,128)(2,1)S(1)} %get-tuple-element.218, bf16[2048,1408]{1,0:T(8,128)(2,1)} %param.35), kind=kOutput, calls=%fused_computation.266 | convolution fusion | flops 2214592512 | bytes 9994240 | tf_op jit(solution)/shard_map/dot_general | solution.py:17
  150.9 5.3 add_convert_fusion.3
  158.4 5.5 convolution_convert_fusion.5
  164.3 13.8 %collective-permute-done.9 = bf16[192,2048]{1,0:T(8,128)(2,1)S(1)} collective-permute-done((bf16[192,2048]{1,0:T(8,128)(2,1)S(1)}, bf16[192,2048]{1,0:T(8,128)(2,1)S(1)}, u32[]{:S(2)}, u32[]{:S(2)}) %collective-permute-start.9) | collective-permute-done | bytes 786464 | tf_op jit(solution)/shard_map/ppermute | solution.py:640
  178.3 2.6 fusion.112
  181.0 4.0 fusion.113
  185.0 12.3 %collective-permute-done.7 = bf16[192,2048]{1,0:T(8,128)(2,1)S(1)} collective-permute-done((bf16[192,2048]{1,0:T(8,128)(2,1)S(1)}, bf16[192,2048]{1,0:T(8,128)(2,1)S(1)}, u32[]{:S(2)}, u32[]{:S(2)}) %collective-permute-start.7) | collective-permute-done | bytes 786464 | tf_op jit(solution)/shard_map/ppermute | solution.py:640
  197.5 8.3 %multiply_convert_fusion = (bf16[384,1408]{1,0:T(8,128)(2,1)S(1)}, bf16[384,1408]{1,0:T(8,128)(2,1)S(1)}, bf16[384,1408]{1,0:T(8,128)(2,1)}) fusion(f32[384,1408]{1,0:T(8,128)S(1)} %fusion.112, f32[384,1408]{1,0:T(8,128)} %fusion.113, bf16[384,2048]{1,0:T(8,128)(2,1)S(1)} %get-tuple-element.222, bf16[1408,2048]{1,0:T(8,128)(2,1)} %param.37), kind=kOutput, calls=%fused_computation.43 | convolution fusion | flops 2222702592 | bytes 14909440 | tf_op jit(solution)/shard_map/dot_general | solution.py:17
  205.7 5.5 fusion.114
  211.2 5.3 add_convert_fusion.2
  218.7 7.2 %convolution_convert_fusion.2 = bf16[2048,1408]{1,0:T(8,128)(2,1)} fusion(bf16[384,2048]{1,0:T(8,128)(2,1)S(1)} %get-tuple-element.222, bf16[384,2048]{1,0:T(8,128)(2,1)S(1)} %get-tuple-element.223, bf16[384,1408]{1,0:T(8,128)(2,1)S(1)} %copy-done.110, bf16[384,1408]{1,0:T(8,128)(2,1)S(1)} %copy-done.109), kind=kOutput, calls=%fused_computation.4 | convolution fusion | flops 4442685440 | bytes 11075584 | tf_op jit(solution)/shard_map/dot_general | solution.py:17
  231.3 3.8 collective-permute-start.13
  235.1 5.3 convolution_convert_fusion.4
  245.6 11.9 %convolution_convert_fusion = bf16[2048,2816]{1,0:T(8,128)(2,1)S(1)} fusion(bf16[768,2048]{1,0:T(8,128)(2,1)} %pad_maximum_fusion.2, bf16[384,1408]{1,0:T(8,128)(2,1)} %copy-done.105, bf16[384,1408]{1,0:T(8,128)(2,1)} %copy-done.107, bf16[384,1408]{1,0:T(8,128)(2,1)S(1)} %get-tuple-element.217, bf16[384,1408]{1,0:T(8,128)(2,1)} %copy-done.106), kind=kOutput, calls=%fused_computation.1 | convolution fusion | flops 8881438720 | bytes 19005440 | tf_op jit(solution)/shard_map/dot_general | solution.py:17
  257.5 9.7 %pad_maximum_fusion = bf16[2048,4224]{1,0:T(8,128)(2,1)} fusion(bf16[2048,1408]{1,0:T(8,128)(2,1)} %convolution_convert_fusion.2, bf16[2048,2816]{1,0:T(8,128)(2,1)S(1)} %convolution_convert_fusion), kind=kLoop, calls=%fused_computation | loop fusion | flops 34603008 | bytes 34603008 | tf_op jit(solution)/shard_map/concatenate | solution.py:817
  268.3 2.9 collective-permute-start.11
  271.2 4.6 pad_maximum_fusion.3
  276.6 21.6 %collective-permute-done.11 = bf16[96,2048]{1,0:T(8,128)(2,1)S(1)} collective-permute-done((bf16[96,2048]{1,0:T(8,128)(2,1)}, bf16[96,2048]{1,0:T(8,128)(2,1)S(1)}, u32[]{:S(2)}, u32[]{:S(2)}) %collective-permute-start.11) | collective-permute-done | bytes 393248 | tf_op jit(solution)/shard_map/ppermute | solution.py:640
  299.6 23.8 %collective-permute-done.18 = bf16[96,2048]{1,0:T(8,128)(2,1)S(1)} collective-permute-done((bf16[96,2048]{1,0:T(8,128)(2,1)S(1)}, bf16[96,2048]{1,0:T(8,128)(2,1)S(1)}, u32[]{:S(2)}, u32[]{:S(2)}) %collective-permute-start.18) | collective-permute-done | bytes 393248 | tf_op jit(solution)/shard_map/ppermute | solution.py:640
  330.1 2.8 fusion.115.grad_ref
  333.0 15.7 %mixer_backward.2 = (bf16[384,2048]{1,0:T(8,128)(2,1)}, f32[384,4]{1,0:T(8,128)S(1)}, f32[384,4]{1,0:T(8,128)S(1)}, f32[3,4,512]{2,1,0:T(4,128)S(1)}, f32[1,4]{1...) custom-call(f32[384,512]{1,0:T(8,128)S(1)} %fusion.115.grad_ref, f32[384,512]{1,0:T(8,128)S(1)} %copy-done.10, ...), custom_call_target="tpu_custom_call" | custom-call | tf_op jit(solution)/shard_map/mixer_backward/pallas_call | solution.py:442
  352.8 2.5 collective-permute-start.20
  365.1 10.0 %collective-permute-done.22 = bf16[192,2048]{1,0:T(8,128)(2,1)S(1)} collective-permute-done((bf16[192,2048]{1,0:T(8,128)(2,1)S(1)}, bf16[192,2048]{1,0:T(8,128)(2,1)S(1)}, u32[]{:S(2)}, u32[]{:S(2)}) %collective-permute-start.22) | collective-permute-done | bytes 786464 | tf_op jit(solution)/shard_map/ppermute | solution.py:640
  377.2 15.4 %mixer_backward.3 = (bf16[384,2048]{1,0:T(8,128)(2,1)}, f32[384,4]{1,0:T(8,128)S(1)}, f32[384,4]{1,0:T(8,128)S(1)}, f32[3,4,512]{2,1,0:T(4,128)S(1)}, f32[1,4]{1...) custom-call(f32[384,512]{1,0:T(8,128)S(1)} %fusion.118.grad_ref, f32[384,512]{1,0:T(8,128)S(1)} %fusion.103.query_ref, ...), custom_call_target="tpu_custom_call" | custom-call | tf_op jit(solution)/shard_map/mixer_backward/pallas_call | solution.py:442
  408.0 3.3 convolution_convert_fusion.3
  411.3 4.0 convert_element_type.400
  415.9 7.1 %convolution_convert_fusion.1 = bf16[2048,2048]{0,1:T(8,128)(2,1)S(1)} fusion(bf16[768,2048]{1,0:T(8,128)(2,1)S(1)} %copy-done.45, bf16[384,2048]{1,0:T(8,128)(2,1)S(1)} %copy-done.91, bf16[384,2048]{1,0:T(8,128)(2,1)S(1)} %copy-done.89), kind=kOutput, calls=%fused_computation.3 | convolution fusion | flops 6452936704 | bytes 14680064 | tf_op jit(solution)/shard_map/dot_general | solution.py:17
  423.0 12.6 %pad_maximum_fusion.1 = bf16[2048,2560]{0,1:T(8,128)(2,1)} fusion(bf16[2048,512]{0,1:T(8,128)(2,1)S(1)} %copy-done.75, bf16[2048,2048]{0,1:T(8,128)(2,1)S(1)} %convolution_convert_fusion.1), kind=kLoop, calls=%fused_computation.2 | loop fusion | flops 20971520 | bytes 20971520 | tf_op jit(solution)/shard_map/concatenate | solution.py:871
  438.4 3.3 fusion.66
  441.7 13.8 %collective-permute-done.28 = bf16[192,2048]{1,0:T(8,128)(2,1)} collective-permute-done((bf16[192,2048]{1,0:T(8,128)(2,1)}, bf16[192,2048]{1,0:T(8,128)(2,1)}, u32[]{:S(2)}, u32[]{:S(2)}) %collective-permute-start.28) | collective-permute-done | bytes 786464 | tf_op jit(solution)/shard_map/ppermute | solution.py:640
  457.5 10.5 %collective-permute-done.23 = bf16[192,2048]{1,0:T(8,128)(2,1)S(1)} collective-permute-done((bf16[192,2048]{1,0:T(8,128)(2,1)}, bf16[192,2048]{1,0:T(8,128)(2,1)S(1)}, u32[]{:S(2)}, u32[]{:S(2)}) %collective-permute-start.23) | collective-permute-done | bytes 786464 | tf_op jit(solution)/shard_map/ppermute | solution.py:640
  479.3 8.7 %collective-permute-done.26 = bf16[96,2048]{1,0:T(8,128)(2,1)S(1)} collective-permute-done((bf16[96,2048]{1,0:T(8,128)(2,1)S(1)}, bf16[96,2048]{1,0:T(8,128)(2,1)S(1)}, u32[]{:S(2)}, u32[]{:S(2)}) %collective-permute-start.26) | collective-permute-done | bytes 393248 | tf_op jit(solution)/shard_map/ppermute | solution.py:640
  488.1 6.3 %collective-permute-start.27 = (bf16[192,2048]{1,0:T(8,128)(2,1)S(1)}, bf16[192,2048]{1,0:T(8,128)(2,1)S(1)}, u32[]{:S(2)}, u32[]{:S(2)}) collective-permute-start(bf16[192,2048]{1,0:T(8,128)(2,1)S(1)} %pad_maximum_fusion.18), channel_id=1, source_target_pairs={{0,1},{1,0},{2,3},{3,2},{4,5},{5,4},{6,7},{7,6},{8,9},{9,8},{10,11... | collective-permute-start | bytes 2359304 | tf_op jit(solution)/shard_map/ppermute | solution.py:640
  498.6 12.6 %collective-permute-done.27 = bf16[192,2048]{1,0:T(8,128)(2,1)S(1)} collective-permute-done((bf16[192,2048]{1,0:T(8,128)(2,1)S(1)}, bf16[192,2048]{1,0:T(8,128)(2,1)S(1)}, u32[]{:S(2)}, u32[]{:S(2)}) %collective-permute-start.27) | collective-permute-done | bytes 786464 | tf_op jit(solution)/shard_map/ppermute | solution.py:640
  516.1 2.6 slice_bitcast_fusion
  518.7 2.9 copy.68
  528.1 7.0 %collective-permute-start.31 = (bf16[192,2048]{1,0:T(8,128)(2,1)}, bf16[192,2048]{1,0:T(8,128)(2,1)}, u32[]{:S(2)}, u32[]{:S(2)}) collective-permute-start(bf16[192,2048]{1,0:T(8,128)(2,1)} %pad_maximum_fusion.20), channel_id=1, source_target_pairs={{0,1},{1,0},{2,3},{3,2},{4,5},{5,4},{6,7},{7,6},{8,9},{9,8},{10,11... | collective-permute-start | bytes 2359304 | tf_op jit(solution)/shard_map/ppermute | solution.py:640
  537.4 14.4 %collective-permute-done.36 = f32[40,128]{1,0:T(8,128)S(1)} collective-permute-done((f32[40,128]{1,0:T(8,128)S(1)}, f32[40,128]{1,0:T(8,128)S(1)}, u32[]{:S(2)}, u32[]{:S(2)}) %collective-permute-start.36) | collective-permute-done | bytes 20512 | tf_op jit(solution)/shard_map/ppermute | solution.py:640
  (478 shorter events, 158.5 us)
Async XLA Ops:
  7.2 404.1 %reduce-scatter.3.cloned.1.call-start = ((), (), s32[]{:S(2)}) async-start(), calls=%async_computation.2 | async-start | bytes 19464192 | tf_op jit(solution)/shard_map/reduce_scatter | solution.py:793
  36.5 21.1 %collective-permute-start = (bf16[192,2048]{1,0:T(8,128)(2,1)}, bf16[192,2048]{1,0:T(8,128)(2,1)}, u32[]{:S(2)}, u32[]{:S(2)}) collective-permute-start(bf16[192,2048]{1,0:T(8,128)(2,1)} %pad_maximum_fusion.5), channel_id=1, source_target_pairs={{0,1},{1,0},{2,3},{3,2},{4,5},{5,4},{6,7},{7,6},{8,9},{9,8},{10,11... | collective-permute-start | bytes 2359304 | tf_op jit(solution)/shard_map/ppermute | solution.py:640
  58.8 14.4 %collective-permute-start.1 = (bf16[96,2048]{1,0:T(8,128)(2,1)S(1)}, bf16[96,2048]{1,0:T(8,128)(2,1)S(1)}, u32[]{:S(2)}, u32[]{:S(2)}) collective-permute-start(bf16[96,2048]{1,0:T(8,128)(2,1)S(1)} %add_convert_fusion.13), channel_id=1, source_target_pairs={{0,3},{1,2},{2,1},{3,0},{4,7},{5,6},{6,5},{7,4},{8,11},{9,10},{10,... | collective-permute-start | bytes 1179656 | tf_op jit(solution)/shard_map/ppermute | solution.py:640
  73.1 31.2 %collective-permute-start.4 = (bf16[192,2048]{1,0:T(8,128)(2,1)S(1)}, bf16[192,2048]{1,0:T(8,128)(2,1)S(1)}, u32[]{:S(2)}, u32[]{:S(2)}) collective-permute-start(bf16[192,2048]{1,0:T(8,128)(2,1)S(1)} %pad_maximum_fusion.7), channel_id=1, source_target_pairs={{0,1},{1,0},{2,3},{3,2},{4,5},{5,4},{6,7},{7,6},{8,9},{9,8},{10,11... | collective-permute-start | bytes 2359304 | tf_op jit(solution)/shard_map/ppermute | solution.py:640
  75.6 31.1 %collective-permute-start.2 = (bf16[96,2048]{1,0:T(8,128)(2,1)S(1)}, bf16[96,2048]{1,0:T(8,128)(2,1)S(1)}, u32[]{:S(2)}, u32[]{:S(2)}) collective-permute-start(bf16[96,2048]{1,0:T(8,128)(2,1)S(1)} %get-tuple-element.211), channel_id=1, source_target_pairs={{0,3},{1,2},{2,1},{3,0},{4,7},{5,6},{6,5},{7,4},{8,11},{9,10},{10,... | collective-permute-start | bytes 1179656 | tf_op jit(solution)/shard_map/ppermute | solution.py:640
  104.4 14.1 %collective-permute-start.5 = (bf16[96,2048]{1,0:T(8,128)(2,1)S(1)}, bf16[96,2048]{1,0:T(8,128)(2,1)S(1)}, u32[]{:S(2)}, u32[]{:S(2)}) collective-permute-start(bf16[96,2048]{1,0:T(8,128)(2,1)S(1)} %add_convert_fusion.12), channel_id=1, source_target_pairs={{0,3},{1,2},{2,1},{3,0},{4,7},{5,6},{6,5},{7,4},{8,11},{9,10},{10,... | collective-permute-start | bytes 1179656 | tf_op jit(solution)/shard_map/ppermute | solution.py:640
  106.7 26.6 %collective-permute-start.3 = (bf16[192,2048]{1,0:T(8,128)(2,1)S(1)}, bf16[192,2048]{1,0:T(8,128)(2,1)S(1)}, u32[]{:S(2)}, u32[]{:S(2)}) collective-permute-start(bf16[192,2048]{1,0:T(8,128)(2,1)S(1)} %pad_maximum_fusion.6), channel_id=1, source_target_pairs={{0,1},{1,0},{2,3},{3,2},{4,5},{5,4},{6,7},{7,6},{8,9},{9,8},{10,11... | collective-permute-start | bytes 2359304 | tf_op jit(solution)/shard_map/ppermute | solution.py:640
  120.9 17.9 %collective-permute-start.6 = (bf16[96,2048]{1,0:T(8,128)(2,1)S(1)}, bf16[96,2048]{1,0:T(8,128)(2,1)S(1)}, u32[]{:S(2)}, u32[]{:S(2)}) collective-permute-start(bf16[96,2048]{1,0:T(8,128)(2,1)S(1)} %get-tuple-element.207), channel_id=1, source_target_pairs={{0,3},{1,2},{2,1},{3,0},{4,7},{5,6},{6,5},{7,4},{8,11},{9,10},{10,... | collective-permute-start | bytes 1179656 | tf_op jit(solution)/shard_map/ppermute | solution.py:640
  138.9 25.3 %collective-permute-start.8 = (bf16[192,2048]{1,0:T(8,128)(2,1)S(1)}, bf16[192,2048]{1,0:T(8,128)(2,1)S(1)}, u32[]{:S(2)}, u32[]{:S(2)}) collective-permute-start(bf16[192,2048]{1,0:T(8,128)(2,1)S(1)} %pad_maximum_fusion.8), channel_id=1, source_target_pairs={{0,1},{1,0},{2,3},{3,2},{4,5},{5,4},{6,7},{7,6},{8,9},{9,8},{10,11... | collective-permute-start | bytes 2359304 | tf_op jit(solution)/shard_map/ppermute | solution.py:640
  156.4 21.7 %collective-permute-start.9 = (bf16[192,2048]{1,0:T(8,128)(2,1)S(1)}, bf16[192,2048]{1,0:T(8,128)(2,1)S(1)}, u32[]{:S(2)}, u32[]{:S(2)}) collective-permute-start(bf16[192,2048]{1,0:T(8,128)(2,1)S(1)} %pad_maximum_fusion.9), channel_id=1, source_target_pairs={{0,1},{1,0},{2,3},{3,2},{4,5},{5,4},{6,7},{7,6},{8,9},{9,8},{10,11... | collective-permute-start | bytes 2359304 | tf_op jit(solution)/shard_map/ppermute | solution.py:640
  164.0 33.2 %collective-permute-start.7 = (bf16[192,2048]{1,0:T(8,128)(2,1)S(1)}, bf16[192,2048]{1,0:T(8,128)(2,1)S(1)}, u32[]{:S(2)}, u32[]{:S(2)}) collective-permute-start(bf16[192,2048]{1,0:T(8,128)(2,1)S(1)} %pad_maximum_fusion.10), channel_id=1, source_target_pairs={{0,1},{1,0},{2,3},{3,2},{4,5},{5,4},{6,7},{7,6},{8,9},{9,8},{10,11... | collective-permute-start | bytes 2359304 | tf_op jit(solution)/shard_map/ppermute | solution.py:640
  178.2 49.8 %collective-permute-start.12 = (bf16[96,2048]{1,0:T(8,128)(2,1)S(1)}, bf16[96,2048]{1,0:T(8,128)(2,1)S(1)}, u32[]{:S(2)}, u32[]{:S(2)}) collective-permute-start(bf16[96,2048]{1,0:T(8,128)(2,1)S(1)} %add_convert_fusion.11), channel_id=1, source_target_pairs={{0,3},{1,2},{2,1},{3,0},{4,7},{5,6},{6,5},{7,4},{8,11},{9,10},{10,... | collective-permute-start | bytes 1179656 | tf_op jit(solution)/shard_map/ppermute | solution.py:640
  197.4 44.4 %collective-permute-start.10 = (bf16[96,2048]{1,0:T(8,128)(2,1)S(1)}, bf16[96,2048]{1,0:T(8,128)(2,1)S(1)}, u32[]{:S(2)}, u32[]{:S(2)}) collective-permute-start(bf16[96,2048]{1,0:T(8,128)(2,1)S(1)} %add_convert_fusion.10), channel_id=1, source_target_pairs={{0,3},{1,2},{2,1},{3,0},{4,7},{5,6},{6,5},{7,4},{8,11},{9,10},{10,... | collective-permute-start | bytes 1179656 | tf_op jit(solution)/shard_map/ppermute | solution.py:640
  216.7 27.6 %collective-permute-start.14 = (bf16[192,2048]{1,0:T(8,128)(2,1)S(1)}, bf16[192,2048]{1,0:T(8,128)(2,1)S(1)}, u32[]{:S(2)}, u32[]{:S(2)}) collective-permute-start(bf16[192,2048]{1,0:T(8,128)(2,1)S(1)} %pad_maximum_fusion.11), channel_id=1, source_target_pairs={{0,1},{1,0},{2,3},{3,2},{4,5},{5,4},{6,7},{7,6},{8,9},{9,8},{10,11... | collective-permute-start | bytes 2359304 | tf_op jit(solution)/shard_map/ppermute | solution.py:640
  231.3 12.0 %collective-permute-start.13 = (bf16[96,2048]{1,0:T(8,128)(2,1)S(1)}, bf16[96,2048]{1,0:T(8,128)(2,1)S(1)}, u32[]{:S(2)}, u32[]{:S(2)}) collective-permute-start(bf16[96,2048]{1,0:T(8,128)(2,1)S(1)} %get-tuple-element.202), channel_id=1, source_target_pairs={{0,3},{1,2},{2,1},{3,0},{4,7},{5,6},{6,5},{7,4},{8,11},{9,10},{10,... | collective-permute-start | bytes 1179656 | tf_op jit(solution)/shard_map/ppermute | solution.py:640
  267.2 293.8 %reduce-scatter.5.cloned.1.call-start = ((), (), s32[]{:S(2)}) async-start(), calls=%async_computation.3 | async-start | bytes 11796480 | tf_op jit(solution)/shard_map/reduce_scatter | solution.py:793
  267.5 30.8 %copy-start.80 = (bf16[96,2048]{1,0:T(8,128)(2,1)S(1)}, bf16[96,2048]{1,0:T(8,128)(2,1)}, u32[]{:S(2)}) copy-start(bf16[96,2048]{1,0:T(8,128)(2,1)} %get-tuple-element.205) | copy-start | bytes 1179652
  267.5 30.9 %copy-start.82 = (bf16[384,2048]{1,0:T(8,128)(2,1)S(1)}, bf16[384,2048]{1,0:T(8,128)(2,1)}, u32[]{:S(2)}) copy-start(bf16[384,2048]{1,0:T(8,128)(2,1)} %copy-done.81) | copy-start | bytes 4718596
  267.5 30.9 %collective-permute-start.17 = (bf16[192,2048]{1,0:T(8,128)(2,1)}, bf16[192,2048]{1,0:T(8,128)(2,1)S(1)}, u32[]{:S(2)}, u32[]{:S(2)}) collective-permute-start(bf16[192,2048]{1,0:T(8,128)(2,1)} %pad_maximum_fusion.13), channel_id=1, source_target_pairs={{0,1},{1,0},{2,3},{3,2},{4,5},{5,4},{6,7},{7,6},{8,9},{9,8},{10,11... | collective-permute-start | bytes 2359304 | tf_op jit(solution)/shard_map/ppermute | solution.py:640
  268.3 30.0 %collective-permute-start.11 = (bf16[96,2048]{1,0:T(8,128)(2,1)}, bf16[96,2048]{1,0:T(8,128)(2,1)S(1)}, u32[]{:S(2)}, u32[]{:S(2)}) collective-permute-start(bf16[96,2048]{1,0:T(8,128)(2,1)} %get-tuple-element.205), channel_id=1, source_target_pairs={{0,3},{1,2},{2,1},{3,0},{4,7},{5,6},{6,5},{7,4},{8,11},{9,10},{10,... | collective-permute-start | bytes 1179656 | tf_op jit(solution)/shard_map/ppermute | solution.py:640
  271.2 52.2 %copy-start.79 = (bf16[192,2048]{1,0:T(8,128)(2,1)S(1)}, bf16[192,2048]{1,0:T(8,128)(2,1)}, u32[]{:S(2)}) copy-start(bf16[192,2048]{1,0:T(8,128)(2,1)} %copy-done.78) | copy-start | bytes 2359300
  275.8 47.5 %copy-start.43 = (f32[96,2048]{1,0:T(8,128)S(1)}, f32[96,2048]{1,0:T(8,128)}, u32[]{:S(2)}) copy-start(f32[96,2048]{1,0:T(8,128)} %copy-done.42) | copy-start | bytes 2359300
  275.8 47.5 %copy-start.74 = (bf16[384,2048]{1,0:T(8,128)(2,1)S(1)}, bf16[384,2048]{1,0:T(8,128)(2,1)}, u32[]{:S(2)}) copy-start(bf16[384,2048]{1,0:T(8,128)(2,1)} %copy-done.73) | copy-start | bytes 4718596
  275.8 51.8 %collective-permute-start.16 = (bf16[192,2048]{1,0:T(8,128)(2,1)S(1)}, bf16[192,2048]{1,0:T(8,128)(2,1)S(1)}, u32[]{:S(2)}, u32[]{:S(2)}) collective-permute-start(bf16[192,2048]{1,0:T(8,128)(2,1)S(1)} %copy-done.94), channel_id=1, source_target_pairs={{0,1},{1,0},{2,3},{3,2},{4,5},{5,4},{6,7},{7,6},{8,9},{9,8},{10,11... | collective-permute-start | bytes 2359304 | tf_op jit(solution)/shard_map/ppermute | solution.py:640
  275.9 47.4 %collective-permute-start.18 = (bf16[96,2048]{1,0:T(8,128)(2,1)S(1)}, bf16[96,2048]{1,0:T(8,128)(2,1)S(1)}, u32[]{:S(2)}, u32[]{:S(2)}) collective-permute-start(bf16[96,2048]{1,0:T(8,128)(2,1)S(1)} %copy-done.96), channel_id=1, source_target_pairs={{0,3},{1,2},{2,1},{3,0},{4,7},{5,6},{6,5},{7,4},{8,11},{9,10},{10,... | collective-permute-start | bytes 1179656 | tf_op jit(solution)/shard_map/ppermute | solution.py:640
  298.3 50.4 %collective-permute-start.15 = (bf16[192,2048]{1,0:T(8,128)(2,1)S(1)}, bf16[192,2048]{1,0:T(8,128)(2,1)S(1)}, u32[]{:S(2)}, u32[]{:S(2)}) collective-permute-start(bf16[192,2048]{1,0:T(8,128)(2,1)S(1)} %pad_maximum_fusion.14), channel_id=1, source_target_pairs={{0,1},{1,0},{2,3},{3,2},{4,5},{5,4},{6,7},{7,6},{8,9},{9,8},{10,11... | collective-permute-start | bytes 2359304 | tf_op jit(solution)/shard_map/ppermute | solution.py:640
  298.6 50.2 %collective-permute-start.19 = (bf16[96,2048]{1,0:T(8,128)(2,1)S(1)}, bf16[96,2048]{1,0:T(8,128)(2,1)S(1)}, u32[]{:S(2)}, u32[]{:S(2)}) collective-permute-start(bf16[96,2048]{1,0:T(8,128)(2,1)S(1)} %add_convert_fusion.7), channel_id=1, source_target_pairs={{0,3},{1,2},{2,1},{3,0},{4,7},{5,6},{6,5},{7,4},{8,11},{9,10},{10,... | collective-permute-start | bytes 1179656 | tf_op jit(solution)/shard_map/ppermute | solution.py:640
  326.3 29.6 %collective-permute-start.21 = (bf16[96,2048]{1,0:T(8,128)(2,1)S(1)}, bf16[96,2048]{1,0:T(8,128)(2,1)S(1)}, u32[]{:S(2)}, u32[]{:S(2)}) collective-permute-start(bf16[96,2048]{1,0:T(8,128)(2,1)S(1)} %get-tuple-element.197), channel_id=1, source_target_pairs={{0,3},{1,2},{2,1},{3,0},{4,7},{5,6},{6,5},{7,4},{8,11},{9,10},{10,... | collective-permute-start | bytes 1179656 | tf_op jit(solution)/shard_map/ppermute | solution.py:640
  352.8 39.8 %collective-permute-start.20 = (bf16[96,2048]{1,0:T(8,128)(2,1)}, bf16[96,2048]{1,0:T(8,128)(2,1)}, u32[]{:S(2)}, u32[]{:S(2)}) collective-permute-start(bf16[96,2048]{1,0:T(8,128)(2,1)} %get-tuple-element.200), channel_id=1, source_target_pairs={{0,3},{1,2},{2,1},{3,0},{4,7},{5,6},{6,5},{7,4},{8,11},{9,10},{10,... | collective-permute-start | bytes 1179656 | tf_op jit(solution)/shard_map/ppermute | solution.py:640
  356.7 18.4 %collective-permute-start.22 = (bf16[192,2048]{1,0:T(8,128)(2,1)S(1)}, bf16[192,2048]{1,0:T(8,128)(2,1)S(1)}, u32[]{:S(2)}, u32[]{:S(2)}) collective-permute-start(bf16[192,2048]{1,0:T(8,128)(2,1)S(1)} %pad_maximum_fusion.15), channel_id=1, source_target_pairs={{0,1},{1,0},{2,3},{3,2},{4,5},{5,4},{6,7},{7,6},{8,9},{9,8},{10,11... | collective-permute-start | bytes 2359304 | tf_op jit(solution)/shard_map/ppermute | solution.py:640
  363.9 28.7 %collective-permute-start.24 = (bf16[192,2048]{1,0:T(8,128)(2,1)S(1)}, bf16[192,2048]{1,0:T(8,128)(2,1)S(1)}, u32[]{:S(2)}, u32[]{:S(2)}) collective-permute-start(bf16[192,2048]{1,0:T(8,128)(2,1)S(1)} %pad_maximum_fusion.16), channel_id=1, source_target_pairs={{0,1},{1,0},{2,3},{3,2},{4,5},{5,4},{6,7},{7,6},{8,9},{9,8},{10,11... | collective-permute-start | bytes 2359304 | tf_op jit(solution)/shard_map/ppermute | solution.py:640
  435.7 19.8 %collective-permute-start.28 = (bf16[192,2048]{1,0:T(8,128)(2,1)}, bf16[192,2048]{1,0:T(8,128)(2,1)}, u32[]{:S(2)}, u32[]{:S(2)}) collective-permute-start(bf16[192,2048]{1,0:T(8,128)(2,1)} %pad_maximum_fusion.19), channel_id=1, source_target_pairs={{0,1},{1,0},{2,3},{3,2},{4,5},{5,4},{6,7},{7,6},{8,9},{9,8},{10,11... | collective-permute-start | bytes 2359304 | tf_op jit(solution)/shard_map/ppermute | solution.py:640
  436.9 20.6 %collective-permute-start.25 = (bf16[96,2048]{1,0:T(8,128)(2,1)}, bf16[96,2048]{1,0:T(8,128)(2,1)}, u32[]{:S(2)}, u32[]{:S(2)}) collective-permute-start(bf16[96,2048]{1,0:T(8,128)(2,1)} %add_convert_fusion.5), channel_id=1, source_target_pairs={{0,3},{1,2},{2,1},{3,0},{4,7},{5,6},{6,5},{7,4},{8,11},{9,10},{10,... | collective-permute-start | bytes 1179656 | tf_op jit(solution)/shard_map/ppermute | solution.py:640
  437.3 30.8 %collective-permute-start.23 = (bf16[192,2048]{1,0:T(8,128)(2,1)}, bf16[192,2048]{1,0:T(8,128)(2,1)S(1)}, u32[]{:S(2)}, u32[]{:S(2)}) collective-permute-start(bf16[192,2048]{1,0:T(8,128)(2,1)} %pad_maximum_fusion.17), channel_id=1, source_target_pairs={{0,1},{1,0},{2,3},{3,2},{4,5},{5,4},{6,7},{7,6},{8,9},{9,8},{10,11... | collective-permute-start | bytes 2359304 | tf_op jit(solution)/shard_map/ppermute | solution.py:640
  457.5 11.6 %collective-permute-start.29 = (bf16[96,2048]{1,0:T(8,128)(2,1)}, bf16[96,2048]{1,0:T(8,128)(2,1)S(1)}, u32[]{:S(2)}, u32[]{:S(2)}) collective-permute-start(bf16[96,2048]{1,0:T(8,128)(2,1)} %add_convert_fusion.4), channel_id=1, source_target_pairs={{0,3},{1,2},{2,1},{3,0},{4,7},{5,6},{6,5},{7,4},{8,11},{9,10},{10,... | collective-permute-start | bytes 1179656 | tf_op jit(solution)/shard_map/ppermute | solution.py:640
  469.0 8.6 %collective-permute-start.37 = (f32[184,128]{1,0:T(8,128)S(1)}, f32[184,128]{1,0:T(8,128)S(1)}, u32[]{:S(2)}, u32[]{:S(2)}) collective-permute-start(f32[184,128]{1,0:T(8,128)S(1)} %pad_bitcast_fusion), channel_id=1, source_target_pairs={{0,4},{4,0},{8,12},{12,8},{16,20},{20,16},{24,28},{28,24},{1,5},{5... | collective-permute-start | bytes 282632 | tf_op jit(solution)/shard_map/ppermute | solution.py:640
  474.6 13.4 %collective-permute-start.26 = (bf16[96,2048]{1,0:T(8,128)(2,1)S(1)}, bf16[96,2048]{1,0:T(8,128)(2,1)S(1)}, u32[]{:S(2)}, u32[]{:S(2)}) collective-permute-start(bf16[96,2048]{1,0:T(8,128)(2,1)S(1)} %get-tuple-element.195), channel_id=1, source_target_pairs={{0,3},{1,2},{2,1},{3,0},{4,7},{5,6},{6,5},{7,4},{8,11},{9,10},{10,... | collective-permute-start | bytes 1179656 | tf_op jit(solution)/shard_map/ppermute | solution.py:640
  477.6 33.7 %copy-start.70 = (f32[96,2048]{1,0:T(8,128)S(1)}, f32[96,2048]{1,0:T(8,128)}, u32[]{:S(2)}) copy-start(f32[96,2048]{1,0:T(8,128)} %get-tuple-element.198) | copy-start | bytes 2359300
  477.6 16.7 %collective-permute-start.38 = (f32[184,128]{1,0:T(8,128)S(1)}, f32[184,128]{1,0:T(8,128)S(1)}, u32[]{:S(2)}, u32[]{:S(2)}) collective-permute-start(f32[184,128]{1,0:T(8,128)S(1)} %fusion.87), channel_id=1, source_target_pairs={{0,8},{4,12},{8,0},{12,4},{16,24},{20,28},{24,16},{28,20},{1,9},{5... | collective-permute-start | bytes 282632 | tf_op jit(solution)/shard_map/ppermute | solution.py:640
  488.1 23.1 %collective-permute-start.27 = (bf16[192,2048]{1,0:T(8,128)(2,1)S(1)}, bf16[192,2048]{1,0:T(8,128)(2,1)S(1)}, u32[]{:S(2)}, u32[]{:S(2)}) collective-permute-start(bf16[192,2048]{1,0:T(8,128)(2,1)S(1)} %pad_maximum_fusion.18), channel_id=1, source_target_pairs={{0,1},{1,0},{2,3},{3,2},{4,5},{5,4},{6,7},{7,6},{8,9},{9,8},{10,11... | collective-permute-start | bytes 2359304 | tf_op jit(solution)/shard_map/ppermute | solution.py:640
  494.4 27.3 %collective-permute-start.39 = (f32[184,128]{1,0:T(8,128)S(1)}, f32[184,128]{1,0:T(8,128)S(1)}, u32[]{:S(2)}, u32[]{:S(2)}) collective-permute-start(f32[184,128]{1,0:T(8,128)S(1)} %fusion.197), channel_id=1, source_target_pairs={{0,16},{4,20},{8,24},{12,28},{16,0},{20,4},{24,8},{28,12},{1,17},{... | collective-permute-start | bytes 282632 | tf_op jit(solution)/shard_map/ppermute | solution.py:640
  496.0 1.3 collective-permute-start.32
  497.2 24.5 %collective-permute-start.33 = (f32[40,128]{1,0:T(8,128)S(1)}, f32[40,128]{1,0:T(8,128)}, u32[]{:S(2)}, u32[]{:S(2)}) collective-permute-start(f32[40,128]{1,0:T(8,128)S(1)} %fusion.86), channel_id=1, source_target_pairs={{0,8},{4,12},{8,0},{12,4},{16,24},{20,28},{24,16},{28,20},{1,9},{5... | collective-permute-start | bytes 61448 | tf_op jit(solution)/shard_map/ppermute | solution.py:640
  514.6 12.5 %collective-permute-start.30 = (bf16[96,2048]{1,0:T(8,128)(2,1)S(1)}, bf16[96,2048]{1,0:T(8,128)(2,1)S(1)}, u32[]{:S(2)}, u32[]{:S(2)}) collective-permute-start(bf16[96,2048]{1,0:T(8,128)(2,1)S(1)} %get-tuple-element.193), channel_id=1, source_target_pairs={{0,3},{1,2},{2,1},{3,0},{4,7},{5,6},{6,5},{7,4},{8,11},{9,10},{10,... | collective-permute-start | bytes 1179656 | tf_op jit(solution)/shard_map/ppermute | solution.py:640
  522.4 3.8 collective-permute-start.34
  526.3 9.4 %collective-permute-start.35 = (f32[40,128]{1,0:T(8,128)S(1)}, f32[40,128]{1,0:T(8,128)S(1)}, u32[]{:S(2)}, u32[]{:S(2)}) collective-permute-start(f32[40,128]{1,0:T(8,128)S(1)} %add.392), channel_id=1, source_target_pairs={{0,1},{1,0},{2,3},{3,2},{4,5},{5,4},{6,7},{7,6},{8,9},{9,8},{10,11... | collective-permute-start | bytes 61448 | tf_op jit(solution)/shard_map/ppermute | solution.py:640
  528.1 24.8 %collective-permute-start.31 = (bf16[192,2048]{1,0:T(8,128)(2,1)}, bf16[192,2048]{1,0:T(8,128)(2,1)}, u32[]{:S(2)}, u32[]{:S(2)}) collective-permute-start(bf16[192,2048]{1,0:T(8,128)(2,1)} %pad_maximum_fusion.20), channel_id=1, source_target_pairs={{0,1},{1,0},{2,3},{3,2},{4,5},{5,4},{6,7},{7,6},{8,9},{9,8},{10,11... | collective-permute-start | bytes 2359304 | tf_op jit(solution)/shard_map/ppermute | solution.py:640
  535.7 16.1 %collective-permute-start.36 = (f32[40,128]{1,0:T(8,128)S(1)}, f32[40,128]{1,0:T(8,128)S(1)}, u32[]{:S(2)}, u32[]{:S(2)}) collective-permute-start(f32[40,128]{1,0:T(8,128)S(1)} %add.393), channel_id=1, source_target_pairs={{0,2},{1,3},{2,0},{3,1},{4,6},{5,7},{6,4},{7,5},{8,10},{9,11},{10,... | collective-permute-start | bytes 61448 | tf_op jit(solution)/shard_map/ppermute | solution.py:640
  (113 other events, 592.7 us)
Sparse Core Ops, SparseCore 0:
  267.3 118.5 reduce-scatter.2
  435.8 81.7 reduce-scatter.4

commit v4 on v3

--- a/solution.py
+++ b/solution.py
@@ -478,150 +478,141 @@
     return inverse * (scaled - normal * jnp.mean(scaled * normal, axis=-1, keepdims=True))
 
 
+def codes(parts):
+    masks = []
+    while 1 << len(masks) < parts:
+        masks.append((2 << len(masks)) - 1)
+    order = []
+    for code in range(parts):
+        place = 0
+        for index, mask in enumerate(masks):
+            if code >> (len(masks) - 1 - index) & 1:
+                place ^= mask
+        order.append(place)
+    return masks, order
+
+
+def own_code():
+    order = codes(lax.axis_size("head"))[1]
+    place = lax.axis_index("head")
+    return sum(jnp.where(place == at, code, 0) for code, at in enumerate(order))
+
+
 def scatter_steps(partial_sum):
     parts = lax.axis_size("head")
+    code = own_code()
+    for mask in codes(parts)[0]:
+        half = partial_sum.shape[0] // 2
+        parts //= 2
+        bit = lax.rem(code // parts, 2)
+        payload = lax.dynamic_slice_in_dim(partial_sum, (1 - bit) * half, half, 0)
+        kept = lax.dynamic_slice_in_dim(partial_sum, bit * half, half, 0)
+        pairs = [(at, at ^ mask) for at in range(lax.axis_size("head"))]
+        (other,) = yield [(payload.astype(LOW), "head", pairs)]
+        partial_sum = kept.astype(FULL) + other.astype(FULL)
+    return partial_sum
+
+
+def gather_steps(own, buffer=None, micro=0):
+    parts = lax.axis_size("head")
+    code = own_code()
+    step = 1
+    for mask in codes(parts)[0][::-1]:
+        (other,) = yield [(own, "head", [(at, at ^ mask) for at in range(parts)])]
+        bit = lax.rem(code // step, 2)
+        size = own.shape[0]
+        step *= 2
+        if buffer is not None and step == parts:
+            for piece, index in ((own, bit), (other, 1 - bit)):
+                buffer[0] = lax.dynamic_update_slice(
+                    buffer[0], piece[None], (micro, index * size, 0)
+                )
+            return buffer
+        shape = list(own.shape)
+        shape[0] *= 2
+        joined = jnp.zeros(shape, own.dtype)
+        joined = lax.dynamic_update_slice_in_dim(joined, own, bit * size, 0)
+        own = lax.dynamic_update_slice_in_dim(joined, other, (1 - bit) * size, 0)
+    return own
+
+
+OUTER, INNER, BACK = [(0, 1), (3, 2)], [(1, 2), (2, 1)], [(1, 0), (2, 3)]
+
+
+def hub_scatter_steps(partial_sum):
+    half = partial_sum.shape[0] // 2
+    bit = lax.axis_index("head") // 2
+    near = lax.dynamic_slice_in_dim(partial_sum, bit * half, half, 0)
+    far = lax.dynamic_slice_in_dim(partial_sum, (1 - bit) * half, half, 0)
+    (first,) = yield [(far, "head", OUTER)]
+    passed = (far.astype(FULL) + first.astype(FULL)).astype(LOW)
+    second, last = yield [(passed, "head", INNER), (near, "head", OUTER)]
+    return near.astype(FULL) + second.astype(FULL) + last.astype(FULL)
+
+
+def hub_gather_steps(own, buffer=None, micro=0):
+    half, width = own.shape
     place = lax.axis_index("head")
-    own_len = partial_sum.shape[0] // parts
-
-    def share(index):
-        start = jnp.clip(index, 0, parts - 1) * own_len
-        return lax.dynamic_slice_in_dim(partial_sum, start, own_len, 0).astype(FULL)
-
-    right = left = 0.0
-    for step in range(1, parts):
-        right, left = yield [
-            (
-                (share(parts - step + place) + right).astype(LOW),
-                "head",
-                [(source, source + 1) for source in range(step)],
-            ),
-            (
-                (share(step - parts + place) + left).astype(LOW),
-                "head",
-                [(source, source - 1) for source in range(parts - step, parts)],
-            ),
-        ]
-        right, left = right.astype(FULL), left.astype(FULL)
-    return share(place) + right + left
-
-
-def gather_steps(own, buffer, micro):
-    parts = lax.axis_size("head")
-    place = lax.axis_index("head")
-    right = left = own
-    before, behind = [None] * parts, [None] * parts
-    for step in range(1, parts):
-        right, left = yield [
-            (right, "head", [(source, source + 1) for source in range(step - 1, parts - 1)]),
-            (left, "head", [(source, source - 1) for source in range(1, parts - step + 1)]),
-        ]
-        before[step], behind[step] = right, left
-    pieces = [(own, place)]
-    for step in range(1, parts):
-        piece = jnp.where(place >= step, before[step], behind[parts - step])
-        pieces.append((piece, lax.rem(place - step + parts, parts)))
-    return placed_pieces(pieces, buffer, micro)
-
-
-def offload_scatter_steps(partial_sum):
-    yield from ()
-    return lax.psum_scatter(partial_sum, "head", scatter_dimension=0, tiled=True).astype(FULL)
-
-
-def offload_gather_steps(own, buffer, micro):
-    yield from ()
-    whole = lax.all_gather(own, "head", axis=0, tiled=True)
+    bit = place // 2
+    middle = (place == 1) | (place == 2)
+    other, near = yield [(own, "head", INNER), (own, "head", BACK)]
+    (far,) = yield [(other, "head", BACK)]
+    pieces = (jnp.where(middle, own, near), bit), (jnp.where(middle, other, far), 1 - bit)
     if buffer is None:
-        return whole
-    buffer[0] = lax.dynamic_update_slice(buffer[0], whole[None], (micro, 0, 0))
-    return buffer
-
-
-def spans(size):
-    masks = []
-    while 1 << len(masks) < size:
-        masks.append((2 << len(masks)) - 1)
-    rest = [[0]]
-    for mask in masks[::-1]:
-        rest.append(rest[-1] + [mask ^ value for value in rest[-1]])
-    return masks, rest[::-1][1:]
-
-
-def pair_scatter_steps(partial_sum):
-    parts = lax.axis_size("head")
-    place = lax.axis_index("head")
-    own_len = partial_sum.shape[0] // parts
-    masks, rests = spans(parts)
-    kept = {
-        code: lax.dynamic_slice_in_dim(partial_sum, (place ^ code) * own_len, own_len, 0)
-        for code in range(parts)
-    }
-    for mask, rest in zip(masks, rests):
-        payload = jnp.concatenate([kept[mask ^ code].astype(LOW) for code in rest], axis=0)
-        (other,) = yield [(payload, "head", [(at, at ^ mask) for at in range(parts)])]
-        kept = {
-            code: kept[code].astype(FULL)
-            + other[index * own_len : (index + 1) * own_len].astype(FULL)
-            for index, code in enumerate(rest)
-        }
-    return kept[0]
-
-
-def pair_gather_steps(own, buffer, micro):
-    parts = lax.axis_size("head")
-    place = lax.axis_index("head")
-    own_len = own.shape[0]
-    masks, rests = spans(parts)
-    kept = {0: own}
-    for mask, rest in zip(masks[::-1], rests[::-1]):
-        payload = jnp.concatenate([kept[code] for code in rest], axis=0)
-        (other,) = yield [(payload, "head", [(at, at ^ mask) for at in range(parts)])]
-        for index, code in enumerate(rest):
-            kept[mask ^ code] = other[index * own_len : (index + 1) * own_len]
-    return placed_pieces(
-        [(kept[code], place ^ code) for code in range(parts)], buffer, micro
-    )
-
-
-def placed_pieces(pieces, buffer, micro):
-    own_len, width = pieces[0][0].shape
-    if buffer is None:
-        whole = jnp.zeros((len(pieces) * own_len, width), pieces[0][0].dtype)
+        whole = jnp.zeros((2 * half, width), own.dtype)
         for piece, index in pieces:
-            whole = lax.dynamic_update_slice_in_dim(whole, piece, index * own_len, 0)
+            whole = lax.dynamic_update_slice_in_dim(whole, piece, index * half, 0)
         return whole
     for piece, index in pieces:
-        buffer[0] = lax.dynamic_update_slice(
-            buffer[0], piece[None], (micro, index * own_len, 0)
-        )
+        buffer[0] = lax.dynamic_update_slice(buffer[0], piece[None], (micro, index * half, 0))
     return buffer
 
 
-def butterfly_steps(value, *axes):
-    for axis in axes:
+def batch_scatter_steps(value):
+    size = lax.axis_size("batch")
+    place = lax.axis_index("batch")
+    while size > 1:
+        size //= 2
+        half = value.shape[0] // 2
+        bit = lax.rem(place // size, 2)
+        payload = lax.dynamic_slice_in_dim(value, (1 - bit) * half, half, 0)
+        kept = lax.dynamic_slice_in_dim(value, bit * half, half, 0)
+        (other,) = yield [
+            (payload.astype(LOW), "batch", [(at, at ^ size) for at in range(lax.axis_size("batch"))])
+        ]
+        value = kept.astype(FULL) + other.astype(FULL)
+    return value
+
+
+def butterfly_steps(local, wide):
+    for axis in ("batch", "head"):
         size = lax.axis_size(axis)
         bit = 1
         while bit < size:
-            (other,) = yield [(value, axis, [(place, place ^ bit) for place in range(size)])]
+            value = jnp.concatenate([local, wide], axis=0) if axis == "batch" else wide
+            (other,) = yield [(value, axis, [(at, at ^ bit) for at in range(size)])]
             value = value + other
+            if axis == "batch":
+                local, wide = value[: local.shape[0]], value[local.shape[0] :]
+            else:
+                wide = value
             bit *= 2
-    return value
-
-
-SCATTERS = dict(C=scatter_steps, P=pair_scatter_steps, S=offload_scatter_steps)
-GATHERS = dict(C=gather_steps, P=pair_gather_steps, S=offload_gather_steps)
-PLAN = dict(
-    out="PP", mid="PP", down="PP", result="PP", grad="PP", attn="PP", inner="PP", final="PP"
-)
+    return local, wide
+
+
+LAG = 2
 
 
 class Flow:
-    def __init__(self, steps):
+    def __init__(self, steps, lag=0):
         self.steps = steps
+        self.lag = lag
+        self.fresh = True
         self.result = None
         self.advance(None)
 
     def advance(self, received):
+        self.fresh = True
         try:
             self.pending = self.steps.send(received)
         except StopIteration as stop:
@@ -629,19 +620,39 @@
             self.result = stop.value
 
 
-def tick(flows, work=None):
-    flows[:] = [flow for flow in flows if flow.pending is not None]
-    payloads = [request[0] for flow in flows for request in flow.pending]
-    token = ()
-    if work is not None:
-        token = work(lambda value: after(value, *payloads) if payloads else value)
-        token = tuple(token) if isinstance(token, (tuple, list)) else (token,)
-    for flow in flows:
-        received = [lax.ppermute(*request) for request in flow.pending]
-        if token:
-            received = lax.optimization_barrier(tuple(received) + token)[: len(received)]
-        flow.advance(received)
-    flows[:] = [flow for flow in flows if flow.pending is not None]
+class Clock:
+    def __init__(self):
+        self.flows = []
+        self.due = []
+
+    def join(self, steps, lag=0):
+        flow = Flow(steps, lag)
+        self.flows.append(flow)
+        return flow
+
+    def step(self, work=None):
+        flows = [flow for flow in self.flows if flow.pending is not None]
+        for flow in flows:
+            self.due.extend([flow.lag, request[0]] for request in flow.pending)
+        token = ()
+        if work is not None:
+            ahead = [value for lag, value in self.due if lag <= 0]
+            token = work(lambda value: after(value, *ahead) if ahead else value)
+            token = tuple(token) if isinstance(token, (tuple, list)) else (token,)
+            self.due = [[lag - 1, value] for lag, value in self.due if lag > 0]
+        for flow in flows:
+            received = [lax.ppermute(*request) for request in flow.pending]
+            if token:
+                received = lax.optimization_barrier(tuple(received) + token)[: len(received)]
+            flow.advance(received)
+            if flow.pending is None:
+                self.due.extend([flow.lag, value] for value in received)
+        self.flows = [flow for flow in flows if flow.pending is not None]
+
+    def until(self, flow):
+        while flow.result is None:
+            self.step()
+        return flow.result
 
 
 def packed(entries):
@@ -670,8 +681,18 @@
     micro_count, seq_len, model_dim = tokens.shape
     head_parts = lax.axis_size("head")
     batch_parts = lax.axis_size("batch")
-    own_len = seq_len // head_parts
-    first_row = lax.axis_index("head") * own_len
+    hub = False
+    place = lax.axis_index("head")
+    if hub:
+        own_len = seq_len // 2
+        first_row = place // 2 * own_len
+        counts = jnp.where((place == 1) | (place == 2), 1.0, 0.0)
+        scatter, gather = hub_scatter_steps, hub_gather_steps
+    else:
+        own_len = seq_len // head_parts
+        first_row = own_code() * own_len
+        counts = 1.0
+        scatter, gather = scatter_steps, gather_steps
     positions = lax.broadcasted_iota(jnp.int32, (seq_len, 1), 0)
     in_weights = (w_query, w_key, w_value, w_gate)
     hidden_width = w_up.shape[1]
@@ -689,11 +710,6 @@
             self.keep_own = own_of(keep).astype(FULL)
             self.down_grad = keep * cotangent[micro]
 
-        def scatter(self, name, value):
-            return join(Flow(SCATTERS[PLAN[name][self.micro]](value)))
-
-        def gather(self, name, value, buffer=None):
-            return join(Flow(GATHERS[PLAN[name][self.micro]](value, buffer, self.micro)))
 
         def project(self, tie):
             rows = tie(tokens[self.micro]).astype(FULL)
@@ -717,7 +733,7 @@
 
         def after_mixer(self, out_sum):
             self.middle = self.rows + self.keep_own * out_sum
-            return self.gather("mid", rms_scale(self.middle, norm_mid).astype(LOW))
+            return join(gather(rms_scale(self.middle, norm_mid).astype(LOW)))
 
         def up(self, tie):
             mid = tie(self.mid)
@@ -748,12 +764,12 @@
 
         def after_down(self, down_sum):
             own = (self.middle + self.keep_own * down_sum).astype(LOW)
-            return self.gather("result", own, out_buffer)
+            return join(gather(own, out_buffer, self.micro), LAG)
 
         def after_up_back(self, mid_sum):
-            self.gain_mid = jnp.sum(rms_scale(self.middle, 1.0) * mid_sum, axis=0)
+            self.gain_mid = counts * jnp.sum(rms_scale(self.middle, 1.0) * mid_sum, axis=0)
             self.grad_middle = self.grad_rows + rms_back(mid_sum, self.middle, norm_mid)
-            return self.gather("attn", (self.keep_own * self.grad_middle).astype(LOW))
+            return join(gather((self.keep_own * self.grad_middle).astype(LOW)))
 
         def mix_back(self, tie):
             grad_gated = mm(tie(self.attn), w_out, NT)
@@ -772,14 +788,16 @@
                     grads[:, index * head_width : (index + 1) * head_width], weight, NT
                 )
             self.in_part = in_part.astype(LOW)
-            return self.in_part
+            rows = tokens[self.micro].astype(FULL)
+            self.gain_in = jnp.sum(rms_scale(rows, 1.0) * in_part, axis=0)
+            return self.in_part, self.gain_in
 
         def after_project_back(self, in_sum):
-            self.gain_in = jnp.sum(rms_scale(self.rows, 1.0) * in_sum, axis=0)
             own = (self.grad_middle + rms_back(in_sum, self.rows, norm_in)).astype(LOW)
-            return self.gather("final", own, grad_buffer)
-
-    flows = []
+            return join(gather(own, grad_buffer, self.micro), LAG)
+
+    clock = Clock()
+    join, step, until = clock.join, clock.step, clock.until
     out_buffer, grad_buffer = [jnp.zeros_like(tokens)], [jnp.zeros_like(tokens)]
     one, two = Micro(0), Micro(1)
     held = (one, two)
@@ -790,31 +808,27 @@
         )
 
     def shared(product):
-        return lax.psum_scatter(product, "batch", scatter_dimension=0, tiled=True).astype(FULL)
+        return lax.psum_scatter(product, "batch", scatter_dimension=0, tiled=True)
 
     def together(*works):
-        return lambda tie: sum((as_tuple(work(tie)) for work in works), ())
-
-    def as_tuple(value):
-        return tuple(value) if isinstance(value, (tuple, list)) else (value,)
-
-    def join(flow):
-        flows.append(flow)
-        return flow
-
-    def until(flow, *works):
-        for work in works:
-            tick(flows, work)
-        while flow.result is None:
-            tick(flows)
-        return flow.result
+        def run(tie):
+            token = ()
+            for work in works:
+                value = work(tie)
+                token += tuple(value) if isinstance(value, (tuple, list)) else (value,)
+            return token
+
+        return run
 
     product = {}
 
-    def ff_products(tie):
-        ups = mm(tie(both("mid")), both("grad_gate", "grad_up"), TN).astype(LOW)
-        downs = mm(both("down_grad"), both("hidden"), TN).astype(LOW)
-        product["ff"] = jnp.concatenate([ups, downs], axis=1)
+    def ups_product(tie):
+        product["ups"] = mm(tie(both("mid")), both("grad_gate", "grad_up"), TN).astype(LOW)
+        return product["ups"]
+
+    def downs_product(tie):
+        downs = mm(tie(both("down_grad")), both("hidden"), TN).astype(LOW)
+        product["ff"] = jnp.concatenate([product["ups"], downs], axis=1)
         return product["ff"]
 
     def out_product(tie):
@@ -831,55 +845,56 @@
         return value
 
     one.project(free), one.mix(free), one.project_out(free)
-    flow = one.scatter("out", one.out_part)
-    until(
-        flow,
-        lambda tie: two.project(lambda value: after(tie(value), one.out_part)),
-        two.mix,
-        two.project_out,
-    )
-    flow_two = two.scatter("out", two.out_part)
-    one.mid = until(one.after_mixer(flow.result))
-    flow = two.after_mixer(until(flow_two))
-    tick(flows, one.up)
-    tick(flows, one.activate)
-    tick(flows, one.up_back)
-    sum_one = one.scatter("grad", one.mid_part)
-    two.mid = until(flow)
-    tick(flows, one.down)
-    down_one = one.scatter("down", one.down_part)
-    until(sum_one, two.up, two.activate, two.up_back)
-    attn_one = one.after_up_back(sum_one.result)
-    sum_two = two.scatter("grad", two.mid_part)
-    tick(flows, two.down)
+    sum_one = join(scatter(one.out_part))
+    step(lambda tie: two.project(lambda value: after(tie(value), one.out_part)))
+    step(two.mix)
+    until(sum_one)
+    mid_one = one.after_mixer(sum_one.result)
+    two.project_out(free)
+    sum_two = join(scatter(two.out_part))
+    one.mid = until(mid_one)
+    mid_two = two.after_mixer(until(sum_two))
+    step(one.up)
+    step(together(one.activate, one.up_back))
+    sum_one = join(scatter(one.mid_part))
+    two.mid = until(mid_two)
+    step(together(one.down, two.up))
+    down_one = join(scatter(one.down_part), LAG)
+    step(together(two.activate, two.up_back))
+    attn_one = one.after_up_back(until(sum_one))
+    sum_two = join(scatter(two.mid_part))
+    step(ups_product)
+    step(together(downs_product, two.down))
+    share_ff = shared(product["ff"])
     out_one = one.after_down(until(down_one))
-    down_two = two.scatter("down", two.down_part)
-    tick(flows, ff_products)
-    share_ff = shared(product["ff"])
     one.attn = until(attn_one)
     attn_two = two.after_up_back(until(sum_two))
-    tick(flows, one.mix_back)
-    tick(flows, one.project_back)
-    sum_one = one.scatter("inner", one.in_part)
+    down_two = join(scatter(two.down_part), LAG)
+    step(one.mix_back)
+    step(one.project_back)
+    sum_one = join(scatter(one.in_part), LAG)
     two.attn = until(attn_two)
-    until(out_one)
-    out_two = two.after_down(until(down_two))
-    tick(flows, lambda tie: two.mix_back(lambda value: after(tie(value), one.in_part)))
-    tick(flows, two.project_back)
-    sum_two = two.scatter("inner", two.in_part)
-    tick(flows, together(in_product, out_product))
-    share_in = shared(jnp.concatenate([product["in"], product["out"]], axis=1))
+    step(
+        together(
+            out_product, lambda tie: two.mix_back(lambda value: after(tie(value), one.in_part))
+        )
+    )
+    out_flow = join(batch_scatter_steps(product["out"]), LAG)
+    step(in_product)
+    share_in = shared(product["in"])
+    step(two.project_back)
+    sum_two = join(scatter(two.in_part))
     small = [a + b for a, b in zip(one.small, two.small)]
     local = (product["tiny"], small[0], small[1][0], small[2][0])
-    local_flow = join(Flow(butterfly_steps(packed(local), "batch")))
+    wide = (one.gain_in + two.gain_in, small[3][0], one.gain_mid + two.gain_mid)
+    small_flow = join(butterfly_steps(packed(local), packed(wide)))
+    out_two = two.after_down(until(down_two))
     grad_one = one.after_project_back(until(sum_one))
     grad_two = two.after_project_back(until(sum_two))
-    wide = (one.gain_in + two.gain_in, small[3][0], one.gain_mid + two.gain_mid)
-    wide_flow = join(Flow(butterfly_steps(packed(wide), "batch", "head")))
-    while flows:
-        tick(flows)
-    tiny, grad_taps, grad_dlog, grad_dbias = unpacked(local_flow.result, local)
-    gains = unpacked(wide_flow.result, wide)
+    while clock.flows:
+        step()
+    tiny, grad_taps, grad_dlog, grad_dbias = unpacked(small_flow.result[0], local)
+    gains = unpacked(small_flow.result[1], wide)
     width = model_dim // batch_parts
     tiny = lax.dynamic_slice_in_dim(tiny, lax.axis_index("batch") * width, width, 1).T
     count = w_beta.shape[1]
@@ -887,18 +902,18 @@
     def pieces(matrix, *widths):
         outs, start = [], 0
         for extent in widths:
-            outs.append(matrix[:, start : start + extent])
+            outs.append(matrix[:, start : start + extent].astype(FULL))
             start += extent
         return outs
 
-    *share_in, share_out = pieces(share_in, *([head_width] * 5))
+    share_in = pieces(share_in, *([head_width] * 4))
     share_gate, share_up, share_down = pieces(share_ff, *([hidden_width] * 3))
     return (
         out_buffer[0],
         grad_buffer[0],
         gains[0], *share_in, tiny[:, :count], tiny[:, count:],
         grad_taps, grad_dlog, grad_dbias, gains[1],
-        share_out.T, gains[2], share_gate, share_up, share_down.T,
+        out_flow.result.T, gains[2], share_gate, share_up, share_down.T,
     )
 
 

time: 583 us -> 539 us (0.925)
  waiting for transfers between devices: 196 us -> 148 us
  local copies, waits for them, and re-layouts: 62.5 us -> 83.6 us
  other arithmetic: 79 us -> 60.3 us
    ppermute x40, waiting for transfers between devices: 196 us -> 148 us  [step(): received = [lax.ppermute(*request) for request in flow.pending]]
    concatenate x18 -> x2, other arithmetic: 30.5 us -> 6.7 us  [the longest x1 6.69 us: downs_product(): product['ff'] = jnp.concatenate([product['ups'], downs], axis=1)]
    add x0 -> x10, other arithmetic: none -> 11.6 us  [the longest x8 8.46 us: scatter_steps(): partial_sum = kept.astype(FULL) + other.astype(FULL)]
    dynamic_update_slice x23 -> x24, local copies, waits for them, and re-layouts: 13.2 us -> 24 us  [the longest x8 15.7 us: gather_steps(): lax.dynamic_update_slice(buffer[0], piece[None], (micro, index * size, 0))]
    convert_element_type x10 -> x1, other arithmetic: 12.3 us -> 2.61 us  [pieces(): outs.append(matrix[:, start:start + extent].astype(FULL))]
    unnamed x245 -> x276, local copies, waits for them, and re-layouts: 30.2 us -> 29.2 us
  transfers between devices with their start and end apart: 42 -> 42, of which waited for: 15 -> 15; matrix products, arithmetic and copies ran while one was open for 30% -> 40% of each run, Pallas kernels for 7% -> 8%
where the time goes in v4:
time: 539 us; the launch traced here: 533 us
  waiting for transfers between devices  148 us (27%)
  matrix products  123 us (23%)
  local copies, waits for them, and re-layouts  83.6 us (16%)
  other arithmetic  60.3 us (11%)
  starting transfers between devices  51.8 us (10%)
  Pallas kernels  50.1 us (9%)
  between operations  16.7 us (3%)
    ppermute x40, waiting for transfers between devices, step(): received = [lax.ppermute(*request) for request in flow.pending]  148 us
    dot_general x45, matrix products, mm(): lax.dot_general(left.astype(LOW), right.astype(LOW), (dims, ((), ())), pr...  123 us
    ppermute x40, starting transfers between devices, step(): received = [lax.ppermute(*request) for request in flow.pending]  51.7 us
    pallas_call x2, Pallas kernels, mixer_backward(): pl.pallas_call(mixer_backward_body, grid=(heads // group,), in_specs=[wid...  31.7 us
    unnamed x276, local copies, waits for them, and re-layouts  29.2 us
    pallas_call x2, Pallas kernels, mixer_forward(): pl.pallas_call(mixer_forward_body, grid=(heads // group,), in_specs=[wide...  18.4 us
    dynamic_update_slice x8, local copies, waits for them, and re-layouts, gather_steps(): lax.dynamic_update_slice(buffer[0], piece[None], (micro, index * size, 0))  15.7 us
    dynamic_update_slice x8, other arithmetic, gather_steps(): joined = lax.dynamic_update_slice_in_dim(joined, own, bit * size, 0)  10.9 us
  transfers between devices with their start and end apart: 42, of which 15 were waited for; matrix products, arithmetic and copies ran while one was open for 40% of the time, Pallas kernels for 8%

profile of v4, /device:TPU:0, one launch (start us, length us, event | category | flops | bytes accessed | tf_op | source)
XLA Modules:
  0.0 533.0 jit_solution(1576776094077870768)
XLA Ops:
  7.3 2.7 fusion.14
  24.2 9.2 %mixer_forward.2 = (bf16[384,512]{1,0:T(8,128)(2,1)S(1)}, f32[384,512]{1,0:T(8,128)S(1)}, bf16[384,512]{1,0:T(8,128)(2,1)S(1)}, bf16[4,3,128,128]{3,2,1,0:T(8,128)(2,1)S(1)}, bf16[4,3,128,128]{3,2,1,0:T(8,128)(2,1)S(1)}) custom-call(f32[384,512]{1,0:T(8,128)S(1)} %fusion.88.query_ref, f32[384,512]{1,0:T(8,128)S(1)} %copy-done.9, f32[384,512]{1,0:T(8,128)S(1)} %copy-done.11, ...), custom_call_target="tpu_custom_call" | custom-call | tf_op jit(solution)/shard_map/mixer_forward/pallas_call | solution.py:411
  36.2 3.0 collective-permute-start
  39.2 2.4 fusion.84
  64.1 2.7 collective-permute-start.1
  66.8 9.2 %mixer_forward.3 = (bf16[384,512]{1,0:T(8,128)(2,1)S(1)}, f32[384,512]{1,0:T(8,128)S(1)}, bf16[384,512]{1,0:T(8,128)(2,1)S(1)}, bf16[4,3,128,128]{3,2,1,0:T(8,128)(2,1)S(1)}, bf16[4,3,128,128]{3,2,1,0:T(8,128)(2,1)S(1)}) custom-call(f32[384,512]{1,0:T(8,128)S(1)} %fusion.94.query_ref, f32[384,512]{1,0:T(8,128)S(1)} %copy-done.1, f32[384,512]{1,0:T(8,128)S(1)} %copy-done.3, ...), custom_call_target="tpu_custom_call" | custom-call | tf_op jit(solution)/shard_map/mixer_forward/pallas_call | solution.py:411
  76.1 3.4 convolution_convert_fusion.6
  82.9 28.7 %collective-permute-done.4 = bf16[192,2048]{1,0:T(8,128)(2,1)S(1)} collective-permute-done((bf16[192,2048]{1,0:T(8,128)(2,1)S(1)}, bf16[192,2048]{1,0:T(8,128)(2,1)S(1)}, u32[]{:S(2)}, u32[]{:S(2)}) %collective-permute-start.4) | collective-permute-done | bytes 786464 | tf_op jit(solution)/shard_map/ppermute | solution.py:644
  112.4 13.6 %collective-permute-done.5 = bf16[96,2048]{1,0:T(8,128)(2,1)S(1)} collective-permute-done((bf16[96,2048]{1,0:T(8,128)(2,1)S(1)}, bf16[96,2048]{1,0:T(8,128)(2,1)S(1)}, u32[]{:S(2)}, u32[]{:S(2)}) %collective-permute-start.5) | collective-permute-done | bytes 393248 | tf_op jit(solution)/shard_map/ppermute | solution.py:644
  128.6 11.6 %collective-permute-done.3 = bf16[192,2048]{1,0:T(8,128)(2,1)S(1)} collective-permute-done((bf16[192,2048]{1,0:T(8,128)(2,1)S(1)}, bf16[192,2048]{1,0:T(8,128)(2,1)S(1)}, u32[]{:S(2)}, u32[]{:S(2)}) %collective-permute-start.3) | collective-permute-done | bytes 786464 | tf_op jit(solution)/shard_map/ppermute | solution.py:644
  140.3 2.6 fusion.100
  142.9 2.6 fusion.101
  145.7 7.0 %multiply_convert_fusion.3 = (bf16[384,1408]{1,0:T(8,128)(2,1)S(1)}, bf16[384,1408]{1,0:T(8,128)(2,1)S(1)}, bf16[384,1408]{1,0:T(8,128)(2,1)}) fusion(f32[384,1408]{1,0:T(8,128)S(1)} %fusion.100, f32[384,1408]{1,0:T(8,128)S(1)} %fusion.101, bf16[384,2048]{1,0:T(8,128)(2,1)S(1)} %get-tuple-element.231, bf16[1408,2048]{1,0:T(8,128)(2,1)} %param.37), kind=kOutput, calls=%fused_computation.52 | convolution fusion | flops 2222702592 | bytes 14909440 | tf_op jit(solution)/shard_map/dot_general | solution.py:17
  152.7 2.6 fusion.102
  155.3 5.7 %add_convert_fusion.1 = bf16[384,2048]{1,0:T(8,128)(2,1)S(1)} fusion(f32[384,2048]{1,0:T(8,128)S(1)} %fusion.102, bf16[384,1408]{1,0:T(8,128)(2,1)S(1)} %get-tuple-element.221, bf16[2048,1408]{1,0:T(8,128)(2,1)} %param.36), kind=kOutput, calls=%fused_computation.38 | convolution fusion | flops 2216165376 | bytes 11567104 | tf_op jit(solution)/shard_map/dot_general | solution.py:17
  163.6 2.6 fusion.103
  167.6 2.7 convolution_convert_fusion.5
  170.4 4.0 fusion.104
  174.4 4.6 collective-permute-done.9
  180.3 8.4 %multiply_convert_fusion = (bf16[384,1408]{1,0:T(8,128)(2,1)S(1)}, bf16[384,1408]{1,0:T(8,128)(2,1)S(1)}, bf16[384,1408]{1,0:T(8,128)(2,1)}) fusion(f32[384,1408]{1,0:T(8,128)S(1)} %fusion.103, f32[384,1408]{1,0:T(8,128)} %fusion.104, bf16[384,2048]{1,0:T(8,128)(2,1)S(1)} %get-tuple-element.230, bf16[1408,2048]{1,0:T(8,128)(2,1)} %param.37), kind=kOutput, calls=%fused_computation.47 | convolution fusion | flops 2222702592 | bytes 14909440 | tf_op jit(solution)/shard_map/dot_general | solution.py:17
  188.8 2.6 fusion.105
  191.4 5.3 add_convert_fusion
  201.8 3.8 collective-permute-start.13
  205.6 12.2 %convolution_convert_fusion = bf16[2048,2816]{1,0:T(8,128)(2,1)S(1)} fusion(bf16[768,2048]{1,0:T(8,128)(2,1)} %pad_maximum_fusion.1, bf16[384,1408]{1,0:T(8,128)(2,1)} %copy-done.122, bf16[384,1408]{1,0:T(8,128)(2,1)} %copy-done.124, bf16[384,1408]{1,0:T(8,128)(2,1)} %copy-done.121, bf16[384,1408]{1,0:T(8,128)(2,1)} %copy-done.123), kind=kOutput, calls=%fused_computation.1 | convolution fusion | flops 8881438720 | bytes 19005440 | tf_op jit(solution)/shard_map/dot_general | solution.py:17
  223.6 6.8 %convolution_convert_fusion.2 = bf16[2048,1408]{1,0:T(8,128)(2,1)S(1)} fusion(bf16[768,2048]{1,0:T(8,128)(2,1)S(1)} %copy-done.79, bf16[384,1408]{1,0:T(8,128)(2,1)S(1)} %copy-done.125, bf16[384,1408]{1,0:T(8,128)(2,1)} %get-tuple-element.97), kind=kOutput, calls=%fused_computation.3 | convolution fusion | flops 4436393984 | bytes 11075584 | tf_op jit(solution)/shard_map/dot_general | solution.py:17
  230.5 6.7 %pad_maximum_fusion = bf16[2048,4224]{1,0:T(8,128)(2,1)} fusion(bf16[2048,1408]{1,0:T(8,128)(2,1)S(1)} %convolution_convert_fusion.2, bf16[2048,2816]{1,0:T(8,128)(2,1)S(1)} %convolution_convert_fusion), kind=kLoop, calls=%fused_computation | loop fusion | flops 34603008 | bytes 34603008 | tf_op jit(solution)/shard_map/concatenate | solution.py:831
  237.4 4.1 pad_maximum_fusion.4
  245.9 21.2 %collective-permute-done.8 = bf16[192,2048]{1,0:T(8,128)(2,1)} collective-permute-done((bf16[192,2048]{1,0:T(8,128)(2,1)}, bf16[192,2048]{1,0:T(8,128)(2,1)}, u32[]{:S(2)}, u32[]{:S(2)}) %collective-permute-start.8) | collective-permute-done | bytes 786464 | tf_op jit(solution)/shard_map/ppermute | solution.py:644
  270.4 5.3 convolution_convert_fusion.4
  276.2 16.0 %collective-permute-done.10 = bf16[96,2048]{1,0:T(8,128)(2,1)S(1)} collective-permute-done((bf16[96,2048]{1,0:T(8,128)(2,1)S(1)}, bf16[96,2048]{1,0:T(8,128)(2,1)S(1)}, u32[]{:S(2)}, u32[]{:S(2)}) %collective-permute-start.10) | collective-permute-done | bytes 393248 | tf_op jit(solution)/shard_map/ppermute | solution.py:644
  296.3 2.5 constant_dynamic-update-slice_fusion.9
  304.2 16.0 %mixer_backward.2 = (bf16[384,2048]{1,0:T(8,128)(2,1)}, f32[384,4]{1,0:T(8,128)S(1)}, f32[384,4]{1,0:T(8,128)S(1)}, f32[3,4,512]{2,1,0:T(4,128)S(1)}, f32[1,4]{1...) custom-call(f32[384,512]{1,0:T(8,128)S(1)} %fusion.106.grad_ref, f32[384,512]{1,0:T(8,128)S(1)} %copy-done.8, ...), custom_call_target="tpu_custom_call" | custom-call | tf_op jit(solution)/shard_map/mixer_backward/pallas_call | solution.py:442
  341.2 2.7 fusion.10
  359.5 15.8 %mixer_backward.3 = (bf16[384,2048]{1,0:T(8,128)(2,1)}, f32[384,4]{1,0:T(8,128)S(1)}, f32[384,4]{1,0:T(8,128)S(1)}, f32[3,4,512]{2,1,0:T(4,128)S(1)}, f32[1,4]{1...) custom-call(f32[384,512]{1,0:T(8,128)S(1)} %fusion.109.grad_ref, f32[384,512]{1,0:T(8,128)S(1)} %fusion.94.query_ref, ...), custom_call_target="tpu_custom_call" | custom-call | tf_op jit(solution)/shard_map/mixer_backward/pallas_call | solution.py:442
  387.8 2.8 fusion.16
  390.6 11.5 %convolution_convert_fusion.1 = bf16[2048,2048]{1,0:T(8,128)(2,1)} fusion(bf16[768,2048]{1,0:T(8,128)(2,1)} %pad_maximum_fusion.4, bf16[384,2048]{1,0:T(8,128)(2,1)} %get-tuple-element.141, bf16[384,2048]{1,0:T(8,128)(2,1)} %get-tuple-element.122), kind=kOutput, calls=%fused_computation.2 | convolution fusion | flops 6452936704 | bytes 14680064 | tf_op jit(solution)/shard_map/dot_general | solution.py:17
  404.8 2.6 collective-permute-start.25
  415.8 7.5 %collective-permute-done.28 = bf16[192,2048]{1,0:T(8,128)(2,1)} collective-permute-done((bf16[192,2048]{1,0:T(8,128)(2,1)}, bf16[192,2048]{1,0:T(8,128)(2,1)}, u32[]{:S(2)}, u32[]{:S(2)}) %collective-permute-start.28) | collective-permute-done | bytes 786464 | tf_op jit(solution)/shard_map/ppermute | solution.py:644
  425.7 2.6 collective-permute-start.29
  428.3 3.3 collective-permute-done.22
  443.5 2.5 constant_dynamic-update-slice_fusion.1
  446.0 2.4 collective-permute-start.30
  453.5 6.3 %collective-permute-done.33 = f32[224,128]{1,0:T(8,128)S(1)} collective-permute-done((f32[224,128]{1,0:T(8,128)S(1)}, f32[224,128]{1,0:T(8,128)S(1)}, u32[]{:S(2)}, u32[]{:S(2)}) %collective-permute-start.33) | collective-permute-done | bytes 114720 | tf_op jit(solution)/shard_map/ppermute | solution.py:644
  463.5 2.9 copy.62
  474.0 9.6 %collective-permute-done.36 = f32[40,128]{1,0:T(8,128)S(1)} collective-permute-done((f32[40,128]{1,0:T(8,128)S(1)}, f32[40,128]{1,0:T(8,128)S(1)}, u32[]{:S(2)}, u32[]{:S(2)}) %collective-permute-start.36) | collective-permute-done | bytes 20512 | tf_op jit(solution)/shard_map/ppermute | solution.py:644
  498.0 8.3 %collective-permute-done.27 = bf16[192,2048]{1,0:T(8,128)(2,1)} collective-permute-done((bf16[192,2048]{1,0:T(8,128)(2,1)}, bf16[192,2048]{1,0:T(8,128)(2,1)}, u32[]{:S(2)}, u32[]{:S(2)}) %collective-permute-start.27) | collective-permute-done | bytes 786464 | tf_op jit(solution)/shard_map/ppermute | solution.py:644
  510.5 10.7 %collective-permute-done.31 = bf16[192,2048]{1,0:T(8,128)(2,1)} collective-permute-done((bf16[192,2048]{1,0:T(8,128)(2,1)}, bf16[192,2048]{1,0:T(8,128)(2,1)}, u32[]{:S(2)}, u32[]{:S(2)}) %collective-permute-start.31) | collective-permute-done | bytes 786464 | tf_op jit(solution)/shard_map/ppermute | solution.py:644
  523.3 2.6 slice_convert_fusion.2
  (512 shorter events, 190.3 us)
Async XLA Ops:
  7.2 383.3 %reduce-scatter.3.cloned.1.call-start = ((), (), s32[]{:S(2)}) async-start(), calls=%async_computation.2 | async-start | bytes 19464192 | tf_op jit(solution)/shard_map/reduce_scatter | solution.py:811
  36.2 26.2 %collective-permute-start = (bf16[192,2048]{1,0:T(8,128)(2,1)}, bf16[192,2048]{1,0:T(8,128)(2,1)}, u32[]{:S(2)}, u32[]{:S(2)}) collective-permute-start(bf16[192,2048]{1,0:T(8,128)(2,1)} %constant_dynamic-slice_fusion.9), channel_id=1, source_target_pairs={{0,1},{1,0},{2,3},{3,2},{4,5},{5,4},{6,7},{7,6},{8,9},{9,8},{10,11... | collective-permute-start | bytes 2359304 | tf_op jit(solution)/shard_map/ppermute | solution.py:644
  53.4 242.8 %copy-start.113 = (f32[96]{0:T(128)}, f32[96]{0:T(128)S(1)}, u32[]{:S(2)}) copy-start(f32[96]{0:T(128)S(1)} %fusion.74) | copy-start | bytes 1156
  64.1 16.2 %collective-permute-start.1 = (bf16[96,2048]{1,0:T(8,128)(2,1)S(1)}, bf16[96,2048]{1,0:T(8,128)(2,1)S(1)}, u32[]{:S(2)}, u32[]{:S(2)}) collective-permute-start(bf16[96,2048]{1,0:T(8,128)(2,1)S(1)} %dynamic-slice_convert_fusion.8), channel_id=1, source_target_pairs={{0,3},{1,2},{2,1},{3,0},{4,7},{5,6},{6,5},{7,4},{8,11},{9,10},{10,... | collective-permute-start | bytes 1179656 | tf_op jit(solution)/shard_map/ppermute | solution.py:644
  79.7 32.0 %collective-permute-start.4 = (bf16[192,2048]{1,0:T(8,128)(2,1)S(1)}, bf16[192,2048]{1,0:T(8,128)(2,1)S(1)}, u32[]{:S(2)}, u32[]{:S(2)}) collective-permute-start(bf16[192,2048]{1,0:T(8,128)(2,1)S(1)} %constant_dynamic-slice_fusion.8), channel_id=1, source_target_pairs={{0,1},{1,0},{2,3},{3,2},{4,5},{5,4},{6,7},{7,6},{8,9},{9,8},{10,11... | collective-permute-start | bytes 2359304 | tf_op jit(solution)/shard_map/ppermute | solution.py:644
  81.6 118.8 %copy-start.48 = (f32[96,2048]{1,0:T(8,128)}, f32[96,2048]{1,0:T(8,128)S(1)}, u32[]{:S(2)}) copy-start(f32[96,2048]{1,0:T(8,128)S(1)} %get-tuple-element.217) | copy-start | bytes 2359300
  81.8 30.2 %collective-permute-start.2 = (bf16[96,2048]{1,0:T(8,128)(2,1)S(1)}, bf16[96,2048]{1,0:T(8,128)(2,1)S(1)}, u32[]{:S(2)}, u32[]{:S(2)}) collective-permute-start(bf16[96,2048]{1,0:T(8,128)(2,1)S(1)} %get-tuple-element.215), channel_id=1, source_target_pairs={{0,3},{1,2},{2,1},{3,0},{4,7},{5,6},{6,5},{7,4},{8,11},{9,10},{10,... | collective-permute-start | bytes 1179656 | tf_op jit(solution)/shard_map/ppermute | solution.py:644
  111.7 28.5 %slice-start = ((s8[5767168]{0:T(1024)(128)(4,1)}), s8[4194304]{0:T(1024)(128)(4,1)S(1)}, s32[]{:S(2)}) async-start(s8[5767168]{0:T(1024)(128)(4,1)} %bitcast.189), calls=%async_computation.4 | async-start | bytes 8388608
  112.0 14.1 %collective-permute-start.5 = (bf16[96,2048]{1,0:T(8,128)(2,1)S(1)}, bf16[96,2048]{1,0:T(8,128)(2,1)S(1)}, u32[]{:S(2)}, u32[]{:S(2)}) collective-permute-start(bf16[96,2048]{1,0:T(8,128)(2,1)S(1)} %dynamic-slice_convert_fusion.7), channel_id=1, source_target_pairs={{0,3},{1,2},{2,1},{3,0},{4,7},{5,6},{6,5},{7,4},{8,11},{9,10},{10,... | collective-permute-start | bytes 1179656 | tf_op jit(solution)/shard_map/ppermute | solution.py:644
  112.1 28.0 %collective-permute-start.3 = (bf16[192,2048]{1,0:T(8,128)(2,1)S(1)}, bf16[192,2048]{1,0:T(8,128)(2,1)S(1)}, u32[]{:S(2)}, u32[]{:S(2)}) collective-permute-start(bf16[192,2048]{1,0:T(8,128)(2,1)S(1)} %constant_dynamic-update-slice_fusion.22), channel_id=1, source_target_pairs={{0,1},{1,0},{2,3},{3,2},{4,5},{5,4},{6,7},{7,6},{8,9},{9,8},{10,11... | collective-permute-start | bytes 2359304 | tf_op jit(solution)/shard_map/ppermute | solution.py:644
  112.4 27.9 %slice-start.1 = ((s8[5767168]{0:T(1024)(128)(4,1)}), s8[1572864]{0:T(1024)(128)(4,1)S(1)}, s32[]{:S(2)}) async-start(s8[5767168]{0:T(1024)(128)(4,1)} %bitcast.189), calls=%async_computation.5 | async-start | bytes 3145728
  128.5 17.1 %collective-permute-start.6 = (bf16[96,2048]{1,0:T(8,128)(2,1)S(1)}, bf16[96,2048]{1,0:T(8,128)(2,1)S(1)}, u32[]{:S(2)}, u32[]{:S(2)}) collective-permute-start(bf16[96,2048]{1,0:T(8,128)(2,1)S(1)} %get-tuple-element.211), channel_id=1, source_target_pairs={{0,3},{1,2},{2,1},{3,0},{4,7},{5,6},{6,5},{7,4},{8,11},{9,10},{10,... | collective-permute-start | bytes 1179656 | tf_op jit(solution)/shard_map/ppermute | solution.py:644
  145.6 17.9 %collective-permute-start.7 = (bf16[192,2048]{1,0:T(8,128)(2,1)S(1)}, bf16[192,2048]{1,0:T(8,128)(2,1)S(1)}, u32[]{:S(2)}, u32[]{:S(2)}) collective-permute-start(bf16[192,2048]{1,0:T(8,128)(2,1)S(1)} %constant_dynamic-update-slice_fusion.18), channel_id=1, source_target_pairs={{0,1},{1,0},{2,3},{3,2},{4,5},{5,4},{6,7},{7,6},{8,9},{9,8},{10,11... | collective-permute-start | bytes 2359304 | tf_op jit(solution)/shard_map/ppermute | solution.py:644
  161.1 17.8 %collective-permute-start.9 = (bf16[192,2048]{1,0:T(8,128)(2,1)S(1)}, bf16[192,2048]{1,0:T(8,128)(2,1)S(1)}, u32[]{:S(2)}, u32[]{:S(2)}) collective-permute-start(bf16[192,2048]{1,0:T(8,128)(2,1)S(1)} %constant_dynamic-slice_fusion.7), channel_id=1, source_target_pairs={{0,1},{1,0},{2,3},{3,2},{4,5},{5,4},{6,7},{7,6},{8,9},{9,8},{10,11... | collective-permute-start | bytes 2359304 | tf_op jit(solution)/shard_map/ppermute | solution.py:644
  179.2 20.7 %collective-permute-start.11 = (bf16[96,2048]{1,0:T(8,128)(2,1)S(1)}, bf16[96,2048]{1,0:T(8,128)(2,1)S(1)}, u32[]{:S(2)}, u32[]{:S(2)}) collective-permute-start(bf16[96,2048]{1,0:T(8,128)(2,1)S(1)} %dynamic-slice_convert_fusion.6), channel_id=1, source_target_pairs={{0,3},{1,2},{2,1},{3,0},{4,7},{5,6},{6,5},{7,4},{8,11},{9,10},{10,... | collective-permute-start | bytes 1179656 | tf_op jit(solution)/shard_map/ppermute | solution.py:644
  197.8 22.2 %collective-permute-start.15 = (bf16[192,2048]{1,0:T(8,128)(2,1)}, bf16[192,2048]{1,0:T(8,128)(2,1)}, u32[]{:S(2)}, u32[]{:S(2)}) collective-permute-start(bf16[192,2048]{1,0:T(8,128)(2,1)} %constant_dynamic-slice_fusion.5), channel_id=1, source_target_pairs={{0,1},{1,0},{2,3},{3,2},{4,5},{5,4},{6,7},{7,6},{8,9},{9,8},{10,11... | collective-permute-start | bytes 2359304 | tf_op jit(solution)/shard_map/ppermute | solution.py:644
  201.8 21.7 %collective-permute-start.13 = (bf16[96,2048]{1,0:T(8,128)(2,1)}, bf16[96,2048]{1,0:T(8,128)(2,1)S(1)}, u32[]{:S(2)}, u32[]{:S(2)}) collective-permute-start(bf16[96,2048]{1,0:T(8,128)(2,1)} %get-tuple-element.206), channel_id=1, source_target_pairs={{0,3},{1,2},{2,1},{3,0},{4,7},{5,6},{6,5},{7,4},{8,11},{9,10},{10,... | collective-permute-start | bytes 1179656 | tf_op jit(solution)/shard_map/ppermute | solution.py:644
  237.2 286.1 %reduce-scatter.5.cloned.1.call-start = ((), (), s32[]{:S(2)}) async-start(), calls=%async_computation.3 | async-start | bytes 9437184 | tf_op jit(solution)/shard_map/reduce_scatter | solution.py:811
  237.2 29.8 %collective-permute-start.8 = (bf16[192,2048]{1,0:T(8,128)(2,1)}, bf16[192,2048]{1,0:T(8,128)(2,1)}, u32[]{:S(2)}, u32[]{:S(2)}) collective-permute-start(bf16[192,2048]{1,0:T(8,128)(2,1)} %constant_dynamic-slice_fusion.6), channel_id=1, source_target_pairs={{0,1},{1,0},{2,3},{3,2},{4,5},{5,4},{6,7},{7,6},{8,9},{9,8},{10,11... | collective-permute-start | bytes 2359304 | tf_op jit(solution)/shard_map/ppermute | solution.py:644
  237.4 29.7 %copy-start.92 = (bf16[384,2048]{1,0:T(8,128)(2,1)S(1)}, bf16[384,2048]{1,0:T(8,128)(2,1)}, u32[]{:S(2)}) copy-start(bf16[384,2048]{1,0:T(8,128)(2,1)} %copy-done.91) | copy-start | bytes 4718596
  241.5 28.9 %copy-start.126 = (bf16[384,1408]{1,0:T(8,128)(2,1)S(1)}, bf16[384,1408]{1,0:T(8,128)(2,1)}, u32[]{:S(2)}) copy-start(bf16[384,1408]{1,0:T(8,128)(2,1)} %get-tuple-element.109) | copy-start | bytes 3244036
  242.5 33.7 %collective-permute-start.16 = (bf16[96,2048]{1,0:T(8,128)(2,1)S(1)}, bf16[96,2048]{1,0:T(8,128)(2,1)S(1)}, u32[]{:S(2)}, u32[]{:S(2)}) collective-permute-start(bf16[96,2048]{1,0:T(8,128)(2,1)S(1)} %copy-done.100), channel_id=1, source_target_pairs={{0,3},{1,2},{2,1},{3,0},{4,7},{5,6},{6,5},{7,4},{8,11},{9,10},{10,... | collective-permute-start | bytes 1179656 | tf_op jit(solution)/shard_map/ppermute | solution.py:644
  244.9 56.2 %collective-permute-start.14 = (bf16[192,2048]{1,0:T(8,128)(2,1)S(1)}, bf16[192,2048]{1,0:T(8,128)(2,1)S(1)}, u32[]{:S(2)}, u32[]{:S(2)}) collective-permute-start(bf16[192,2048]{1,0:T(8,128)(2,1)S(1)} %copy-done.81), channel_id=1, source_target_pairs={{0,1},{1,0},{2,3},{3,2},{4,5},{5,4},{6,7},{7,6},{8,9},{9,8},{10,11... | collective-permute-start | bytes 2359304 | tf_op jit(solution)/shard_map/ppermute | solution.py:644
  268.5 23.7 %collective-permute-start.10 = (bf16[96,2048]{1,0:T(8,128)(2,1)S(1)}, bf16[96,2048]{1,0:T(8,128)(2,1)S(1)}, u32[]{:S(2)}, u32[]{:S(2)}) collective-permute-start(bf16[96,2048]{1,0:T(8,128)(2,1)S(1)} %dynamic-slice_convert_fusion.5), channel_id=1, source_target_pairs={{0,3},{1,2},{2,1},{3,0},{4,7},{5,6},{6,5},{7,4},{8,11},{9,10},{10,... | collective-permute-start | bytes 1179656 | tf_op jit(solution)/shard_map/ppermute | solution.py:644
  275.8 44.4 %collective-permute-start.19 = (bf16[192,2048]{1,0:T(8,128)(2,1)S(1)}, bf16[192,2048]{1,0:T(8,128)(2,1)S(1)}, u32[]{:S(2)}, u32[]{:S(2)}) collective-permute-start(bf16[192,2048]{1,0:T(8,128)(2,1)S(1)} %constant_dynamic-slice_fusion.4), channel_id=1, source_target_pairs={{0,1},{1,0},{2,3},{3,2},{4,5},{5,4},{6,7},{7,6},{8,9},{9,8},{10,11... | collective-permute-start | bytes 2359304 | tf_op jit(solution)/shard_map/ppermute | solution.py:644
  294.6 37.9 %collective-permute-start.12 = (bf16[96,2048]{1,0:T(8,128)(2,1)}, bf16[96,2048]{1,0:T(8,128)(2,1)}, u32[]{:S(2)}, u32[]{:S(2)}) collective-permute-start(bf16[96,2048]{1,0:T(8,128)(2,1)} %get-tuple-element.209), channel_id=1, source_target_pairs={{0,3},{1,2},{2,1},{3,0},{4,7},{5,6},{6,5},{7,4},{8,11},{9,10},{10,... | collective-permute-start | bytes 1179656 | tf_op jit(solution)/shard_map/ppermute | solution.py:644
  298.8 32.6 %collective-permute-start.18 = (bf16[96,2048]{1,0:T(8,128)(2,1)}, bf16[96,2048]{1,0:T(8,128)(2,1)}, u32[]{:S(2)}, u32[]{:S(2)}) collective-permute-start(bf16[96,2048]{1,0:T(8,128)(2,1)} %get-tuple-element.203), channel_id=1, source_target_pairs={{0,3},{1,2},{2,1},{3,0},{4,7},{5,6},{6,5},{7,4},{8,11},{9,10},{10,... | collective-permute-start | bytes 1179656 | tf_op jit(solution)/shard_map/ppermute | solution.py:644
  327.9 22.3 %collective-permute-start.20 = (bf16[96,2048]{1,0:T(8,128)(2,1)}, bf16[96,2048]{1,0:T(8,128)(2,1)S(1)}, u32[]{:S(2)}, u32[]{:S(2)}) collective-permute-start(bf16[96,2048]{1,0:T(8,128)(2,1)} %dynamic-slice_convert_fusion.3), channel_id=1, source_target_pairs={{0,3},{1,2},{2,1},{3,0},{4,7},{5,6},{6,5},{7,4},{8,11},{9,10},{10,... | collective-permute-start | bytes 1179656 | tf_op jit(solution)/shard_map/ppermute | solution.py:644
  332.4 23.9 %collective-permute-start.24 = (bf16[192,2048]{1,0:T(8,128)(2,1)S(1)}, bf16[192,2048]{1,0:T(8,128)(2,1)}, u32[]{:S(2)}, u32[]{:S(2)}) collective-permute-start(bf16[192,2048]{1,0:T(8,128)(2,1)S(1)} %constant_dynamic-update-slice_fusion.8), channel_id=1, source_target_pairs={{0,1},{1,0},{2,3},{3,2},{4,5},{5,4},{6,7},{7,6},{8,9},{9,8},{10,11... | collective-permute-start | bytes 2359304 | tf_op jit(solution)/shard_map/ppermute | solution.py:644
  334.3 47.0 %collective-permute-start.17 = (bf16[192,2048]{1,0:T(8,128)(2,1)}, bf16[192,2048]{1,0:T(8,128)(2,1)}, u32[]{:S(2)}, u32[]{:S(2)}) collective-permute-start(bf16[192,2048]{1,0:T(8,128)(2,1)} %constant_dynamic-update-slice_fusion.10), channel_id=1, source_target_pairs={{0,1},{1,0},{2,3},{3,2},{4,5},{5,4},{6,7},{7,6},{8,9},{9,8},{10,11... | collective-permute-start | bytes 2359304 | tf_op jit(solution)/shard_map/ppermute | solution.py:644
  345.0 45.6 %collective-permute-start.23 = (bf16[192,2048]{1,0:T(8,128)(2,1)}, bf16[192,2048]{1,0:T(8,128)(2,1)}, u32[]{:S(2)}, u32[]{:S(2)}) collective-permute-start(bf16[192,2048]{1,0:T(8,128)(2,1)} %constant_dynamic-slice_fusion.3), channel_id=1, source_target_pairs={{0,1},{1,0},{2,3},{3,2},{4,5},{5,4},{6,7},{7,6},{8,9},{9,8},{10,11... | collective-permute-start | bytes 2359304 | tf_op jit(solution)/shard_map/ppermute | solution.py:644
  352.5 56.9 %collective-permute-start.21 = (bf16[96,2048]{1,0:T(8,128)(2,1)}, bf16[96,2048]{1,0:T(8,128)(2,1)}, u32[]{:S(2)}, u32[]{:S(2)}) collective-permute-start(bf16[96,2048]{1,0:T(8,128)(2,1)} %get-tuple-element.201), channel_id=1, source_target_pairs={{0,3},{1,2},{2,1},{3,0},{4,7},{5,6},{6,5},{7,4},{8,11},{9,10},{10,... | collective-permute-start | bytes 1179656 | tf_op jit(solution)/shard_map/ppermute | solution.py:644
  379.5 54.8 %collective-permute-start.37 = (bf16[1024,512]{1,0:T(8,128)(2,1)}, bf16[1024,512]{1,0:T(8,128)(2,1)}, u32[]{:S(2)}, u32[]{:S(2)}) collective-permute-start(bf16[1024,512]{1,0:T(8,128)(2,1)} %constant_dynamic-slice_fusion), channel_id=1, source_target_pairs={{0,16},{4,20},{8,24},{12,28},{16,0},{20,4},{24,8},{28,12},{1,17},{... | collective-permute-start | bytes 3145736 | tf_op jit(solution)/shard_map/ppermute | solution.py:644
  404.8 35.2 %collective-permute-start.25 = (bf16[96,2048]{1,0:T(8,128)(2,1)}, bf16[96,2048]{1,0:T(8,128)(2,1)S(1)}, u32[]{:S(2)}, u32[]{:S(2)}) collective-permute-start(bf16[96,2048]{1,0:T(8,128)(2,1)} %dynamic-slice_convert_fusion.2), channel_id=1, source_target_pairs={{0,3},{1,2},{2,1},{3,0},{4,7},{5,6},{6,5},{7,4},{8,11},{9,10},{10,... | collective-permute-start | bytes 1179656 | tf_op jit(solution)/shard_map/ppermute | solution.py:644
  408.4 14.9 %collective-permute-start.28 = (bf16[192,2048]{1,0:T(8,128)(2,1)}, bf16[192,2048]{1,0:T(8,128)(2,1)}, u32[]{:S(2)}, u32[]{:S(2)}) collective-permute-start(bf16[192,2048]{1,0:T(8,128)(2,1)} %constant_dynamic-slice_fusion.2), channel_id=1, source_target_pairs={{0,1},{1,0},{2,3},{3,2},{4,5},{5,4},{6,7},{7,6},{8,9},{9,8},{10,11... | collective-permute-start | bytes 2359304 | tf_op jit(solution)/shard_map/ppermute | solution.py:644
  410.5 21.2 %collective-permute-start.22 = (bf16[192,2048]{1,0:T(8,128)(2,1)S(1)}, bf16[192,2048]{1,0:T(8,128)(2,1)}, u32[]{:S(2)}, u32[]{:S(2)}) collective-permute-start(bf16[192,2048]{1,0:T(8,128)(2,1)S(1)} %constant_dynamic-update-slice_fusion.6), channel_id=1, source_target_pairs={{0,1},{1,0},{2,3},{3,2},{4,5},{5,4},{6,7},{7,6},{8,9},{9,8},{10,11... | collective-permute-start | bytes 2359304 | tf_op jit(solution)/shard_map/ppermute | solution.py:644
  425.7 14.3 %collective-permute-start.29 = (bf16[96,2048]{1,0:T(8,128)(2,1)}, bf16[96,2048]{1,0:T(8,128)(2,1)}, u32[]{:S(2)}, u32[]{:S(2)}) collective-permute-start(bf16[96,2048]{1,0:T(8,128)(2,1)} %dynamic-slice_convert_fusion.1), channel_id=1, source_target_pairs={{0,3},{1,2},{2,1},{3,0},{4,7},{5,6},{6,5},{7,4},{8,11},{9,10},{10,... | collective-permute-start | bytes 1179656 | tf_op jit(solution)/shard_map/ppermute | solution.py:644
  438.1 51.2 %collective-permute-start.38 = (bf16[512,512]{1,0:T(8,128)(2,1)}, bf16[512,512]{1,0:T(8,128)(2,1)}, u32[]{:S(2)}, u32[]{:S(2)}) collective-permute-start(bf16[512,512]{1,0:T(8,128)(2,1)} %dynamic-slice_convert_fusion), channel_id=1, source_target_pairs={{0,8},{4,12},{8,0},{12,4},{16,24},{20,28},{24,16},{28,20},{1,9},{5... | collective-permute-start | bytes 1572872 | tf_op jit(solution)/shard_map/ppermute | solution.py:644
  440.0 8.4 %collective-permute-start.32 = (f32[224,128]{1,0:T(8,128)S(1)}, f32[224,128]{1,0:T(8,128)S(1)}, u32[]{:S(2)}, u32[]{:S(2)}) collective-permute-start(f32[224,128]{1,0:T(8,128)S(1)} %pad_maximum_fusion.5), channel_id=1, source_target_pairs={{0,4},{4,0},{8,12},{12,8},{16,20},{20,16},{24,28},{28,24},{1,5},{5... | collective-permute-start | bytes 344072 | tf_op jit(solution)/shard_map/ppermute | solution.py:644
  446.0 39.5 %collective-permute-start.30 = (bf16[96,2048]{1,0:T(8,128)(2,1)}, bf16[96,2048]{1,0:T(8,128)(2,1)}, u32[]{:S(2)}, u32[]{:S(2)}) collective-permute-start(bf16[96,2048]{1,0:T(8,128)(2,1)} %get-tuple-element.197), channel_id=1, source_target_pairs={{0,3},{1,2},{2,1},{3,0},{4,7},{5,6},{6,5},{7,4},{8,11},{9,10},{10,... | collective-permute-start | bytes 1179656 | tf_op jit(solution)/shard_map/ppermute | solution.py:644
  448.4 11.4 %collective-permute-start.33 = (f32[224,128]{1,0:T(8,128)S(1)}, f32[224,128]{1,0:T(8,128)S(1)}, u32[]{:S(2)}, u32[]{:S(2)}) collective-permute-start(f32[224,128]{1,0:T(8,128)S(1)} %fusion.80), channel_id=1, source_target_pairs={{0,8},{4,12},{8,0},{12,4},{16,24},{20,28},{24,16},{28,20},{1,9},{5... | collective-permute-start | bytes 344072 | tf_op jit(solution)/shard_map/ppermute | solution.py:644
  452.5 32.2 %collective-permute-start.26 = (bf16[96,2048]{1,0:T(8,128)(2,1)}, bf16[96,2048]{1,0:T(8,128)(2,1)S(1)}, u32[]{:S(2)}, u32[]{:S(2)}) collective-permute-start(bf16[96,2048]{1,0:T(8,128)(2,1)} %get-tuple-element.199), channel_id=1, source_target_pairs={{0,3},{1,2},{2,1},{3,0},{4,7},{5,6},{6,5},{7,4},{8,11},{9,10},{10,... | collective-permute-start | bytes 1179656 | tf_op jit(solution)/shard_map/ppermute | solution.py:644
  459.8 6.6 %collective-permute-start.34 = (f32[224,128]{1,0:T(8,128)S(1)}, f32[224,128]{1,0:T(8,128)S(1)}, u32[]{:S(2)}, u32[]{:S(2)}) collective-permute-start(f32[224,128]{1,0:T(8,128)S(1)} %add.453), channel_id=1, source_target_pairs={{0,16},{4,20},{8,24},{12,28},{16,0},{20,4},{24,8},{28,12},{1,17},{... | collective-permute-start | bytes 344072 | tf_op jit(solution)/shard_map/ppermute | solution.py:644
  466.5 3.8 collective-permute-start.35
  470.4 13.2 %collective-permute-start.36 = (f32[40,128]{1,0:T(8,128)S(1)}, f32[40,128]{1,0:T(8,128)S(1)}, u32[]{:S(2)}, u32[]{:S(2)}) collective-permute-start(f32[40,128]{1,0:T(8,128)S(1)} %slice_add_fusion), channel_id=1, source_target_pairs={{0,2},{1,3},{2,0},{3,1},{4,6},{5,7},{6,4},{7,5},{8,10},{9,11},{10,... | collective-permute-start | bytes 61448 | tf_op jit(solution)/shard_map/ppermute | solution.py:644
  485.5 20.8 %collective-permute-start.27 = (bf16[192,2048]{1,0:T(8,128)(2,1)}, bf16[192,2048]{1,0:T(8,128)(2,1)}, u32[]{:S(2)}, u32[]{:S(2)}) collective-permute-start(bf16[192,2048]{1,0:T(8,128)(2,1)} %constant_dynamic-update-slice_fusion.2), channel_id=1, source_target_pairs={{0,1},{1,0},{2,3},{3,2},{4,5},{5,4},{6,7},{7,6},{8,9},{9,8},{10,11... | collective-permute-start | bytes 2359304 | tf_op jit(solution)/shard_map/ppermute | solution.py:644
  487.3 33.9 %collective-permute-start.31 = (bf16[192,2048]{1,0:T(8,128)(2,1)}, bf16[192,2048]{1,0:T(8,128)(2,1)}, u32[]{:S(2)}, u32[]{:S(2)}) collective-permute-start(bf16[192,2048]{1,0:T(8,128)(2,1)} %constant_dynamic-update-slice_fusion), channel_id=1, source_target_pairs={{0,1},{1,0},{2,3},{3,2},{4,5},{5,4},{6,7},{7,6},{8,9},{9,8},{10,11... | collective-permute-start | bytes 2359304 | tf_op jit(solution)/shard_map/ppermute | solution.py:644
  490.9 4.2 collective-permute-start.39
  (130 other events, 584.0 us)
Sparse Core Ops, SparseCore 0:
  237.3 118.5 reduce-scatter.2
  402.3 78.1 reduce-scatter.4

commit v5 on v4

--- a/solution.py
+++ b/solution.py
@@ -764,7 +764,7 @@
 
         def after_down(self, down_sum):
             own = (self.middle + self.keep_own * down_sum).astype(LOW)
-            return join(gather(own, out_buffer, self.micro), LAG)
+            return join(gather(own, out_buffer, self.micro), 3)
 
         def after_up_back(self, mid_sum):
             self.gain_mid = counts * jnp.sum(rms_scale(self.middle, 1.0) * mid_sum, axis=0)
@@ -794,7 +794,7 @@
 
         def after_project_back(self, in_sum):
             own = (self.grad_middle + rms_back(in_sum, self.rows, norm_in)).astype(LOW)
-            return join(gather(own, grad_buffer, self.micro), LAG)
+            return join(gather(own, grad_buffer, self.micro), 3)
 
     clock = Clock()
     join, step, until = clock.join, clock.step, clock.until
@@ -879,7 +879,7 @@
             out_product, lambda tie: two.mix_back(lambda value: after(tie(value), one.in_part))
         )
     )
-    out_flow = join(batch_scatter_steps(product["out"]), LAG)
+    out_flow = join(batch_scatter_steps(product["out"]), 4)
     step(in_product)
     share_in = shared(product["in"])
     step(two.project_back)

time: 539 us -> 539 us (level)
  transfers between devices with their start and end apart: 42 -> 42, of which waited for: 15 -> 14; matrix products, arithmetic and copies ran while one was open for 40% -> 40% of each run, Pallas kernels for 8% -> 8%
where the time goes in v5:
time: 539 us; the launch traced here: 533 us
  waiting for transfers between devices  147 us (27%)
  matrix products  124 us (23%)
  local copies, waits for them, and re-layouts  83.9 us (16%)
  other arithmetic  61.7 us (11%)
  Pallas kernels  50.1 us (9%)
  starting transfers between devices  49 us (9%)
  between operations  16.7 us (3%)
    ppermute x40, waiting for transfers between devices, step(): received = [lax.ppermute(*request) for request in flow.pending]  147 us
    dot_general x45, matrix products, mm(): lax.dot_general(left.astype(LOW), right.astype(LOW), (dims, ((), ())), pr...  124 us
    ppermute x40, starting transfers between devices, step(): received = [lax.ppermute(*request) for request in flow.pending]  48.9 us
    pallas_call x2, Pallas kernels, mixer_backward(): pl.pallas_call(mixer_backward_body, grid=(heads // group,), in_specs=[wid...  31.7 us
    unnamed x276, local copies, waits for them, and re-layouts  29.1 us
    pallas_call x2, Pallas kernels, mixer_forward(): pl.pallas_call(mixer_forward_body, grid=(heads // group,), in_specs=[wide...  18.4 us
    dynamic_update_slice x8, local copies, waits for them, and re-layouts, gather_steps(): lax.dynamic_update_slice(buffer[0], piece[None], (micro, index * size, 0))  15.7 us
    dynamic_update_slice x8, other arithmetic, gather_steps(): joined = lax.dynamic_update_slice_in_dim(joined, own, bit * size, 0)  12 us
  transfers between devices with their start and end apart: 42, of which 14 were waited for; matrix products, arithmetic and copies ran while one was open for 40% of the time, Pallas kernels for 8%

profile of v5, /device:TPU:0, one launch (start us, length us, event | category | flops | bytes accessed | tf_op | source)
XLA Modules:
  0.0 532.6 jit_solution(6223501446506266635)
XLA Ops:
  7.3 2.7 fusion.14
  24.1 9.2 %mixer_forward.2 = (bf16[384,512]{1,0:T(8,128)(2,1)S(1)}, f32[384,512]{1,0:T(8,128)S(1)}, bf16[384,512]{1,0:T(8,128)(2,1)S(1)}, bf16[4,3,128,128]{3,2,1,0:T(8,128)(2,1)S(1)}, bf16[4,3,128,128]{3,2,1,0:T(8,128)(2,1)S(1)}) custom-call(f32[384,512]{1,0:T(8,128)S(1)} %fusion.88.query_ref, f32[384,512]{1,0:T(8,128)S(1)} %copy-done.9, f32[384,512]{1,0:T(8,128)S(1)} %copy-done.11, ...), custom_call_target="tpu_custom_call" | custom-call | tf_op jit(solution)/shard_map/mixer_forward/pallas_call | solution.py:411
  36.2 3.0 collective-permute-start
  39.2 2.5 fusion.84
  64.1 2.8 collective-permute-start.1
  66.9 9.2 %mixer_forward.3 = (bf16[384,512]{1,0:T(8,128)(2,1)S(1)}, f32[384,512]{1,0:T(8,128)S(1)}, bf16[384,512]{1,0:T(8,128)(2,1)S(1)}, bf16[4,3,128,128]{3,2,1,0:T(8,128)(2,1)S(1)}, bf16[4,3,128,128]{3,2,1,0:T(8,128)(2,1)S(1)}) custom-call(f32[384,512]{1,0:T(8,128)S(1)} %fusion.94.query_ref, f32[384,512]{1,0:T(8,128)S(1)} %copy-done.1, f32[384,512]{1,0:T(8,128)S(1)} %copy-done.3, ...), custom_call_target="tpu_custom_call" | custom-call | tf_op jit(solution)/shard_map/mixer_forward/pallas_call | solution.py:411
  76.2 3.4 convolution_convert_fusion.6
  83.0 28.8 %collective-permute-done.4 = bf16[192,2048]{1,0:T(8,128)(2,1)S(1)} collective-permute-done((bf16[192,2048]{1,0:T(8,128)(2,1)S(1)}, bf16[192,2048]{1,0:T(8,128)(2,1)S(1)}, u32[]{:S(2)}, u32[]{:S(2)}) %collective-permute-start.4) | collective-permute-done | bytes 786464 | tf_op jit(solution)/shard_map/ppermute | solution.py:644
  112.5 13.6 %collective-permute-done.5 = bf16[96,2048]{1,0:T(8,128)(2,1)S(1)} collective-permute-done((bf16[96,2048]{1,0:T(8,128)(2,1)S(1)}, bf16[96,2048]{1,0:T(8,128)(2,1)S(1)}, u32[]{:S(2)}, u32[]{:S(2)}) %collective-permute-start.5) | collective-permute-done | bytes 393248 | tf_op jit(solution)/shard_map/ppermute | solution.py:644
  128.6 11.5 %collective-permute-done.3 = bf16[192,2048]{1,0:T(8,128)(2,1)S(1)} collective-permute-done((bf16[192,2048]{1,0:T(8,128)(2,1)S(1)}, bf16[192,2048]{1,0:T(8,128)(2,1)S(1)}, u32[]{:S(2)}, u32[]{:S(2)}) %collective-permute-start.3) | collective-permute-done | bytes 786464 | tf_op jit(solution)/shard_map/ppermute | solution.py:644
  140.3 2.6 fusion.100
  142.9 2.6 fusion.101
  145.7 7.0 %multiply_convert_fusion.3 = (bf16[384,1408]{1,0:T(8,128)(2,1)S(1)}, bf16[384,1408]{1,0:T(8,128)(2,1)S(1)}, bf16[384,1408]{1,0:T(8,128)(2,1)}) fusion(f32[384,1408]{1,0:T(8,128)S(1)} %fusion.100, f32[384,1408]{1,0:T(8,128)S(1)} %fusion.101, bf16[384,2048]{1,0:T(8,128)(2,1)S(1)} %get-tuple-element.231, bf16[1408,2048]{1,0:T(8,128)(2,1)} %param.37), kind=kOutput, calls=%fused_computation.52 | convolution fusion | flops 2222702592 | bytes 14909440 | tf_op jit(solution)/shard_map/dot_general | solution.py:17
  152.7 2.6 fusion.102
  155.3 5.7 %add_convert_fusion.1 = bf16[384,2048]{1,0:T(8,128)(2,1)S(1)} fusion(f32[384,2048]{1,0:T(8,128)S(1)} %fusion.102, bf16[384,1408]{1,0:T(8,128)(2,1)S(1)} %get-tuple-element.221, bf16[2048,1408]{1,0:T(8,128)(2,1)} %param.36), kind=kOutput, calls=%fused_computation.38 | convolution fusion | flops 2216165376 | bytes 11567104 | tf_op jit(solution)/shard_map/dot_general | solution.py:17
  163.6 2.6 fusion.103
  167.6 2.7 convolution_convert_fusion.5
  170.4 4.0 fusion.104
  174.4 4.6 collective-permute-done.9
  180.4 8.4 %multiply_convert_fusion = (bf16[384,1408]{1,0:T(8,128)(2,1)S(1)}, bf16[384,1408]{1,0:T(8,128)(2,1)S(1)}, bf16[384,1408]{1,0:T(8,128)(2,1)}) fusion(f32[384,1408]{1,0:T(8,128)S(1)} %fusion.103, f32[384,1408]{1,0:T(8,128)} %fusion.104, bf16[384,2048]{1,0:T(8,128)(2,1)S(1)} %get-tuple-element.230, bf16[1408,2048]{1,0:T(8,128)(2,1)} %param.37), kind=kOutput, calls=%fused_computation.47 | convolution fusion | flops 2222702592 | bytes 14909440 | tf_op jit(solution)/shard_map/dot_general | solution.py:17
  188.8 2.6 fusion.105
  191.5 5.3 add_convert_fusion
  201.9 3.8 collective-permute-start.13
  205.7 12.2 %convolution_convert_fusion = bf16[2048,2816]{1,0:T(8,128)(2,1)S(1)} fusion(bf16[768,2048]{1,0:T(8,128)(2,1)} %pad_maximum_fusion.1, bf16[384,1408]{1,0:T(8,128)(2,1)} %copy-done.122, bf16[384,1408]{1,0:T(8,128)(2,1)} %copy-done.124, bf16[384,1408]{1,0:T(8,128)(2,1)} %copy-done.121, bf16[384,1408]{1,0:T(8,128)(2,1)} %copy-done.123), kind=kOutput, calls=%fused_computation.1 | convolution fusion | flops 8881438720 | bytes 19005440 | tf_op jit(solution)/shard_map/dot_general | solution.py:17
  223.7 6.8 %convolution_convert_fusion.2 = bf16[2048,1408]{1,0:T(8,128)(2,1)S(1)} fusion(bf16[768,2048]{1,0:T(8,128)(2,1)S(1)} %copy-done.79, bf16[384,1408]{1,0:T(8,128)(2,1)S(1)} %copy-done.125, bf16[384,1408]{1,0:T(8,128)(2,1)} %get-tuple-element.97), kind=kOutput, calls=%fused_computation.3 | convolution fusion | flops 4436393984 | bytes 11075584 | tf_op jit(solution)/shard_map/dot_general | solution.py:17
  230.6 6.8 %pad_maximum_fusion = bf16[2048,4224]{1,0:T(8,128)(2,1)} fusion(bf16[2048,1408]{1,0:T(8,128)(2,1)S(1)} %convolution_convert_fusion.2, bf16[2048,2816]{1,0:T(8,128)(2,1)S(1)} %convolution_convert_fusion), kind=kLoop, calls=%fused_computation | loop fusion | flops 34603008 | bytes 34603008 | tf_op jit(solution)/shard_map/concatenate | solution.py:831
  237.6 4.1 pad_maximum_fusion.4
  246.2 21.1 %collective-permute-done.8 = bf16[192,2048]{1,0:T(8,128)(2,1)} collective-permute-done((bf16[192,2048]{1,0:T(8,128)(2,1)}, bf16[192,2048]{1,0:T(8,128)(2,1)}, u32[]{:S(2)}, u32[]{:S(2)}) %collective-permute-start.8) | collective-permute-done | bytes 786464 | tf_op jit(solution)/shard_map/ppermute | solution.py:644
  270.6 5.3 convolution_convert_fusion.4
  276.4 16.0 %collective-permute-done.10 = bf16[96,2048]{1,0:T(8,128)(2,1)S(1)} collective-permute-done((bf16[96,2048]{1,0:T(8,128)(2,1)S(1)}, bf16[96,2048]{1,0:T(8,128)(2,1)S(1)}, u32[]{:S(2)}, u32[]{:S(2)}) %collective-permute-start.10) | collective-permute-done | bytes 393248 | tf_op jit(solution)/shard_map/ppermute | solution.py:644
  292.9 2.4 constant_dynamic-update-slice_fusion.9
  304.2 15.9 %mixer_backward.2 = (bf16[384,2048]{1,0:T(8,128)(2,1)}, f32[384,4]{1,0:T(8,128)S(1)}, f32[384,4]{1,0:T(8,128)S(1)}, f32[3,4,512]{2,1,0:T(4,128)S(1)}, f32[1,4]{1...) custom-call(f32[384,512]{1,0:T(8,128)S(1)} %fusion.106.grad_ref, f32[384,512]{1,0:T(8,128)S(1)} %copy-done.8, ...), custom_call_target="tpu_custom_call" | custom-call | tf_op jit(solution)/shard_map/mixer_backward/pallas_call | solution.py:442
  338.4 2.7 fusion.10
  359.3 15.7 %mixer_backward.3 = (bf16[384,2048]{1,0:T(8,128)(2,1)}, f32[384,4]{1,0:T(8,128)S(1)}, f32[384,4]{1,0:T(8,128)S(1)}, f32[3,4,512]{2,1,0:T(4,128)S(1)}, f32[1,4]{1...) custom-call(f32[384,512]{1,0:T(8,128)S(1)} %fusion.109.grad_ref, f32[384,512]{1,0:T(8,128)S(1)} %fusion.94.query_ref, ...), custom_call_target="tpu_custom_call" | custom-call | tf_op jit(solution)/shard_map/mixer_backward/pallas_call | solution.py:442
  387.5 2.9 fusion.16
  390.4 11.7 %convolution_convert_fusion.1 = bf16[2048,2048]{1,0:T(8,128)(2,1)} fusion(bf16[768,2048]{1,0:T(8,128)(2,1)} %pad_maximum_fusion.4, bf16[384,2048]{1,0:T(8,128)(2,1)} %get-tuple-element.141, bf16[384,2048]{1,0:T(8,128)(2,1)} %get-tuple-element.122), kind=kOutput, calls=%fused_computation.2 | convolution fusion | flops 6452936704 | bytes 14680064 | tf_op jit(solution)/shard_map/dot_general | solution.py:17
  414.7 9.3 %collective-permute-done.28 = bf16[192,2048]{1,0:T(8,128)(2,1)} collective-permute-done((bf16[192,2048]{1,0:T(8,128)(2,1)}, bf16[192,2048]{1,0:T(8,128)(2,1)}, u32[]{:S(2)}, u32[]{:S(2)}) %collective-permute-start.28) | collective-permute-done | bytes 786464 | tf_op jit(solution)/shard_map/ppermute | solution.py:644
  427.4 5.0 collective-permute-done.22
  440.4 2.5 fusion.30
  443.9 2.5 constant_dynamic-update-slice_fusion.1
  451.5 2.9 collective-permute-start.26
  454.4 3.9 collective-permute-done.33
  462.0 2.9 copy.62
  468.8 2.6 collective-permute-start.36
  472.6 10.3 %collective-permute-done.36 = f32[40,128]{1,0:T(8,128)S(1)} collective-permute-done((f32[40,128]{1,0:T(8,128)S(1)}, f32[40,128]{1,0:T(8,128)S(1)}, u32[]{:S(2)}, u32[]{:S(2)}) %collective-permute-start.36) | collective-permute-done | bytes 20512 | tf_op jit(solution)/shard_map/ppermute | solution.py:644
  497.4 8.2 %collective-permute-done.27 = bf16[192,2048]{1,0:T(8,128)(2,1)} collective-permute-done((bf16[192,2048]{1,0:T(8,128)(2,1)}, bf16[192,2048]{1,0:T(8,128)(2,1)}, u32[]{:S(2)}, u32[]{:S(2)}) %collective-permute-start.27) | collective-permute-done | bytes 786464 | tf_op jit(solution)/shard_map/ppermute | solution.py:644
  509.8 11.0 %collective-permute-done.31 = bf16[192,2048]{1,0:T(8,128)(2,1)} collective-permute-done((bf16[192,2048]{1,0:T(8,128)(2,1)}, bf16[192,2048]{1,0:T(8,128)(2,1)}, u32[]{:S(2)}, u32[]{:S(2)}) %collective-permute-start.31) | collective-permute-done | bytes 786464 | tf_op jit(solution)/shard_map/ppermute | solution.py:644
  522.9 2.6 slice_convert_fusion.2
  (512 shorter events, 187.3 us)
Async XLA Ops:
  7.2 383.2 %reduce-scatter.3.cloned.1.call-start = ((), (), s32[]{:S(2)}) async-start(), calls=%async_computation.2 | async-start | bytes 19464192 | tf_op jit(solution)/shard_map/reduce_scatter | solution.py:811
  36.2 26.3 %collective-permute-start = (bf16[192,2048]{1,0:T(8,128)(2,1)}, bf16[192,2048]{1,0:T(8,128)(2,1)}, u32[]{:S(2)}, u32[]{:S(2)}) collective-permute-start(bf16[192,2048]{1,0:T(8,128)(2,1)} %constant_dynamic-slice_fusion.9), channel_id=1, source_target_pairs={{0,1},{1,0},{2,3},{3,2},{4,5},{5,4},{6,7},{7,6},{8,9},{9,8},{10,11... | collective-permute-start | bytes 2359304 | tf_op jit(solution)/shard_map/ppermute | solution.py:644
  53.5 239.4 %copy-start.113 = (f32[96]{0:T(128)}, f32[96]{0:T(128)S(1)}, u32[]{:S(2)}) copy-start(f32[96]{0:T(128)S(1)} %fusion.74) | copy-start | bytes 1156
  64.1 16.2 %collective-permute-start.1 = (bf16[96,2048]{1,0:T(8,128)(2,1)S(1)}, bf16[96,2048]{1,0:T(8,128)(2,1)S(1)}, u32[]{:S(2)}, u32[]{:S(2)}) collective-permute-start(bf16[96,2048]{1,0:T(8,128)(2,1)S(1)} %dynamic-slice_convert_fusion.8), channel_id=1, source_target_pairs={{0,3},{1,2},{2,1},{3,0},{4,7},{5,6},{6,5},{7,4},{8,11},{9,10},{10,... | collective-permute-start | bytes 1179656 | tf_op jit(solution)/shard_map/ppermute | solution.py:644
  79.7 32.0 %collective-permute-start.4 = (bf16[192,2048]{1,0:T(8,128)(2,1)S(1)}, bf16[192,2048]{1,0:T(8,128)(2,1)S(1)}, u32[]{:S(2)}, u32[]{:S(2)}) collective-permute-start(bf16[192,2048]{1,0:T(8,128)(2,1)S(1)} %constant_dynamic-slice_fusion.8), channel_id=1, source_target_pairs={{0,1},{1,0},{2,3},{3,2},{4,5},{5,4},{6,7},{7,6},{8,9},{9,8},{10,11... | collective-permute-start | bytes 2359304 | tf_op jit(solution)/shard_map/ppermute | solution.py:644
  81.6 118.8 %copy-start.48 = (f32[96,2048]{1,0:T(8,128)}, f32[96,2048]{1,0:T(8,128)S(1)}, u32[]{:S(2)}) copy-start(f32[96,2048]{1,0:T(8,128)S(1)} %get-tuple-element.217) | copy-start | bytes 2359300
  81.9 30.2 %collective-permute-start.2 = (bf16[96,2048]{1,0:T(8,128)(2,1)S(1)}, bf16[96,2048]{1,0:T(8,128)(2,1)S(1)}, u32[]{:S(2)}, u32[]{:S(2)}) collective-permute-start(bf16[96,2048]{1,0:T(8,128)(2,1)S(1)} %get-tuple-element.215), channel_id=1, source_target_pairs={{0,3},{1,2},{2,1},{3,0},{4,7},{5,6},{6,5},{7,4},{8,11},{9,10},{10,... | collective-permute-start | bytes 1179656 | tf_op jit(solution)/shard_map/ppermute | solution.py:644
  111.7 28.5 %slice-start = ((s8[5767168]{0:T(1024)(128)(4,1)}), s8[4194304]{0:T(1024)(128)(4,1)S(1)}, s32[]{:S(2)}) async-start(s8[5767168]{0:T(1024)(128)(4,1)} %bitcast.189), calls=%async_computation.4 | async-start | bytes 8388608
  112.0 14.1 %collective-permute-start.5 = (bf16[96,2048]{1,0:T(8,128)(2,1)S(1)}, bf16[96,2048]{1,0:T(8,128)(2,1)S(1)}, u32[]{:S(2)}, u32[]{:S(2)}) collective-permute-start(bf16[96,2048]{1,0:T(8,128)(2,1)S(1)} %dynamic-slice_convert_fusion.7), channel_id=1, source_target_pairs={{0,3},{1,2},{2,1},{3,0},{4,7},{5,6},{6,5},{7,4},{8,11},{9,10},{10,... | collective-permute-start | bytes 1179656 | tf_op jit(solution)/shard_map/ppermute | solution.py:644
  112.2 28.0 %collective-permute-start.3 = (bf16[192,2048]{1,0:T(8,128)(2,1)S(1)}, bf16[192,2048]{1,0:T(8,128)(2,1)S(1)}, u32[]{:S(2)}, u32[]{:S(2)}) collective-permute-start(bf16[192,2048]{1,0:T(8,128)(2,1)S(1)} %constant_dynamic-update-slice_fusion.22), channel_id=1, source_target_pairs={{0,1},{1,0},{2,3},{3,2},{4,5},{5,4},{6,7},{7,6},{8,9},{9,8},{10,11... | collective-permute-start | bytes 2359304 | tf_op jit(solution)/shard_map/ppermute | solution.py:644
  112.4 27.8 %slice-start.1 = ((s8[5767168]{0:T(1024)(128)(4,1)}), s8[1572864]{0:T(1024)(128)(4,1)S(1)}, s32[]{:S(2)}) async-start(s8[5767168]{0:T(1024)(128)(4,1)} %bitcast.189), calls=%async_computation.5 | async-start | bytes 3145728
  128.5 17.0 %collective-permute-start.6 = (bf16[96,2048]{1,0:T(8,128)(2,1)S(1)}, bf16[96,2048]{1,0:T(8,128)(2,1)S(1)}, u32[]{:S(2)}, u32[]{:S(2)}) collective-permute-start(bf16[96,2048]{1,0:T(8,128)(2,1)S(1)} %get-tuple-element.211), channel_id=1, source_target_pairs={{0,3},{1,2},{2,1},{3,0},{4,7},{5,6},{6,5},{7,4},{8,11},{9,10},{10,... | collective-permute-start | bytes 1179656 | tf_op jit(solution)/shard_map/ppermute | solution.py:644
  145.6 17.9 %collective-permute-start.7 = (bf16[192,2048]{1,0:T(8,128)(2,1)S(1)}, bf16[192,2048]{1,0:T(8,128)(2,1)S(1)}, u32[]{:S(2)}, u32[]{:S(2)}) collective-permute-start(bf16[192,2048]{1,0:T(8,128)(2,1)S(1)} %constant_dynamic-update-slice_fusion.18), channel_id=1, source_target_pairs={{0,1},{1,0},{2,3},{3,2},{4,5},{5,4},{6,7},{7,6},{8,9},{9,8},{10,11... | collective-permute-start | bytes 2359304 | tf_op jit(solution)/shard_map/ppermute | solution.py:644
  161.1 17.9 %collective-permute-start.9 = (bf16[192,2048]{1,0:T(8,128)(2,1)S(1)}, bf16[192,2048]{1,0:T(8,128)(2,1)S(1)}, u32[]{:S(2)}, u32[]{:S(2)}) collective-permute-start(bf16[192,2048]{1,0:T(8,128)(2,1)S(1)} %constant_dynamic-slice_fusion.7), channel_id=1, source_target_pairs={{0,1},{1,0},{2,3},{3,2},{4,5},{5,4},{6,7},{7,6},{8,9},{9,8},{10,11... | collective-permute-start | bytes 2359304 | tf_op jit(solution)/shard_map/ppermute | solution.py:644
  179.3 20.7 %collective-permute-start.11 = (bf16[96,2048]{1,0:T(8,128)(2,1)S(1)}, bf16[96,2048]{1,0:T(8,128)(2,1)S(1)}, u32[]{:S(2)}, u32[]{:S(2)}) collective-permute-start(bf16[96,2048]{1,0:T(8,128)(2,1)S(1)} %dynamic-slice_convert_fusion.6), channel_id=1, source_target_pairs={{0,3},{1,2},{2,1},{3,0},{4,7},{5,6},{6,5},{7,4},{8,11},{9,10},{10,... | collective-permute-start | bytes 1179656 | tf_op jit(solution)/shard_map/ppermute | solution.py:644
  197.9 22.2 %collective-permute-start.15 = (bf16[192,2048]{1,0:T(8,128)(2,1)}, bf16[192,2048]{1,0:T(8,128)(2,1)}, u32[]{:S(2)}, u32[]{:S(2)}) collective-permute-start(bf16[192,2048]{1,0:T(8,128)(2,1)} %constant_dynamic-slice_fusion.5), channel_id=1, source_target_pairs={{0,1},{1,0},{2,3},{3,2},{4,5},{5,4},{6,7},{7,6},{8,9},{9,8},{10,11... | collective-permute-start | bytes 2359304 | tf_op jit(solution)/shard_map/ppermute | solution.py:644
  201.9 21.7 %collective-permute-start.13 = (bf16[96,2048]{1,0:T(8,128)(2,1)}, bf16[96,2048]{1,0:T(8,128)(2,1)S(1)}, u32[]{:S(2)}, u32[]{:S(2)}) collective-permute-start(bf16[96,2048]{1,0:T(8,128)(2,1)} %get-tuple-element.206), channel_id=1, source_target_pairs={{0,3},{1,2},{2,1},{3,0},{4,7},{5,6},{6,5},{7,4},{8,11},{9,10},{10,... | collective-permute-start | bytes 1179656 | tf_op jit(solution)/shard_map/ppermute | solution.py:644
  237.4 285.5 %reduce-scatter.5.cloned.1.call-start = ((), (), s32[]{:S(2)}) async-start(), calls=%async_computation.3 | async-start | bytes 9437184 | tf_op jit(solution)/shard_map/reduce_scatter | solution.py:811
  237.4 29.8 %collective-permute-start.8 = (bf16[192,2048]{1,0:T(8,128)(2,1)}, bf16[192,2048]{1,0:T(8,128)(2,1)}, u32[]{:S(2)}, u32[]{:S(2)}) collective-permute-start(bf16[192,2048]{1,0:T(8,128)(2,1)} %constant_dynamic-slice_fusion.6), channel_id=1, source_target_pairs={{0,1},{1,0},{2,3},{3,2},{4,5},{5,4},{6,7},{7,6},{8,9},{9,8},{10,11... | collective-permute-start | bytes 2359304 | tf_op jit(solution)/shard_map/ppermute | solution.py:644
  237.6 29.7 %copy-start.92 = (bf16[384,2048]{1,0:T(8,128)(2,1)S(1)}, bf16[384,2048]{1,0:T(8,128)(2,1)}, u32[]{:S(2)}) copy-start(bf16[384,2048]{1,0:T(8,128)(2,1)} %copy-done.91) | copy-start | bytes 4718596
  241.7 28.9 %copy-start.126 = (bf16[384,1408]{1,0:T(8,128)(2,1)S(1)}, bf16[384,1408]{1,0:T(8,128)(2,1)}, u32[]{:S(2)}) copy-start(bf16[384,1408]{1,0:T(8,128)(2,1)} %get-tuple-element.109) | copy-start | bytes 3244036
  242.8 33.6 %collective-permute-start.16 = (bf16[96,2048]{1,0:T(8,128)(2,1)S(1)}, bf16[96,2048]{1,0:T(8,128)(2,1)S(1)}, u32[]{:S(2)}, u32[]{:S(2)}) collective-permute-start(bf16[96,2048]{1,0:T(8,128)(2,1)S(1)} %copy-done.100), channel_id=1, source_target_pairs={{0,3},{1,2},{2,1},{3,0},{4,7},{5,6},{6,5},{7,4},{8,11},{9,10},{10,... | collective-permute-start | bytes 1179656 | tf_op jit(solution)/shard_map/ppermute | solution.py:644
  245.1 56.0 %collective-permute-start.14 = (bf16[192,2048]{1,0:T(8,128)(2,1)S(1)}, bf16[192,2048]{1,0:T(8,128)(2,1)S(1)}, u32[]{:S(2)}, u32[]{:S(2)}) collective-permute-start(bf16[192,2048]{1,0:T(8,128)(2,1)S(1)} %copy-done.81), channel_id=1, source_target_pairs={{0,1},{1,0},{2,3},{3,2},{4,5},{5,4},{6,7},{7,6},{8,9},{9,8},{10,11... | collective-permute-start | bytes 2359304 | tf_op jit(solution)/shard_map/ppermute | solution.py:644
  268.7 23.7 %collective-permute-start.10 = (bf16[96,2048]{1,0:T(8,128)(2,1)S(1)}, bf16[96,2048]{1,0:T(8,128)(2,1)S(1)}, u32[]{:S(2)}, u32[]{:S(2)}) collective-permute-start(bf16[96,2048]{1,0:T(8,128)(2,1)S(1)} %dynamic-slice_convert_fusion.5), channel_id=1, source_target_pairs={{0,3},{1,2},{2,1},{3,0},{4,7},{5,6},{6,5},{7,4},{8,11},{9,10},{10,... | collective-permute-start | bytes 1179656 | tf_op jit(solution)/shard_map/ppermute | solution.py:644
  276.1 44.1 %collective-permute-start.19 = (bf16[192,2048]{1,0:T(8,128)(2,1)S(1)}, bf16[192,2048]{1,0:T(8,128)(2,1)S(1)}, u32[]{:S(2)}, u32[]{:S(2)}) collective-permute-start(bf16[192,2048]{1,0:T(8,128)(2,1)S(1)} %constant_dynamic-slice_fusion.4), channel_id=1, source_target_pairs={{0,1},{1,0},{2,3},{3,2},{4,5},{5,4},{6,7},{7,6},{8,9},{9,8},{10,11... | collective-permute-start | bytes 2359304 | tf_op jit(solution)/shard_map/ppermute | solution.py:644
  295.3 35.8 %collective-permute-start.18 = (bf16[96,2048]{1,0:T(8,128)(2,1)}, bf16[96,2048]{1,0:T(8,128)(2,1)}, u32[]{:S(2)}, u32[]{:S(2)}) collective-permute-start(bf16[96,2048]{1,0:T(8,128)(2,1)} %get-tuple-element.203), channel_id=1, source_target_pairs={{0,3},{1,2},{2,1},{3,0},{4,7},{5,6},{6,5},{7,4},{8,11},{9,10},{10,... | collective-permute-start | bytes 1179656 | tf_op jit(solution)/shard_map/ppermute | solution.py:644
  298.8 33.5 %collective-permute-start.12 = (bf16[96,2048]{1,0:T(8,128)(2,1)}, bf16[96,2048]{1,0:T(8,128)(2,1)}, u32[]{:S(2)}, u32[]{:S(2)}) collective-permute-start(bf16[96,2048]{1,0:T(8,128)(2,1)} %get-tuple-element.209), channel_id=1, source_target_pairs={{0,3},{1,2},{2,1},{3,0},{4,7},{5,6},{6,5},{7,4},{8,11},{9,10},{10,... | collective-permute-start | bytes 1179656 | tf_op jit(solution)/shard_map/ppermute | solution.py:644
  326.2 24.3 %collective-permute-start.20 = (bf16[96,2048]{1,0:T(8,128)(2,1)}, bf16[96,2048]{1,0:T(8,128)(2,1)}, u32[]{:S(2)}, u32[]{:S(2)}) collective-permute-start(bf16[96,2048]{1,0:T(8,128)(2,1)} %dynamic-slice_convert_fusion.3), channel_id=1, source_target_pairs={{0,3},{1,2},{2,1},{3,0},{4,7},{5,6},{6,5},{7,4},{8,11},{9,10},{10,... | collective-permute-start | bytes 1179656 | tf_op jit(solution)/shard_map/ppermute | solution.py:644
  332.2 23.9 %collective-permute-start.24 = (bf16[192,2048]{1,0:T(8,128)(2,1)S(1)}, bf16[192,2048]{1,0:T(8,128)(2,1)}, u32[]{:S(2)}, u32[]{:S(2)}) collective-permute-start(bf16[192,2048]{1,0:T(8,128)(2,1)S(1)} %constant_dynamic-update-slice_fusion.8), channel_id=1, source_target_pairs={{0,1},{1,0},{2,3},{3,2},{4,5},{5,4},{6,7},{7,6},{8,9},{9,8},{10,11... | collective-permute-start | bytes 2359304 | tf_op jit(solution)/shard_map/ppermute | solution.py:644
  342.2 48.2 %collective-permute-start.23 = (bf16[192,2048]{1,0:T(8,128)(2,1)}, bf16[192,2048]{1,0:T(8,128)(2,1)}, u32[]{:S(2)}, u32[]{:S(2)}) collective-permute-start(bf16[192,2048]{1,0:T(8,128)(2,1)} %constant_dynamic-slice_fusion.3), channel_id=1, source_target_pairs={{0,1},{1,0},{2,3},{3,2},{4,5},{5,4},{6,7},{7,6},{8,9},{9,8},{10,11... | collective-permute-start | bytes 2359304 | tf_op jit(solution)/shard_map/ppermute | solution.py:644
  345.9 61.9 %collective-permute-start.17 = (bf16[192,2048]{1,0:T(8,128)(2,1)}, bf16[192,2048]{1,0:T(8,128)(2,1)}, u32[]{:S(2)}, u32[]{:S(2)}) collective-permute-start(bf16[192,2048]{1,0:T(8,128)(2,1)} %constant_dynamic-update-slice_fusion.10), channel_id=1, source_target_pairs={{0,1},{1,0},{2,3},{3,2},{4,5},{5,4},{6,7},{7,6},{8,9},{9,8},{10,11... | collective-permute-start | bytes 2359304 | tf_op jit(solution)/shard_map/ppermute | solution.py:644
  353.9 53.9 %collective-permute-start.21 = (bf16[96,2048]{1,0:T(8,128)(2,1)}, bf16[96,2048]{1,0:T(8,128)(2,1)}, u32[]{:S(2)}, u32[]{:S(2)}) collective-permute-start(bf16[96,2048]{1,0:T(8,128)(2,1)} %get-tuple-element.201), channel_id=1, source_target_pairs={{0,3},{1,2},{2,1},{3,0},{4,7},{5,6},{6,5},{7,4},{8,11},{9,10},{10,... | collective-permute-start | bytes 1179656 | tf_op jit(solution)/shard_map/ppermute | solution.py:644
  379.3 55.7 %collective-permute-start.37 = (bf16[1024,512]{1,0:T(8,128)(2,1)}, bf16[1024,512]{1,0:T(8,128)(2,1)}, u32[]{:S(2)}, u32[]{:S(2)}) collective-permute-start(bf16[1024,512]{1,0:T(8,128)(2,1)} %constant_dynamic-slice_fusion), channel_id=1, source_target_pairs={{0,16},{4,20},{8,24},{12,28},{16,0},{20,4},{24,8},{28,12},{1,17},{... | collective-permute-start | bytes 3145736 | tf_op jit(solution)/shard_map/ppermute | solution.py:644
  404.7 35.6 %collective-permute-start.25 = (bf16[96,2048]{1,0:T(8,128)(2,1)}, bf16[96,2048]{1,0:T(8,128)(2,1)S(1)}, u32[]{:S(2)}, u32[]{:S(2)}) collective-permute-start(bf16[96,2048]{1,0:T(8,128)(2,1)} %dynamic-slice_convert_fusion.2), channel_id=1, source_target_pairs={{0,3},{1,2},{2,1},{3,0},{4,7},{5,6},{6,5},{7,4},{8,11},{9,10},{10,... | collective-permute-start | bytes 1179656 | tf_op jit(solution)/shard_map/ppermute | solution.py:644
  407.2 16.8 %collective-permute-start.28 = (bf16[192,2048]{1,0:T(8,128)(2,1)}, bf16[192,2048]{1,0:T(8,128)(2,1)}, u32[]{:S(2)}, u32[]{:S(2)}) collective-permute-start(bf16[192,2048]{1,0:T(8,128)(2,1)} %constant_dynamic-slice_fusion.2), channel_id=1, source_target_pairs={{0,1},{1,0},{2,3},{3,2},{4,5},{5,4},{6,7},{7,6},{8,9},{9,8},{10,11... | collective-permute-start | bytes 2359304 | tf_op jit(solution)/shard_map/ppermute | solution.py:644
  409.0 23.4 %collective-permute-start.22 = (bf16[192,2048]{1,0:T(8,128)(2,1)S(1)}, bf16[192,2048]{1,0:T(8,128)(2,1)}, u32[]{:S(2)}, u32[]{:S(2)}) collective-permute-start(bf16[192,2048]{1,0:T(8,128)(2,1)S(1)} %constant_dynamic-update-slice_fusion.6), channel_id=1, source_target_pairs={{0,1},{1,0},{2,3},{3,2},{4,5},{5,4},{6,7},{7,6},{8,9},{9,8},{10,11... | collective-permute-start | bytes 2359304 | tf_op jit(solution)/shard_map/ppermute | solution.py:644
  426.4 13.9 %collective-permute-start.29 = (bf16[96,2048]{1,0:T(8,128)(2,1)}, bf16[96,2048]{1,0:T(8,128)(2,1)}, u32[]{:S(2)}, u32[]{:S(2)}) collective-permute-start(bf16[96,2048]{1,0:T(8,128)(2,1)} %dynamic-slice_convert_fusion.1), channel_id=1, source_target_pairs={{0,3},{1,2},{2,1},{3,0},{4,7},{5,6},{6,5},{7,4},{8,11},{9,10},{10,... | collective-permute-start | bytes 1179656 | tf_op jit(solution)/shard_map/ppermute | solution.py:644
  438.8 49.9 %collective-permute-start.38 = (bf16[512,512]{1,0:T(8,128)(2,1)}, bf16[512,512]{1,0:T(8,128)(2,1)}, u32[]{:S(2)}, u32[]{:S(2)}) collective-permute-start(bf16[512,512]{1,0:T(8,128)(2,1)} %dynamic-slice_convert_fusion), channel_id=1, source_target_pairs={{0,8},{4,12},{8,0},{12,4},{16,24},{20,28},{24,16},{28,20},{1,9},{5... | collective-permute-start | bytes 1572872 | tf_op jit(solution)/shard_map/ppermute | solution.py:644
  440.3 7.0 %collective-permute-start.32 = (f32[224,128]{1,0:T(8,128)S(1)}, f32[224,128]{1,0:T(8,128)S(1)}, u32[]{:S(2)}, u32[]{:S(2)}) collective-permute-start(f32[224,128]{1,0:T(8,128)S(1)} %pad_maximum_fusion.5), channel_id=1, source_target_pairs={{0,4},{4,0},{8,12},{12,8},{16,20},{20,16},{24,28},{28,24},{1,5},{5... | collective-permute-start | bytes 344072 | tf_op jit(solution)/shard_map/ppermute | solution.py:644
  446.4 38.5 %collective-permute-start.30 = (bf16[96,2048]{1,0:T(8,128)(2,1)}, bf16[96,2048]{1,0:T(8,128)(2,1)}, u32[]{:S(2)}, u32[]{:S(2)}) collective-permute-start(bf16[96,2048]{1,0:T(8,128)(2,1)} %get-tuple-element.197), channel_id=1, source_target_pairs={{0,3},{1,2},{2,1},{3,0},{4,7},{5,6},{6,5},{7,4},{8,11},{9,10},{10,... | collective-permute-start | bytes 1179656 | tf_op jit(solution)/shard_map/ppermute | solution.py:644
  447.3 11.0 %collective-permute-start.33 = (f32[224,128]{1,0:T(8,128)S(1)}, f32[224,128]{1,0:T(8,128)S(1)}, u32[]{:S(2)}, u32[]{:S(2)}) collective-permute-start(f32[224,128]{1,0:T(8,128)S(1)} %fusion.80), channel_id=1, source_target_pairs={{0,8},{4,12},{8,0},{12,4},{16,24},{20,28},{24,16},{28,20},{1,9},{5... | collective-permute-start | bytes 344072 | tf_op jit(solution)/shard_map/ppermute | solution.py:644
  451.5 32.6 %collective-permute-start.26 = (bf16[96,2048]{1,0:T(8,128)(2,1)}, bf16[96,2048]{1,0:T(8,128)(2,1)S(1)}, u32[]{:S(2)}, u32[]{:S(2)}) collective-permute-start(bf16[96,2048]{1,0:T(8,128)(2,1)} %get-tuple-element.199), channel_id=1, source_target_pairs={{0,3},{1,2},{2,1},{3,0},{4,7},{5,6},{6,5},{7,4},{8,11},{9,10},{10,... | collective-permute-start | bytes 1179656 | tf_op jit(solution)/shard_map/ppermute | solution.py:644
  458.3 6.6 %collective-permute-start.34 = (f32[224,128]{1,0:T(8,128)S(1)}, f32[224,128]{1,0:T(8,128)S(1)}, u32[]{:S(2)}, u32[]{:S(2)}) collective-permute-start(f32[224,128]{1,0:T(8,128)S(1)} %add.453), channel_id=1, source_target_pairs={{0,16},{4,20},{8,24},{12,28},{16,0},{20,4},{24,8},{28,12},{1,17},{... | collective-permute-start | bytes 344072 | tf_op jit(solution)/shard_map/ppermute | solution.py:644
  465.0 3.8 collective-permute-start.35
  468.8 14.1 %collective-permute-start.36 = (f32[40,128]{1,0:T(8,128)S(1)}, f32[40,128]{1,0:T(8,128)S(1)}, u32[]{:S(2)}, u32[]{:S(2)}) collective-permute-start(f32[40,128]{1,0:T(8,128)S(1)} %slice_add_fusion), channel_id=1, source_target_pairs={{0,2},{1,3},{2,0},{3,1},{4,6},{5,7},{6,4},{7,5},{8,10},{9,11},{10,... | collective-permute-start | bytes 61448 | tf_op jit(solution)/shard_map/ppermute | solution.py:644
  484.9 20.8 %collective-permute-start.27 = (bf16[192,2048]{1,0:T(8,128)(2,1)}, bf16[192,2048]{1,0:T(8,128)(2,1)}, u32[]{:S(2)}, u32[]{:S(2)}) collective-permute-start(bf16[192,2048]{1,0:T(8,128)(2,1)} %constant_dynamic-update-slice_fusion.2), channel_id=1, source_target_pairs={{0,1},{1,0},{2,3},{3,2},{4,5},{5,4},{6,7},{7,6},{8,9},{9,8},{10,11... | collective-permute-start | bytes 2359304 | tf_op jit(solution)/shard_map/ppermute | solution.py:644
  486.7 34.2 %collective-permute-start.31 = (bf16[192,2048]{1,0:T(8,128)(2,1)}, bf16[192,2048]{1,0:T(8,128)(2,1)}, u32[]{:S(2)}, u32[]{:S(2)}) collective-permute-start(bf16[192,2048]{1,0:T(8,128)(2,1)} %constant_dynamic-update-slice_fusion), channel_id=1, source_target_pairs={{0,1},{1,0},{2,3},{3,2},{4,5},{5,4},{6,7},{7,6},{8,9},{9,8},{10,11... | collective-permute-start | bytes 2359304 | tf_op jit(solution)/shard_map/ppermute | solution.py:644
  490.3 4.2 collective-permute-start.39
  (130 other events, 551.5 us)
Sparse Core Ops, SparseCore 0:
  237.5 118.5 reduce-scatter.2
  402.2 76.2 reduce-scatter.4
